TPU v7x, 256 devices: a whole 4x4x8 slice. The times are simulated.
256 devices in a mesh: dp: 8 (over x, core), expert: 32 (over y, z).
Axes of the slice: x: 4, y: 4, z: 8, core: 2. Of those that a mesh axis runs over, the one named last changes fastest.
Arguments:
- tokens: bfloat16 [8192, 4096], P('expert', 'dp'), may hold values from -6 to 6
- out_grad: bfloat16 [8192, 4096], P('expert', 'dp'), may hold values from -1.5 to 1.5
- slot_token: int32 [32, 64, 16], P('expert'), may hold values from -1 to 255, as said below
- slot_gate: bfloat16 [32, 64, 16], P('expert'), may hold values from 0.099609375 to 1
- w_gate: bfloat16 [64, 4096, 768], P('expert', 'dp'), may hold values from -0.09375 to 0.09375
- w_up: bfloat16 [64, 4096, 768], P('expert', 'dp'), may hold values from -0.09375 to 0.09375
- w_down: bfloat16 [64, 768, 4096], P('expert', None, 'dp'), may hold values from -0.21875 to 0.21875
Outputs:
- moe_out: bfloat16 [8192, 4096], P('expert', 'dp')
- token_grad: bfloat16 [8192, 4096], P('expert', 'dp')
- gate_grad: bfloat16 [32, 64, 16], P('expert')
- grad_w_gate: bfloat16 [64, 4096, 768], P('expert', 'dp')
- grad_w_up: bfloat16 [64, 4096, 768], P('expert', 'dp')
- grad_w_down: bfloat16 [64, 768, 4096], P('expert', None, 'dp')
Inputs may be any that keep to these rules, and one draw needn't show every extreme that they name: `slot_token`: entry [s, e, j] is the row, among sender s's 256 tokens, that slot j of expert e takes from s, or -1 for an empty slot; the rows of one sender and expert are distinct; every expert has exactly 256 non-empty slots in all, at most 16 from one sender, and for every expert some sender fills all 16.
All inputs are finite; a program needn't handle non-finite values.
Results may differ from a plain program's by a relative error of at most 0.0064.
Values may be sent and summed in bfloat16 or wider, within the bound.
No kernel may reach another device: no remote copies, remote signals or barrier semaphores. Data moves between devices by JAX's collectives and lax.ppermute only.
A program may use at most 128 MiB of HBM per device.

v0:
```python
import jax
import jax.numpy as jnp
from jax import lax
from jax.sharding import PartitionSpec as P


def silu_slope(values):
    sigma = jax.nn.sigmoid(values)
    return sigma * (1.0 + values * (1.0 - sigma))


def local(tokens, out_grad, slot_token, slot_gate, w_gate, w_up, w_down):
    senders = lax.axis_size("expert")
    tok_rows = tokens.shape[0]
    slice_width = tokens.shape[1]
    experts = slot_token.shape[1]
    pair_slots = slot_token.shape[2]
    local_experts = w_gate.shape[0]
    hidden_width = w_gate.shape[2]
    slot_rows = senders * pair_slots
    flat_index = slot_token.reshape(experts * pair_slots)
    picker = (flat_index[:, None] == jnp.arange(tok_rows, dtype=jnp.int32)[None, :]).astype(
        jnp.bfloat16
    )
    picked_in = jnp.dot(picker, tokens, preferred_element_type=jnp.float32).astype(jnp.bfloat16)
    picked_grad = jnp.dot(picker, out_grad, preferred_element_type=jnp.float32).astype(jnp.bfloat16)
    sent_in = picked_in.reshape(experts, 1, pair_slots, slice_width)
    sent_grad = picked_grad.reshape(experts, 1, pair_slots, slice_width)
    sent_gate = slot_gate.reshape(experts, 1, pair_slots)
    got_in, got_grad, got_gate = (
        lax.all_to_all(sent_in, "expert", split_axis=0, concat_axis=1, tiled=True),
        lax.all_to_all(sent_grad, "expert", split_axis=0, concat_axis=1, tiled=True),
        lax.all_to_all(sent_gate, "expert", split_axis=0, concat_axis=1, tiled=True),
    )
    rows_in = got_in.reshape(local_experts, slot_rows, slice_width)
    rows_grad = got_grad.reshape(local_experts, slot_rows, slice_width)
    gate_values = got_gate.reshape(local_experts, slot_rows).astype(jnp.float32)
    gate_part = jnp.einsum("erd,edf->ref", rows_in, w_gate, preferred_element_type=jnp.float32)
    up_part = jnp.einsum("erd,edf->ref", rows_in, w_up, preferred_element_type=jnp.float32)
    gate_up = lax.psum(jnp.concatenate([gate_part, up_part], axis=2), "dp")
    gate_pre = gate_up[:, :, :hidden_width]
    up_pre = gate_up[:, :, hidden_width:]
    activated = jax.nn.silu(gate_pre)
    hidden = (activated * up_pre).astype(jnp.bfloat16)
    expert_out = jnp.einsum("ref,efd->erd", hidden, w_down, preferred_element_type=jnp.float32)
    weighted = (gate_values[:, :, None] * expert_out).astype(jnp.bfloat16)
    weighted = weighted.reshape(local_experts, senders, pair_slots, slice_width)
    returned = lax.all_to_all(weighted, "expert", split_axis=1, concat_axis=0, tiled=True)
    moe_out = lax.dot_general(
        picker,
        returned.reshape(experts * pair_slots, slice_width),
        (((0,), (0,)), ((), ())),
        preferred_element_type=jnp.float32,
    ).astype(jnp.bfloat16)
    grad_float = rows_grad.astype(jnp.float32)
    dot_terms = jnp.sum(expert_out * grad_float, axis=2).T
    scaled_grad = (gate_values[:, :, None] * grad_float).astype(jnp.bfloat16)
    hidden_terms = jnp.einsum(
        "erd,efd->ref", scaled_grad, w_down, preferred_element_type=jnp.float32
    )
    hidden_grad, dot_sums = lax.psum((hidden_terms, dot_terms), "dp")
    gate_pre_grad = (hidden_grad * up_pre * silu_slope(gate_pre)).astype(jnp.bfloat16)
    up_pre_grad = (hidden_grad * activated).astype(jnp.bfloat16)
    gate_dots = dot_sums.astype(jnp.bfloat16)
    rows_back = (
        jnp.einsum("ref,edf->erd", gate_pre_grad, w_gate, preferred_element_type=jnp.float32)
        + jnp.einsum("ref,edf->erd", up_pre_grad, w_up, preferred_element_type=jnp.float32)
    ).astype(jnp.bfloat16)
    grad_gate_w = jnp.einsum(
        "erd,ref->edf", rows_in, gate_pre_grad, preferred_element_type=jnp.float32
    ).astype(jnp.bfloat16)
    grad_up_w = jnp.einsum(
        "erd,ref->edf", rows_in, up_pre_grad, preferred_element_type=jnp.float32
    ).astype(jnp.bfloat16)
    grad_down_w = jnp.einsum(
        "ref,erd->efd", hidden, scaled_grad, preferred_element_type=jnp.float32
    ).astype(jnp.bfloat16)
    back_rows = rows_back.reshape(local_experts, senders, pair_slots, slice_width)
    back_dots = gate_dots.T.reshape(local_experts, senders, pair_slots)
    got_back, got_dots = (
        lax.all_to_all(back_rows, "expert", split_axis=1, concat_axis=0, tiled=True),
        lax.all_to_all(back_dots, "expert", split_axis=1, concat_axis=0, tiled=True),
    )
    token_grad = lax.dot_general(
        picker,
        got_back.reshape(experts * pair_slots, slice_width),
        (((0,), (0,)), ((), ())),
        preferred_element_type=jnp.float32,
    ).astype(jnp.bfloat16)
    gate_grad = got_dots.reshape(1, experts, pair_slots)
    return (moe_out, token_grad, gate_grad, grad_gate_w, grad_up_w, grad_down_w)


def solution(mesh):
    placed = (
        P("expert", "dp"),
        P("expert", "dp"),
        P("expert", None, None),
        P("expert", None, None),
        P("expert", "dp", None),
        P("expert", "dp", None),
        P("expert", None, "dp"),
    )
    return jax.shard_map(
        local,
        mesh=mesh,
        in_specs=placed,
        out_specs=(
            P("expert", "dp"),
            P("expert", "dp"),
            P("expert", None, None),
            P("expert", "dp", None),
            P("expert", "dp", None),
            P("expert", None, "dp"),
        ),
        check_vma=False,
    )
```

profile of v0, /device:TPU:6, one launch (start us, length us, event | category | flops | bytes accessed | tf_op | source)
XLA Modules:
  0.0 334.0 jit_solution(3606816864552711107)
XLA Ops:
  7.2 0.0 copy-start
  7.2 1.5 copy.46
  8.7 11.5 %all-to-all-start = ((bf16[64,1,16]{2,1,0:T(2,128)(2,1)}), bf16[64,1,16]{2,1,0:T(2,128)(2,1)S(1)}, u32[]{:S(2)}, u32[]{:S(2)}) async-start(bf16[64,1,16]{2,1,0:T(2,128)(2,1)} %copy.46), calls=%async_computation | async-start | bytes 65536 | tf_op jit(solution)/shard_map/all_to_all | solution.py:33
  20.2 0.8 copy.45
  21.0 0.1 eq.15
  21.1 2.4 convolution_convert_fusion.3
  23.5 6.6 %all-to-all-done = bf16[64,1,16]{2,1,0:T(2,128)(2,1)S(1)} async-done(((bf16[64,1,16]{2,1,0:T(2,128)(2,1)}), bf16[64,1,16]{2,1,0:T(2,128)(2,1)S(1)}, u32[]{:S(2)}, u32[]{:S(2)}) %all-to-all-start) | async-done | bytes 2080 | tf_op jit(solution)/shard_map/all_to_all | solution.py:33
  30.1 3.9 %all-to-all-start.3 = ((bf16[64,1,16,512]{3,2,1,0:T(8,128)(2,1)}), bf16[64,1,16,512]{3,2,1,0:T(8,128)(2,1)S(1)}, u32[]{:S(2)}, u32[]{:S(2)}) async-start(bf16[64,1,16,512]{3,2,1,0:T(8,128)(2,1)} %bitcast.81), calls=%async_computation.3 | async-start | bytes 2097152 | tf_op jit(solution)/shard_map/all_to_all | solution.py:32
  34.1 1.5 convolution_convert_fusion.4
  35.5 26.1 %all-to-all-done.3 = bf16[64,1,16,512]{3,2,1,0:T(8,128)(2,1)S(1)} async-done(((bf16[64,1,16,512]{3,2,1,0:T(8,128)(2,1)}), bf16[64,1,16,512]{3,2,1,0:T(8,128)(2,1)S(1)}, u32[]{:S(2)}, u32[]{:S(2)}) %all-to-all-start.3) | async-done | bytes 1048608 | tf_op jit(solution)/shard_map/all_to_all | solution.py:32
  61.6 5.1 %all-to-all-start.1 = ((bf16[64,1,16,512]{3,2,1,0:T(8,128)(2,1)}), bf16[64,1,16,512]{3,2,1,0:T(8,128)(2,1)}, u32[]{:S(2)}, u32[]{:S(2)}) async-start(bf16[64,1,16,512]{3,2,1,0:T(8,128)(2,1)} %bitcast.80), calls=%async_computation.1 | async-start | bytes 2097152 | tf_op jit(solution)/shard_map/all_to_all | solution.py:31
  66.8 0.0 all-reduce.3.cloned.1.call-start
  66.9 0.1 reshape.74
  67.0 0.3 convert_bitcast_fusion
  67.2 1.6 copy.53
  68.8 25.6 %all-to-all-done.1 = bf16[64,1,16,512]{3,2,1,0:T(8,128)(2,1)} async-done(((bf16[64,1,16,512]{3,2,1,0:T(8,128)(2,1)}), bf16[64,1,16,512]{3,2,1,0:T(8,128)(2,1)}, u32[]{:S(2)}, u32[]{:S(2)}) %all-to-all-start.1) | async-done | bytes 1048608 | tf_op jit(solution)/shard_map/all_to_all | solution.py:31
  94.4 1.3 copy.49
  95.7 0.0 copy-start.8
  95.7 1.0 convolution_bitcast_fusion.1
  96.7 0.8 copy-done.8
  97.5 1.0 convolution_bitcast_fusion.2
  98.5 3.6 %pad_maximum_fusion = f32[512,2,1536]{2,0,1:T(8,128)} fusion(f32[512,2,768]{2,0,1:T(8,128)S(1)} %convolution_bitcast_fusion.1, f32[512,2,768]{2,0,1:T(8,128)S(1)} %convolution_bitcast_fusion.2), kind=kLoop, calls=%fused_computation | loop fusion | flops 1572864 | bytes 12582912 | tf_op jit(solution)/shard_map/concatenate | solution.py:40
  102.1 2.7 convolution_bitcast_fusion
  104.8 0.0 all-reduce.3.cloned.1.call-update
  104.8 113.9 %all-reduce.3.cloned.1.call-done = (f32[512,2,1536]{2,0,1:T(8,128)}, f32[512,2,768]{2,0,1:T(8,128)}) async-done(((f32[512,2,1536]{2,0,1:T(8,128)}, f32[512,2,768]{2,0,1:T(8,128)}), (f32[512,2,1536]{2,0,1:T(8,128)}, f32[512,2,768]{2,0,1:T(8,128)})) %all-reduce.3.cloned.1.call-update) | async-done | bytes 9437200 | tf_op jit(solution)/shard_map/psum | solution.py:40
  218.6 5.9 %multiply_convert_fusion = (bf16[512,2,768]{2,0,1:T(8,128)(2,1)}, bf16[512,2,768]{2,0,1:T(8,128)(2,1)}, bf16[512,2,768]{2,0,1:T(8,128)(2,1)S(1)}) fusion(f32[512,2,768]{2,0,1:T(8,128)} %get-tuple-element.25, f32[512,2,1536]{2,0,1:T(8,128)} %get-tuple-element.24), kind=kLoop, calls=%fused_computation.1 | loop fusion | flops 11796480 | bytes 14155776 | tf_op jit(solution)/shard_map/convert_element_type | solution.py:63
  224.5 2.0 multiply_reduce_fusion
  226.5 11.2 %psum.23 = bf16[512,2]{0,1:T(2,128)(2,1)S(1)} all-reduce(f32[512,2]{0,1:T(2,128)S(1)} %bitcast.86), channel_id=1, replica_groups=mesh['dp'=8,'expert'=32] {'dp'}, use_global_device_ids=true, to_apply=%region_3.4 | all-reduce | flops 1024 | bytes 6144 | tf_op jit(solution)/shard_map/psum | solution.py:61
  237.7 0.1 reshape.72
  237.8 0.6 copy.55
  238.4 9.9 %all-to-all-start.5 = ((bf16[2,32,16]{2,0,1:T(2,128)(2,1)}), bf16[2,32,16]{2,0,1:T(2,128)(2,1)S(1)}, u32[]{:S(2)}, u32[]{:S(2)}) async-start(bf16[2,32,16]{2,0,1:T(2,128)(2,1)} %copy.55), calls=%async_computation.5 | async-start | bytes 32768 | tf_op jit(solution)/shard_map/all_to_all | solution.py:82
  248.2 2.3 copy.50
  250.5 7.4 %all-to-all-done.5 = bf16[2,32,16]{2,0,1:T(2,128)(2,1)S(1)} async-done(((bf16[2,32,16]{2,0,1:T(2,128)(2,1)}), bf16[2,32,16]{2,0,1:T(2,128)(2,1)S(1)}, u32[]{:S(2)}, u32[]{:S(2)}) %all-to-all-start.5) | async-done | bytes 2080 | tf_op jit(solution)/shard_map/all_to_all | solution.py:82
  257.9 4.7 %all-to-all-start.2 = ((bf16[2,32,16,512]{3,2,0,1:T(8,128)(2,1)}), bf16[2,32,16,512]{3,2,0,1:T(8,128)(2,1)}, u32[]{:S(2)}, u32[]{:S(2)}) async-start(bf16[2,32,16,512]{3,2,0,1:T(8,128)(2,1)} %copy.50), calls=%async_computation.2 | async-start | bytes 2097152 | tf_op jit(solution)/shard_map/all_to_all | solution.py:48
  262.6 0.0 copy-start.7
  262.6 0.0 copy-start.10
  262.6 3.0 fusion.5
  265.7 1.0 add_convert_fusion
  266.7 1.0 copy.54
  267.8 23.4 %all-to-all-done.2 = bf16[2,32,16,512]{3,2,0,1:T(8,128)(2,1)} async-done(((bf16[2,32,16,512]{3,2,0,1:T(8,128)(2,1)}), bf16[2,32,16,512]{3,2,0,1:T(8,128)(2,1)}, u32[]{:S(2)}, u32[]{:S(2)}) %all-to-all-start.2) | async-done | bytes 1048608 | tf_op jit(solution)/shard_map/all_to_all | solution.py:48
  291.2 5.3 %all-to-all-start.4 = ((bf16[2,32,16,512]{3,2,0,1:T(8,128)(2,1)}), bf16[2,32,16,512]{3,2,0,1:T(8,128)(2,1)}, u32[]{:S(2)}, u32[]{:S(2)}) async-start(bf16[2,32,16,512]{3,2,0,1:T(8,128)(2,1)} %copy.54), calls=%async_computation.4 | async-start | bytes 2097152 | tf_op jit(solution)/shard_map/all_to_all | solution.py:81
  296.5 4.0 %convolution_convert_fusion.1 = bf16[2,512,768]{2,1,0:T(8,128)(2,1)} fusion(bf16[2,512,512]{2,1,0:T(8,128)(2,1)} %bitcast.77, bf16[512,2,768]{2,0,1:T(8,128)(2,1)} %get-tuple-element.26), kind=kOutput, calls=%fused_computation.15 | convolution fusion | flops 806092800 | bytes 4194304 | tf_op jit(solution)/shard_map/erd,ref->edf/dot_general | solution.py:72
  300.6 2.2 convolution_convert_fusion.2
  302.8 2.3 convolution_convert_fusion
  305.1 0.7 copy.59
  305.7 2.6 convolution_convert_fusion.6
  308.4 16.2 %all-to-all-done.4 = bf16[2,32,16,512]{3,2,0,1:T(8,128)(2,1)} async-done(((bf16[2,32,16,512]{3,2,0,1:T(8,128)(2,1)}), bf16[2,32,16,512]{3,2,0,1:T(8,128)(2,1)}, u32[]{:S(2)}, u32[]{:S(2)}) %all-to-all-start.4) | async-done | bytes 1048608 | tf_op jit(solution)/shard_map/all_to_all | solution.py:81
  324.6 2.6 convolution_convert_fusion.5
  (21 shorter events, 0.1 us)
Async XLA Ops:
  7.2 94.9 %copy-start = (bf16[2,768,512]{2,1,0:T(8,128)(2,1)S(1)}, bf16[2,768,512]{2,1,0:T(8,128)(2,1)}, u32[]{:S(2)}) copy-start(bf16[2,768,512]{2,1,0:T(8,128)(2,1)} %param.13) | copy-start | bytes 4718596
  7.2 26.9 %copy-start.11 = (bf16[256,512]{1,0:T(8,128)(2,1)S(1)}, bf16[256,512]{1,0:T(8,128)(2,1)}, u32[]{:S(2)}) copy-start(bf16[256,512]{1,0:T(8,128)(2,1)} %param.7) | copy-start | bytes 786436
  8.7 21.4 %all-to-all-start = ((bf16[64,1,16]{2,1,0:T(2,128)(2,1)}), bf16[64,1,16]{2,1,0:T(2,128)(2,1)S(1)}, u32[]{:S(2)}, u32[]{:S(2)}) async-start(bf16[64,1,16]{2,1,0:T(2,128)(2,1)} %copy.46), calls=%async_computation | async-start | bytes 65536 | tf_op jit(solution)/shard_map/all_to_all | solution.py:33
  30.1 31.5 %all-to-all-start.3 = ((bf16[64,1,16,512]{3,2,1,0:T(8,128)(2,1)}), bf16[64,1,16,512]{3,2,1,0:T(8,128)(2,1)S(1)}, u32[]{:S(2)}, u32[]{:S(2)}) async-start(bf16[64,1,16,512]{3,2,1,0:T(8,128)(2,1)} %bitcast.81), calls=%async_computation.3 | async-start | bytes 2097152 | tf_op jit(solution)/shard_map/all_to_all | solution.py:32
  61.6 32.8 %all-to-all-start.1 = ((bf16[64,1,16,512]{3,2,1,0:T(8,128)(2,1)}), bf16[64,1,16,512]{3,2,1,0:T(8,128)(2,1)}, u32[]{:S(2)}, u32[]{:S(2)}) async-start(bf16[64,1,16,512]{3,2,1,0:T(8,128)(2,1)} %bitcast.80), calls=%async_computation.1 | async-start | bytes 2097152 | tf_op jit(solution)/shard_map/all_to_all | solution.py:31
  66.8 151.9 %all-reduce.3.cloned.1.call-start = ((), (), s32[]{:S(2)}) async-start(), calls=%async_computation.6 | async-start | bytes 18874368 | tf_op jit(solution)/shard_map/psum | solution.py:40
  68.8 26.9 %copy-start.9 = (bf16[2,512,768]{2,1,0:T(8,128)(2,1)S(1)}, bf16[2,512,768]{2,1,0:T(8,128)(2,1)}, u32[]{:S(2)}) copy-start(bf16[2,512,768]{2,1,0:T(8,128)(2,1)} %param.12) | copy-start | bytes 4718596
  95.7 1.0 copy-start.4
  95.7 1.8 copy-start.8
  98.5 3.6 %copy-start.1 = (f32[2,32,1,16,512]{4,3,1,0,2:T(8,128)S(1)}, f32[2,32,1,16,512]{4,3,1,0,2:T(8,128)}, u32[]{:S(2)}) copy-start(f32[2,32,1,16,512]{4,3,1,0,2:T(8,128)} %copy.53) | copy-start | bytes 6291460
  218.6 5.9 %copy-start.2 = (f32[2,32,1,16,512]{4,3,1,0,2:T(8,128)S(1)}, f32[2,32,1,16,512]{4,3,1,0,2:T(8,128)}, u32[]{:S(2)}) copy-start(f32[2,32,1,16,512]{4,3,1,0,2:T(8,128)} %copy.53) | copy-start | bytes 6291460
  238.4 19.6 %all-to-all-start.5 = ((bf16[2,32,16]{2,0,1:T(2,128)(2,1)}), bf16[2,32,16]{2,0,1:T(2,128)(2,1)S(1)}, u32[]{:S(2)}, u32[]{:S(2)}) async-start(bf16[2,32,16]{2,0,1:T(2,128)(2,1)} %copy.55), calls=%async_computation.5 | async-start | bytes 32768 | tf_op jit(solution)/shard_map/all_to_all | solution.py:82
  257.9 33.2 %all-to-all-start.2 = ((bf16[2,32,16,512]{3,2,0,1:T(8,128)(2,1)}), bf16[2,32,16,512]{3,2,0,1:T(8,128)(2,1)}, u32[]{:S(2)}, u32[]{:S(2)}) async-start(bf16[2,32,16,512]{3,2,0,1:T(8,128)(2,1)} %copy.50), calls=%async_computation.2 | async-start | bytes 2097152 | tf_op jit(solution)/shard_map/all_to_all | solution.py:48
  262.6 3.1 copy-start.7
  262.6 3.1 copy-start.10
  291.2 33.4 %all-to-all-start.4 = ((bf16[2,32,16,512]{3,2,0,1:T(8,128)(2,1)}), bf16[2,32,16,512]{3,2,0,1:T(8,128)(2,1)}, u32[]{:S(2)}, u32[]{:S(2)}) async-start(bf16[2,32,16,512]{3,2,0,1:T(8,128)(2,1)} %copy.54), calls=%async_computation.4 | async-start | bytes 2097152 | tf_op jit(solution)/shard_map/all_to_all | solution.py:81
  296.5 4.1 %copy-start.5 = (bf16[32,2,1,16,512]{4,3,0,1,2:T(8,128)(2,1)S(1)}, bf16[32,2,1,16,512]{4,3,0,1,2:T(8,128)(2,1)}, u32[]{:S(2)}) copy-start(bf16[32,2,1,16,512]{4,3,0,1,2:T(8,128)(2,1)} %copy-done.4) | copy-start | bytes 3145732
  296.5 4.1 %copy-start.6 = (bf16[512,2,768]{2,0,1:T(8,128)(2,1)S(1)}, bf16[512,2,768]{2,0,1:T(8,128)(2,1)}, u32[]{:S(2)}) copy-start(bf16[512,2,768]{2,0,1:T(8,128)(2,1)} %get-tuple-element.27) | copy-start | bytes 4718596
  300.5 2.2 copy-start.3
Sparse Core Ops, SparseCore 0:
  104.9 113.6 all-reduce.2
where the time goes:
time: 335 us; the launch traced here: 334 us
  waiting for transfers between devices  219 us (65%)
  starting transfers between devices  40.4 us (12%)
  matrix products  28.4 us (8%)
  between operations  14.3 us (4%)
  blocking collectives  11.2 us (3%)
  local copies, waits for them, and re-layouts  10.9 us (3%)
  other arithmetic  9.73 us (3%)
    psum x1, waiting for transfers between devices, local(): gate_up = lax.psum(jnp.concatenate([gate_part, up_part], axis=2), 'dp')  114 us
    all_to_all x1, waiting for transfers between devices, local(): lax.all_to_all(sent_grad, 'expert', split_axis=0, concat_axis=1, tiled=True)  26.1 us
    all_to_all x1, waiting for transfers between devices, local(): lax.all_to_all(sent_in, 'expert', split_axis=0, concat_axis=1, tiled=True)  25.6 us
    all_to_all x1, waiting for transfers between devices, local(): lax.all_to_all(weighted, 'expert', split_axis=1, concat_axis=0, tiled=True)  23.4 us
    all_to_all x1, waiting for transfers between devices, local(): lax.all_to_all(back_rows, 'expert', split_axis=1, concat_axis=0, tiled=True)  16.2 us
    all_to_all x1, starting transfers between devices, local(): lax.all_to_all(sent_gate, 'expert', split_axis=0, concat_axis=1, tiled=True)  11.5 us
    psum x1, blocking collectives, local(): hidden_grad, dot_sums = lax.psum((hidden_terms, dot_terms), 'dp')  11.2 us
    all_to_all x1, starting transfers between devices, local(): lax.all_to_all(back_dots, 'expert', split_axis=1, concat_axis=0, tiled=True)  9.85 us
  transfers between devices with their start and end apart: 7, of which 7 were waited for; matrix products, arithmetic and copies ran while one was open for 8% of the time, Pallas kernels for 0%

commit v1 on v0

v1 whole, which is shorter than its diff:
```python
import functools

import jax
import jax.numpy as jnp
from jax import lax
from jax.experimental import pallas as pl
from jax.experimental.pallas import tpu as pltpu
from jax.sharding import PartitionSpec as P

BF = jnp.bfloat16
F32 = jnp.float32
LIVE = 256
EMPTY_MARK = 64.0
VMEM_LIMIT = 48 * 1024 * 1024


def dot(a, b):
    return jnp.dot(a, b, preferred_element_type=F32)


def dot_nt(a, b):
    return lax.dot_general(a, b, (((1,), (1,)), ((), ())), preferred_element_type=F32)


def dot_tn(a, b):
    return lax.dot_general(a, b, (((0,), (0,)), ((), ())), preferred_element_type=F32)


def iota(shape, dim):
    return lax.broadcasted_iota(jnp.int32, shape, dim)


def call(kernel, ids, args, outs, flops, scratch=(), blocks=None):
    blocks = blocks or {}
    in_specs = []
    for n, arg in enumerate(args):
        if n in blocks:
            in_specs.append(pl.BlockSpec(*blocks[n]))
        else:
            rank = arg.ndim
            in_specs.append(pl.BlockSpec(arg.shape, lambda i, ids, rank=rank: (0,) * rank))
    out_specs = [
        pl.BlockSpec(shape, lambda i, ids, rank=len(shape): (0,) * rank) for shape, _ in outs
    ]
    moved = sum(a.size * a.dtype.itemsize for a in args)
    moved += sum(functools.reduce(lambda p, q: p * q, s) * jnp.dtype(t).itemsize for s, t in outs)
    return pl.pallas_call(
        kernel,
        out_shape=[jax.ShapeDtypeStruct(s, t) for s, t in outs],
        grid_spec=pltpu.PrefetchScalarGridSpec(
            num_scalar_prefetch=1,
            grid=(1,),
            in_specs=in_specs,
            out_specs=out_specs,
            scratch_shapes=list(scratch),
        ),
        cost_estimate=pl.CostEstimate(flops=flops, bytes_accessed=moved, transcendentals=0),
        compiler_params=pltpu.CompilerParams(vmem_limit_bytes=VMEM_LIMIT),
    )(ids, *args)


def own_expert(array):
    return ((1,) + array.shape[1:], lambda i, ids: (ids[0], 0, 0))


def slot_column(table, core, slots, pair):
    experts = table.shape[0]
    owner = 2 * (iota((slots, experts), 0) // pair) + core
    spread = dot(
        jnp.where(iota((slots, experts), 1) == owner, 1.0, 0.0).astype(BF), table.astype(BF)
    )
    here = iota((slots, pair), 1) == iota((slots, pair), 0) % pair
    return jnp.sum(jnp.where(here, spread, 0.0), axis=1, keepdims=True)


def slot_row(table, core, slots, pair):
    experts = table.shape[0]
    owner = 2 * (iota((experts, slots), 1) // pair) + core
    chosen = jnp.where(iota((experts, slots), 0) == owner, 1.0, 0.0).astype(BF)
    spread = dot_tn(table.astype(BF), chosen)
    here = iota((pair, slots), 0) == iota((pair, slots), 1) % pair
    return jnp.sum(jnp.where(here, spread, 0.0), axis=0, keepdims=True)


def pick_tokens(ids, slot_ref, own_ref, other_ref, sent_ref):
    slots, pair = sent_ref.shape[0], slot_ref.shape[1]
    width = own_ref.shape[1]
    token = slot_column(slot_ref[...].astype(F32), ids[0], slots, pair)
    count = own_ref.shape[0]
    picker = jnp.where(iota((slots, count), 1).astype(F32) == token, 1.0, 0.0).astype(BF)
    empty = token < 0.0
    sent_ref[:, :width] = jnp.where(empty, EMPTY_MARK, dot(picker, own_ref[...])).astype(BF)
    sent_ref[:, width:] = jnp.where(empty, EMPTY_MARK, dot(picker, other_ref[...])).astype(BF)


def pick_grads(ids, slot_ref, gate_ref, own_ref, other_ref, sent_ref):
    slots, pair = sent_ref.shape[0], slot_ref.shape[1]
    width = own_ref.shape[1]
    token = slot_column(slot_ref[...].astype(F32), ids[0], slots, pair)
    gate = slot_column(gate_ref[...].astype(F32), ids[0], slots, pair)
    count = own_ref.shape[0]
    picker = jnp.where(iota((slots, count), 1).astype(F32) == token, 1.0, 0.0).astype(BF)
    sent_ref[:, :width] = (gate * dot(picker, own_ref[...])).astype(BF)
    sent_ref[:, width:] = (gate * dot(picker, other_ref[...])).astype(BF)


def send_chunks(ids, total_ref, own_ref, send_refs):
    chunk = own_ref.shape[0]
    parts = total_ref.shape[0] // chunk
    for k, ref in enumerate((own_ref, *send_refs)):
        at = pl.multiple_of(((ids[1] + k) % parts) * chunk, chunk)
        ref[...] = total_ref[pl.ds(at, chunk), :].astype(ref.dtype)


def forward_in(ids, got_ref, wg_ref, wu_ref, wo_g_ref, wo_u_ref,
               rows_ref, narrow_ref, widen_ref, own_ref, s1, s2, s3, total_ref):
    slots, both = got_ref.shape
    width, hidden = wg_ref.shape[1], wg_ref.shape[2]
    live_rows = rows_ref.shape[0]
    probe = got_ref[:, :128]
    lane0 = jnp.where(iota((8, 128), 1) == 0, 1.0, 0.0).astype(BF)
    live_row = dot_nt(lane0, probe) < EMPTY_MARK / 2
    before = iota((slots, slots), 0) <= iota((slots, slots), 1)
    place_row = dot(
        jnp.where(live_row, 1.0, 0.0).astype(BF), jnp.where(before, 1.0, 0.0).astype(BF)
    )
    place_row = jnp.where(live_row, place_row - 1.0, -1.0)[:1, :]
    narrow = jnp.where(iota((live_rows, slots), 0).astype(F32) == place_row, 1.0, 0.0).astype(BF)
    narrow_ref[...] = narrow
    lane0 = jnp.where(iota((128, 128), 0) == 0, 1.0, 0.0).astype(BF)
    live_col = dot(probe, lane0) < EMPTY_MARK / 2
    after = iota((slots, slots), 0) >= iota((slots, slots), 1)
    place_col = dot(
        jnp.where(after, 1.0, 0.0).astype(BF), jnp.where(live_col, 1.0, 0.0).astype(BF)
    )
    place_col = jnp.where(live_col, place_col - 1.0, -1.0)[:, :1]
    widen_ref[...] = jnp.where(
        iota((slots, live_rows), 1).astype(F32) == place_col, 1.0, 0.0
    ).astype(BF)
    rows_ref[...] = dot(narrow, got_ref[...]).astype(BF)
    mine = rows_ref[:, :width]
    other = rows_ref[:, width:]
    total_ref[:, :hidden] = dot(mine, wg_ref[0]) + dot(other, wo_g_ref[...])
    total_ref[:, hidden:] = dot(mine, wu_ref[0]) + dot(other, wo_u_ref[...])
    send_chunks(ids, total_ref, own_ref, (s1, s2, s3))


def activate(ids, own_ref, r1, r2, r3, pre_ref, hidden_ref):
    hidden = hidden_ref.shape[1]
    pre = own_ref[...] + r1[...].astype(F32) + r2[...].astype(F32) + r3[...].astype(F32)
    pre_ref[...] = pre
    gate_pre = pre[:, :hidden]
    hidden_ref[...] = (jax.nn.silu(gate_pre) * pre[:, hidden:]).astype(BF)


def gather_chunks(ids, refs, whole_ref):
    chunk = refs[0].shape[0]
    parts = whole_ref.shape[0] // chunk
    for k, ref in enumerate(refs):
        at = pl.multiple_of(((ids[1] + parts - k) % parts) * chunk, chunk)
        whole_ref[pl.ds(at, chunk), :] = ref[...]


def forward_out(ids, h0, h1, h2, h3, wd_ref, wo_d_ref, widen_ref, hidden_ref, sent_ref):
    gather_chunks(ids, (h0, h1, h2, h3), hidden_ref)
    width = wd_ref.shape[2]
    hidden = hidden_ref[...]
    widen = widen_ref[...]
    sent_ref[:, :width] = dot(widen, dot(hidden, wd_ref[0]).astype(BF)).astype(BF)
    sent_ref[:, width:] = dot(widen, dot(hidden, wo_d_ref[...]).astype(BF)).astype(BF)


def backward_in(ids, got_ref, narrow_ref, wd_ref, wo_d_ref, rows_ref, own_ref, s1, s2, s3,
                total_ref):
    width = wd_ref.shape[2]
    rows_ref[...] = dot(narrow_ref[...], got_ref[...]).astype(BF)
    total_ref[...] = dot_nt(rows_ref[:, :width], wd_ref[0]) + dot_nt(
        rows_ref[:, width:], wo_d_ref[...]
    )
    send_chunks(ids, total_ref, own_ref, (s1, s2, s3))


def deactivate(ids, own_ref, r1, r2, r3, pre_ref, out_ref):
    hidden = own_ref.shape[1]
    grad = own_ref[...] + r1[...].astype(F32) + r2[...].astype(F32) + r3[...].astype(F32)
    gate_pre = pre_ref[:, :hidden]
    up_pre = pre_ref[:, hidden:]
    sigma = jax.nn.sigmoid(gate_pre)
    slope = sigma * (1.0 + gate_pre * (1.0 - sigma))
    out_ref[:, :hidden] = (grad * up_pre * slope).astype(BF)
    out_ref[:, hidden:] = (grad * (gate_pre * sigma)).astype(BF)


def backward_out(ids, g0, g1, g2, g3, wg_ref, wu_ref, wo_g_ref, wo_u_ref, widen_ref,
                 grads_ref, sent_ref):
    gather_chunks(ids, (g0, g1, g2, g3), grads_ref)
    width, hidden = wg_ref.shape[1], wg_ref.shape[2]
    gate = grads_ref[:, :hidden]
    up = grads_ref[:, hidden:]
    widen = widen_ref[...]
    back = dot_nt(gate, wg_ref[0]) + dot_nt(up, wu_ref[0])
    sent_ref[:, :width] = dot(widen, back.astype(BF)).astype(BF)
    back = dot_nt(gate, wo_g_ref[...]) + dot_nt(up, wo_u_ref[...])
    sent_ref[:, width:] = dot(widen, back.astype(BF)).astype(BF)


def combine_out(ids, back_ref, slot_ref, gate_ref, own_ref, other_ref, mine_ref, theirs_ref,
                dots_ref):
    slots, both = back_ref.shape
    count, width = own_ref.shape
    pair = slot_ref.shape[1]
    slot_table = slot_ref[...].astype(F32)
    token_row = slot_row(slot_table, ids[0], slots, pair)
    gate_row = slot_row(gate_ref[...].astype(F32), ids[0], slots, pair)
    adder = jnp.where(
        iota((count, slots), 0).astype(F32) == token_row, gate_row, 0.0
    ).astype(BF)
    mine_ref[...] = dot(adder, back_ref[:, :width])
    theirs_ref[...] = dot(adder, back_ref[:, width:])
    token = slot_column(slot_table, ids[0], slots, pair)
    picker = jnp.where(iota((slots, count), 1).astype(F32) == token, 1.0, 0.0).astype(BF)
    terms = dot(picker, own_ref[...]) * back_ref[:, :width].astype(F32)
    terms = terms + dot(picker, other_ref[...]) * back_ref[:, width:].astype(F32)
    sums = jnp.sum(terms, axis=1, keepdims=True)
    here = iota((slots, pair), 1) == iota((slots, pair), 0) % pair
    spread = jnp.where(here, sums, 0.0)
    dots_ref[...] = jnp.sum(spread.reshape(slots // pair, pair, pair), axis=1)


def combine_back(ids, back_ref, slot_ref, mine_ref, theirs_ref):
    slots, both = back_ref.shape
    count, width = mine_ref.shape
    pair = slot_ref.shape[1]
    token_row = slot_row(slot_ref[...].astype(F32), ids[0], slots, pair)
    adder = jnp.where(iota((count, slots), 0).astype(F32) == token_row, 1.0, 0.0).astype(BF)
    mine_ref[...] = dot(adder, back_ref[:, :width])
    theirs_ref[...] = dot(adder, back_ref[:, width:])


def local(tokens, out_grad, slot_token, slot_gate, w_gate, w_up, w_down):
    senders = lax.axis_size("expert")
    devices = lax.axis_size("dp")
    parts = devices // 2
    count, width = tokens.shape
    both = 2 * width
    experts, pair = slot_token.shape[1:]
    hidden = w_gate.shape[2]
    slots = senders * pair
    chunk = LIVE // parts
    place = lax.axis_index("dp")
    core = place % 2
    ids = jnp.stack([core, place // 2]).astype(jnp.int32)
    slot_table = slot_token[0]
    gate_table = slot_gate[0]

    def swap(value):
        return lax.ppermute(value, "dp", [(i, i ^ 1) for i in range(devices)])

    def along(value, k):
        return lax.ppermute(value, "dp", [(i, (i + 2 * k) % devices) for i in range(devices)])

    def exchange(value):
        value = value.reshape(senders, pair, both)
        value = lax.all_to_all(value, "expert", split_axis=0, concat_axis=0, tiled=True)
        return value.reshape(slots, both)

    def of_other(value):
        return lax.dynamic_index_in_dim(value, 1 - core, 0, keepdims=False)

    tok_other = swap(tokens)
    grad_other = swap(out_grad)
    wo_g = swap(of_other(w_gate))
    wo_u = swap(of_other(w_up))
    wo_d = swap(of_other(w_down))
    picks = 4 * slots * count * width
    move = 4 * LIVE * slots * width
    mm = 4 * LIVE * width * hidden

    (sent_in,) = call(pick_tokens, ids, (slot_table, tokens, tok_other), [((slots, both), BF)], picks)
    got_in = exchange(sent_in)
    (sent_grad,) = call(
        pick_grads, ids, (slot_table, gate_table, out_grad, grad_other), [((slots, both), BF)], picks
    )
    got_grad = exchange(sent_grad)

    rows_in, narrow, widen, own, *sends = call(
        forward_in,
        ids,
        (got_in, w_gate, w_up, wo_g, wo_u),
        [((LIVE, both), BF), ((LIVE, slots), BF), ((slots, LIVE), BF), ((chunk, 2 * hidden), F32)]
        + [((chunk, 2 * hidden), BF)] * 3,
        move + 2 * mm,
        scratch=[pltpu.VMEM((LIVE, 2 * hidden), F32)],
        blocks={1: own_expert(w_gate), 2: own_expert(w_up)},
    )
    sums = [along(value, k + 1) for k, value in enumerate(sends)]
    pre, hidden_own = call(
        activate, ids, (own, *sums), [((chunk, 2 * hidden), F32), ((chunk, hidden), BF)],
        8 * chunk * hidden,
    )
    hidden_all, sent_out = call(
        forward_out,
        ids,
        (hidden_own, *[along(hidden_own, k) for k in range(1, parts)], w_down, wo_d, widen),
        [((LIVE, hidden), BF), ((slots, both), BF)],
        move + mm,
        blocks={parts: own_expert(w_down)},
    )
    back_out = exchange(sent_out)

    rows_grad, own, *sends = call(
        backward_in,
        ids,
        (got_grad, narrow, w_down, wo_d),
        [((LIVE, both), BF), ((chunk, hidden), F32)] + [((chunk, hidden), BF)] * 3,
        move + mm,
        scratch=[pltpu.VMEM((LIVE, hidden), F32)],
        blocks={2: own_expert(w_down)},
    )
    sums = [along(value, k + 1) for k, value in enumerate(sends)]
    (pre_grads,) = call(
        deactivate, ids, (own, *sums, pre), [((chunk, 2 * hidden), BF)], 12 * chunk * hidden
    )
    grads_all, sent_back = call(
        backward_out,
        ids,
        (pre_grads, *[along(pre_grads, k) for k in range(1, parts)], w_gate, w_up, wo_g, wo_u, widen),
        [((LIVE, 2 * hidden), BF), ((slots, both), BF)],
        move + 2 * mm,
        blocks={parts: own_expert(w_gate), parts + 1: own_expert(w_up)},
    )
    back_grad = exchange(sent_back)

    out_mine, out_theirs, dots = call(
        combine_out,
        ids,
        (back_out, slot_table, gate_table, out_grad, grad_other),
        [((count, width), F32), ((count, width), F32), ((senders, pair), F32)],
        2 * picks,
    )
    moe_out = (out_mine + swap(out_theirs)).astype(BF)
    dots = dots + along(dots, 1) + along(dots, 2) + along(dots, 3)
    dots = dots.astype(BF)
    dots_other = swap(dots)
    gate_grad = jnp.where(
        core == 0, jnp.stack([dots, dots_other], 1), jnp.stack([dots_other, dots], 1)
    ).reshape(1, experts, pair)

    def place_pair(mine, other):
        return jnp.where(core == 0, jnp.stack([mine, other]), jnp.stack([other, mine]))

    grad_in = dot_tn(rows_in, grads_all).astype(BF)
    grad_in_mine = grad_in[:width]
    grad_in_other = swap(grad_in[width:])
    grad_gate_w = place_pair(grad_in_mine[:, :hidden], grad_in_other[:, :hidden])
    grad_up_w = place_pair(grad_in_mine[:, hidden:], grad_in_other[:, hidden:])
    grad_down_mine = dot_tn(hidden_all, rows_grad[:, :width]).astype(BF)
    grad_down_other = swap(dot_tn(hidden_all, rows_grad[:, width:]).astype(BF))
    grad_down_w = place_pair(grad_down_mine, grad_down_other)

    tok_mine, tok_theirs = call(
        combine_back,
        ids,
        (back_grad, slot_table),
        [((count, width), F32), ((count, width), F32)],
        picks,
    )
    token_grad = (tok_mine + swap(tok_theirs)).astype(BF)
    return (moe_out, token_grad, gate_grad, grad_gate_w, grad_up_w, grad_down_w)


def solution(mesh):
    placed = (
        P("expert", "dp"),
        P("expert", "dp"),
        P("expert", None, None),
        P("expert", None, None),
        P("expert", "dp", None),
        P("expert", "dp", None),
        P("expert", None, "dp"),
    )
    return jax.shard_map(
        local,
        mesh=mesh,
        in_specs=placed,
        out_specs=(
            P("expert", "dp"),
            P("expert", "dp"),
            P("expert", None, None),
            P("expert", "dp", None),
            P("expert", "dp", None),
            P("expert", None, "dp"),
        ),
        check_vma=False,
    )
```

time: 335 us -> 179 us (0.53)
  the two profiles are of different devices: /device:TPU:6 before, /device:TPU:1 now
where the time goes in v1:
time: 179 us; the launch traced here: 178 us
  starting transfers between devices  72.8 us (41%)
  waiting for transfers between devices  52.8 us (29%)
  Pallas kernels  22.5 us (13%)
  local copies, waits for them, and re-layouts  16.7 us (9%)
  other arithmetic  9.67 us (5%)
  matrix products  2.68 us (1%)
    all_to_all x4, starting transfers between devices, exchange(): lax.all_to_all(value, 'expert', split_axis=0, concat_axis=0, tiled=True)  36.3 us
    all_to_all x4, waiting for transfers between devices, exchange(): lax.all_to_all(value, 'expert', split_axis=0, concat_axis=0, tiled=True)  27.1 us
    pallas_call x10, Pallas kernels, call(): pl.pallas_call(kernel, out_shape=[jax.ShapeDtypeStruct(s, t) for s, t in...  22.5 us
    ppermute x15, waiting for transfers between devices, along(): lax.ppermute(value, 'dp', [(i, (i + 2 * k) % devices) for i in range(devi...  22.5 us
    ppermute x15, starting transfers between devices, along(): lax.ppermute(value, 'dp', [(i, (i + 2 * k) % devices) for i in range(devi...  19.8 us
    ppermute x10, starting transfers between devices, swap(): return lax.ppermute(value, 'dp', [(i, i ^ 1) for i in range(devices)])  16.7 us
    unnamed x67, local copies, waits for them, and re-layouts  8.9 us
    select_n x2, other arithmetic, place_pair(): jnp.where(core == 0, jnp.stack([mine, other]), jnp.stack([other, mine]))  6.98 us
  transfers between devices with their start and end apart: 29, of which 17 were waited for; matrix products, arithmetic and copies ran while one was open for 12% of the time, Pallas kernels for 11%

profile of v1, /device:TPU:1, one launch (start us, length us, event | category | flops | bytes accessed | tf_op | source)
XLA Modules:
  0.0 178.1 jit_solution(16816605290158567143)
XLA Ops:
  0.6 3.3 %collective-permute-start = (bf16[256,512]{1,0:T(8,128)(2,1)}, bf16[256,512]{1,0:T(8,128)(2,1)S(1)}, u32[]{:S(2)}, u32[]{:S(2)}) collective-permute-start(bf16[256,512]{1,0:T(8,128)(2,1)} %own_ref.3), channel_id=1, source_target_pairs={{0,32},{32,0},{64,96},{96,64},{128,160},{160,128},{192,224},{224,1... | collective-permute-start | bytes 786440 | tf_op jit(solution)/shard_map/ppermute | solution.py:257
  5.3 0.9 copy-done.18
  6.3 2.1 %shard_map.118 = bf16[512,1024]{1,0:T(8,128)(2,1)} custom-call(s32[2]{0:T(128)S(1)} %pad_add_fusion.ids, s32[64,16]{1,0:T(8,128)S(1)} %bitcast.39, bf16[256,512]{1,0:T(8,128)(2,1)S(1)} %copy-done.18, bf16[256,512]{1,0:T(8,128)(2,1)S(1)} %collective-permute-done.other_ref), custom_call_target="tpu_custom_call" | custom-call | flops 268435456 | bytes 1576960 | tf_op jit(solution)/shard_map/pallas_call | solution.py:47
  8.4 9.5 %all-to-all-start = ((bf16[32,16,1024]{2,1,0:T(8,128)(2,1)}), bf16[32,16,1024]{2,1,0:T(8,128)(2,1)S(1)}, u32[]{:S(2)}, u32[]{:S(2)}) async-start(bf16[32,16,1024]{2,1,0:T(8,128)(2,1)} %bitcast.3), calls=%async_computation | async-start | bytes 2097152 | tf_op jit(solution)/shard_map/all_to_all | solution.py:264
  18.7 1.1 collective-permute-done.10.other_ref
  19.8 2.1 %shard_map.123 = bf16[512,1024]{1,0:T(8,128)(2,1)} custom-call(s32[2]{0:T(128)S(1)} %pad_add_fusion.ids, s32[64,16]{1,0:T(8,128)S(1)} %bitcast.40, bf16[64,16]{1,0:T(8,128)(2,1)S(1)} %bitcast.43, bf16[256,512]{1,0:T(8,128)(2,1)S(1)} %copy-done.19, bf16[256,512]{1,0:T(8,128)(2,1)S(1)} %collective-permute-done.10.other_ref), custom_call_target="tpu_custom_call" | custom-call | flops 268435456 | bytes 1579008 | tf_op jit(solution)/shard_map/pallas_call | solution.py:47
  21.9 21.1 %all-to-all-done = bf16[32,16,1024]{2,1,0:T(8,128)(2,1)S(1)} async-done(((bf16[32,16,1024]{2,1,0:T(8,128)(2,1)}), bf16[32,16,1024]{2,1,0:T(8,128)(2,1)S(1)}, u32[]{:S(2)}, u32[]{:S(2)}) %all-to-all-start) | async-done | bytes 1048608 | tf_op jit(solution)/shard_map/all_to_all | solution.py:264
  43.1 8.1 %all-to-all-start.2 = ((bf16[32,16,1024]{2,1,0:T(8,128)(2,1)}), bf16[32,16,1024]{2,1,0:T(8,128)(2,1)}, u32[]{:S(2)}, u32[]{:S(2)}) async-start(bf16[32,16,1024]{2,1,0:T(8,128)(2,1)} %bitcast.11), calls=%async_computation.2 | async-start | bytes 2097152 | tf_op jit(solution)/shard_map/all_to_all | solution.py:264
  51.3 1.6 collective-permute-start.1
  52.9 1.2 dynamic-slice_bitcast_fusion.1
  54.8 1.6 collective-permute-done.2.wo_u_ref
  56.5 3.8 %shard_map.119 = (bf16[256,1024]{1,0:T(8,128)(2,1)S(1)}, bf16[256,512]{1,0:T(8,128)(2,1)S(1)}, bf16[512,256]{1,0:T(8,128)(2,1)S(1)}, f32[64,1536]{1,0:T(8,128)S(...) custom-call(s32[2]{0:T(128)S(1)} %pad_add_fusion.ids, ...), custom_call_target="tpu_custom_call" | custom-call | flops 1073741824 | bytes 7798784 | tf_op jit(solution)/shard_map/pallas_call | solution.py:47
  61.0 1.2 collective-permute-start.3
  62.2 2.4 %collective-permute-start.4 = (bf16[64,1536]{1,0:T(8,128)(2,1)S(1)}, bf16[64,1536]{1,0:T(8,128)(2,1)S(1)}, u32[]{:S(2)}, u32[]{:S(2)}) collective-permute-start(bf16[64,1536]{1,0:T(8,128)(2,1)S(1)} %get-tuple-element.31), channel_id=1, source_target_pairs={{0,128},{32,160},{64,192},{96,224},{128,0},{160,32},{192,64},{224,... | collective-permute-start | bytes 589832 | tf_op jit(solution)/shard_map/ppermute | solution.py:260
  64.6 1.2 collective-permute-start.5
  65.8 2.8 %collective-permute-done.3.r1 = bf16[64,1536]{1,0:T(8,128)(2,1)S(1)} collective-permute-done((bf16[64,1536]{1,0:T(8,128)(2,1)S(1)}, bf16[64,1536]{1,0:T(8,128)(2,1)S(1)}, u32[]{:S(2)}, u32[]{:S(2)}) %collective-permute-start.3) | collective-permute-done | bytes 196640 | tf_op jit(solution)/shard_map/ppermute | solution.py:260
  68.6 5.2 %collective-permute-done.4.r2 = bf16[64,1536]{1,0:T(8,128)(2,1)S(1)} collective-permute-done((bf16[64,1536]{1,0:T(8,128)(2,1)S(1)}, bf16[64,1536]{1,0:T(8,128)(2,1)S(1)}, u32[]{:S(2)}, u32[]{:S(2)}) %collective-permute-start.4) | collective-permute-done | bytes 196640 | tf_op jit(solution)/shard_map/ppermute | solution.py:260
  76.1 2.8 %collective-permute-start.7 = (bf16[64,768]{1,0:T(8,128)(2,1)S(1)}, bf16[64,768]{1,0:T(8,128)(2,1)S(1)}, u32[]{:S(2)}, u32[]{:S(2)}) collective-permute-start(bf16[64,768]{1,0:T(8,128)(2,1)S(1)} %get-tuple-element.33.h0), channel_id=1, source_target_pairs={{0,128},{32,160},{64,192},{96,224},{128,0},{160,32},{192,64},{224,... | collective-permute-start | bytes 294920 | tf_op jit(solution)/shard_map/ppermute | solution.py:260
  80.3 3.2 %collective-permute-done.7.h2 = bf16[64,768]{1,0:T(8,128)(2,1)S(1)} collective-permute-done((bf16[64,768]{1,0:T(8,128)(2,1)S(1)}, bf16[64,768]{1,0:T(8,128)(2,1)S(1)}, u32[]{:S(2)}, u32[]{:S(2)}) %collective-permute-start.7) | collective-permute-done | bytes 98336 | tf_op jit(solution)/shard_map/ppermute | solution.py:260
  84.4 1.6 shard_map.121
  86.0 1.0 copy-done.11
  87.0 9.8 %all-to-all-start.1 = ((bf16[32,16,1024]{2,1,0:T(8,128)(2,1)}), bf16[32,16,1024]{2,1,0:T(8,128)(2,1)}, u32[]{:S(2)}, u32[]{:S(2)}) async-start(bf16[32,16,1024]{2,1,0:T(8,128)(2,1)} %bitcast.38), calls=%async_computation.1 | async-start | bytes 2097152 | tf_op jit(solution)/shard_map/all_to_all | solution.py:264
  96.8 0.9 copy-done.24
  98.4 3.2 %shard_map.124 = (bf16[256,1024]{1,0:T(8,128)(2,1)S(1)}, f32[64,768]{1,0:T(8,128)S(1)}, bf16[64,768]{1,0:T(8,128)(2,1)S(1)}, bf16[64,768]{1,0:T(8,128)(2,1)S(1)}, bf16[64,768]{1,0:T(8,128)(2,1)S(1)}) custom-call(s32[2]{0:T(128)S(1)} %copy-done.27, bf16[512,1024]{1,0:T(8,128)(2,1)} %bitcast.12.got_ref, bf16[256,512]{1,0:T(8,128)(2,1)S(1)} %copy-done.24, ...), custom_call_target="tpu_custom_call" | custom-call | flops 671088640 | bytes 4685824 | tf_op jit(solution)/shard_map/pallas_call | solution.py:47
  102.5 1.9 %collective-permute-start.13 = (bf16[64,768]{1,0:T(8,128)(2,1)S(1)}, bf16[64,768]{1,0:T(8,128)(2,1)S(1)}, u32[]{:S(2)}, u32[]{:S(2)}) collective-permute-start(bf16[64,768]{1,0:T(8,128)(2,1)S(1)} %get-tuple-element.41), channel_id=1, source_target_pairs={{0,128},{32,160},{64,192},{96,224},{128,0},{160,32},{192,64},{224,... | collective-permute-start | bytes 294920 | tf_op jit(solution)/shard_map/ppermute | solution.py:260
  105.0 1.8 collective-permute-done.12.r1
  106.7 1.1 collective-permute-done.13.r2
  109.8 2.9 %collective-permute-start.16 = (bf16[64,1536]{1,0:T(8,128)(2,1)S(1)}, bf16[64,1536]{1,0:T(8,128)(2,1)S(1)}, u32[]{:S(2)}, u32[]{:S(2)}) collective-permute-start(bf16[64,1536]{1,0:T(8,128)(2,1)S(1)} %shard_map.125.g0), channel_id=1, source_target_pairs={{0,128},{32,160},{64,192},{96,224},{128,0},{160,32},{192,64},{224,... | collective-permute-start | bytes 589832 | tf_op jit(solution)/shard_map/ppermute | solution.py:260
  113.5 1.8 collective-permute-done.15.g1
  115.3 4.2 %collective-permute-done.16.g2 = bf16[64,1536]{1,0:T(8,128)(2,1)S(1)} collective-permute-done((bf16[64,1536]{1,0:T(8,128)(2,1)S(1)}, bf16[64,1536]{1,0:T(8,128)(2,1)S(1)}, u32[]{:S(2)}, u32[]{:S(2)}) %collective-permute-start.16) | collective-permute-done | bytes 196640 | tf_op jit(solution)/shard_map/ppermute | solution.py:260
  119.5 4.2 %shard_map.126 = (bf16[256,1536]{1,0:T(8,128)(2,1)S(1)}, bf16[512,1024]{1,0:T(8,128)(2,1)}) custom-call(s32[2]{0:T(128)S(1)} %copy-done.27, bf16[64,1536]{1,0:T(8,128)(2,1)S(1)} %shard_map.125.g0, bf16[64,1536]{1,0:T(8,128)(2,1)S(1)} %collective-permute-done.15.g1, bf16[64,1536]{1,0:T(8,128)(2,1)S(1)} %collective-permute-done.16.g2, ...), custom_call_target="tpu_custom_call" | custom-call | flops 1073741824 | bytes 7602176 | tf_op jit(solution)/shard_map/pallas_call | solution.py:47
  123.7 1.0 convolution_convert_fusion
  124.7 1.6 copy-done.29
  126.3 1.2 slice.32
  127.6 3.3 %collective-permute-start.23 = (bf16[512,1536]{1,0:T(8,128)(2,1)}, bf16[512,1536]{1,0:T(8,128)(2,1)}, u32[]{:S(2)}, u32[]{:S(2)}) collective-permute-start(bf16[512,1536]{1,0:T(8,128)(2,1)} %slice.32), channel_id=1, source_target_pairs={{0,32},{32,0},{64,96},{96,64},{128,160},{160,128},{192,224},{224,1... | collective-permute-start | bytes 4718600 | tf_op jit(solution)/shard_map/ppermute | solution.py:257
  130.9 9.0 %all-to-all-start.3 = ((bf16[32,16,1024]{2,1,0:T(8,128)(2,1)}), bf16[32,16,1024]{2,1,0:T(8,128)(2,1)S(1)}, u32[]{:S(2)}, u32[]{:S(2)}) async-start(bf16[32,16,1024]{2,1,0:T(8,128)(2,1)} %bitcast.13), calls=%async_computation.3 | async-start | bytes 2097152 | tf_op jit(solution)/shard_map/all_to_all | solution.py:264
  139.9 1.3 convolution_convert_fusion.1
  142.0 2.7 %slice_bitcast_fusion.1 = (bf16[1,512,768]{2,1,0:T(8,128)(2,1)}, bf16[1,512,768]{2,1,0:T(8,128)(2,1)}) fusion(bf16[1024,1536]{1,0:T(8,128)(2,1)} %copy-done.29), kind=kLoop, calls=%fused_computation.8 | loop fusion | bytes 3145728 | tf_op jit(solution)/shard_map/stack | solution.py:350
  144.7 2.8 %maximum_select_fusion.2 = bf16[2,768,512]{2,1,0:T(8,128)(2,1)} fusion(bf16[1,768,512]{2,1,0:T(8,128)(2,1)} %bitcast.23, bf16[1,768,512]{2,1,0:T(8,128)(2,1)S(1)} %fusion, pred[]{:T(512)S(6)} %eq.4), kind=kLoop, calls=%fused_computation.3 | loop fusion | flops 2359296 | bytes 3145729 | tf_op jit(solution)/shard_map/jit(_where)/select_n | solution.py:350
  147.6 3.0 %shard_map.122 = (f32[256,512]{1,0:T(8,128)S(1)}, f32[256,512]{1,0:T(8,128)S(1)}, f32[32,16]{1,0:T(8,128)S(1)}) custom-call(s32[2]{0:T(128)S(1)} %copy-done.28, bf16[512,1024]{1,0:T(8,128)(2,1)} %bitcast.9.back_ref, s32[64,16]{1,0:T(8,128)S(1)} %bitcast.41, bf16[64,16]{1,0:T(8,128)(2,1)S(1)} %bitcast.44, bf16[256,512]{1,0:T(8,128)(2,1)S(1)} %copy-done.20, ...), custom_call_target="tpu_custom_call" | custom-call | flops 536870912 | bytes 2629632 | tf_op jit(solution)/shard_map/pallas_call | solution.py:47
  150.6 2.2 %collective-permute-start.21 = (f32[32,16]{1,0:T(8,128)S(1)}, f32[32,16]{1,0:T(8,128)S(1)}, u32[]{:S(2)}, u32[]{:S(2)}) collective-permute-start(f32[32,16]{1,0:T(8,128)S(1)} %get-tuple-element.47), channel_id=1, source_target_pairs={{0,192},{32,224},{64,0},{96,32},{128,64},{160,96},{192,128},{224,1... | collective-permute-start | bytes 6152 | tf_op jit(solution)/shard_map/ppermute | solution.py:260
  153.6 2.6 %slice_bitcast_fusion = (bf16[1,512,768]{2,1,0:T(8,128)(2,1)}, bf16[1,512,768]{2,1,0:T(8,128)(2,1)}) fusion(bf16[512,1536]{1,0:T(8,128)(2,1)} %collective-permute-done.23), kind=kLoop, calls=%fused_computation.7 | loop fusion | bytes 3145728 | tf_op jit(solution)/shard_map/stack | solution.py:350
  157.7 1.6 collective-permute-start.22
  159.2 5.9 %all-to-all-done.3 = bf16[32,16,1024]{2,1,0:T(8,128)(2,1)S(1)} async-done(((bf16[32,16,1024]{2,1,0:T(8,128)(2,1)}), bf16[32,16,1024]{2,1,0:T(8,128)(2,1)S(1)}, u32[]{:S(2)}, u32[]{:S(2)}) %all-to-all-start.3) | async-done | bytes 1048608 | tf_op jit(solution)/shard_map/all_to_all | solution.py:264
  165.2 1.1 shard_map.127
  166.3 4.4 %collective-permute-start.18 = (f32[256,512]{1,0:T(8,128)S(1)}, f32[256,512]{1,0:T(8,128)S(1)}, u32[]{:S(2)}, u32[]{:S(2)}) collective-permute-start(f32[256,512]{1,0:T(8,128)S(1)} %get-tuple-element.46), channel_id=1, source_target_pairs={{0,32},{32,0},{64,96},{96,64},{128,160},{160,128},{192,224},{224,1... | collective-permute-start | bytes 1572872 | tf_op jit(solution)/shard_map/ppermute | solution.py:257
  170.7 4.1 %maximum_select_fusion = (bf16[2,512,768]{2,1,0:T(8,128)(2,1)}, bf16[2,512,768]{2,1,0:T(8,128)(2,1)}) fusion(bf16[1,512,768]{2,1,0:T(8,128)(2,1)} %get-tuple-element.61, bf16[1,512,768]{2,1,0:T(8,128)(2,1)} %get-tuple-element.59, pred[]{:T(512)S(6)} %eq.4, bf16[1,512,768]{2,1,0:T(8,128)(2,1)} %get-tuple-element.58, bf16[1,512,768]{2,1,0:T(8,128)(2,1)S(1)} %copy-done.30), kind=kLoop, calls=%fused_computation.1 | loop fusion | flops 4718592 | bytes 6291457 | tf_op jit(solution)/shard_map/jit(_where)/select_n | solution.py:350
  175.5 1.8 %add_convert_fusion.1 = bf16[256,512]{1,0:T(8,128)(2,1)} fusion(f32[256,512]{1,0:T(8,128)S(1)} %get-tuple-element.36, f32[256,512]{1,0:T(8,128)} %collective-permute-done.11), kind=kLoop, calls=%fused_computation.15 | loop fusion | flops 262144 | bytes 1310720 | tf_op jit(solution)/shard_map/convert_element_type | solution.py:341
  (104 shorter events, 17.7 us)
Async XLA Ops:
  0.6 4.7 %collective-permute-start = (bf16[256,512]{1,0:T(8,128)(2,1)}, bf16[256,512]{1,0:T(8,128)(2,1)S(1)}, u32[]{:S(2)}, u32[]{:S(2)}) collective-permute-start(bf16[256,512]{1,0:T(8,128)(2,1)} %own_ref.3), channel_id=1, source_target_pairs={{0,32},{32,0},{64,96},{96,64},{128,160},{160,128},{192,224},{224,1... | collective-permute-start | bytes 786440 | tf_op jit(solution)/shard_map/ppermute | solution.py:257
  4.7 15.1 %copy-start.12 = (s32[1,64,16]{2,1,0:T(8,128)}, s32[1,64,16]{2,1,0:T(8,128)S(1)}, u32[]{:S(2)}) copy-start(s32[1,64,16]{2,1,0:T(8,128)S(1)} %copy.15) | copy-start | bytes 12292
  4.8 69.0 %copy-start.25 = (s32[2]{0:T(128)}, s32[2]{0:T(128)S(1)}, u32[]{:S(2)}) copy-start(s32[2]{0:T(128)S(1)} %pad_add_fusion.ids) | copy-start | bytes 28
  6.3 11.6 %copy-start.19 = (bf16[256,512]{1,0:T(8,128)(2,1)S(1)}, bf16[256,512]{1,0:T(8,128)(2,1)}, u32[]{:S(2)}) copy-start(bf16[256,512]{1,0:T(8,128)(2,1)} %own_ref.5) | copy-start | bytes 786436
  6.3 12.4 %copy-start.31 = (bf16[1,64,16]{1,2,0:T(8,128)(2,1)S(1)}, bf16[1,64,16]{1,2,0:T(8,128)(2,1)}, u32[]{:S(2)}) copy-start(bf16[1,64,16]{1,2,0:T(8,128)(2,1)} %param.10) | copy-start | bytes 6148
  8.4 34.7 %all-to-all-start = ((bf16[32,16,1024]{2,1,0:T(8,128)(2,1)}), bf16[32,16,1024]{2,1,0:T(8,128)(2,1)S(1)}, u32[]{:S(2)}, u32[]{:S(2)}) async-start(bf16[32,16,1024]{2,1,0:T(8,128)(2,1)} %bitcast.3), calls=%async_computation | async-start | bytes 2097152 | tf_op jit(solution)/shard_map/all_to_all | solution.py:264
  17.9 1.9 %collective-permute-start.10 = (bf16[256,512]{1,0:T(8,128)(2,1)S(1)}, bf16[256,512]{1,0:T(8,128)(2,1)S(1)}, u32[]{:S(2)}, u32[]{:S(2)}) collective-permute-start(bf16[256,512]{1,0:T(8,128)(2,1)S(1)} %copy-done.19), channel_id=1, source_target_pairs={{0,32},{32,0},{64,96},{96,64},{128,160},{160,128},{192,224},{224,1... | collective-permute-start | bytes 786440 | tf_op jit(solution)/shard_map/ppermute | solution.py:257
  19.8 23.3 %copy-start.21 = (bf16[256,512]{1,0:T(8,128)(2,1)}, bf16[256,512]{1,0:T(8,128)(2,1)S(1)}, u32[]{:S(2)}) copy-start(bf16[256,512]{1,0:T(8,128)(2,1)S(1)} %collective-permute-done.10.other_ref) | copy-start | bytes 786436
  19.8 31.4 %copy-start.1 = (bf16[2,512,768]{2,1,0:T(8,128)(2,1)S(1)}, bf16[2,512,768]{2,1,0:T(8,128)(2,1)}, u32[]{:S(2)}) copy-start(bf16[2,512,768]{2,1,0:T(8,128)(2,1)} %wg_ref.3) | copy-start | bytes 4718596
  43.1 8.1 %copy-start.3 = (bf16[32,16,1024]{2,1,0:T(8,128)(2,1)}, bf16[32,16,1024]{2,1,0:T(8,128)(2,1)S(1)}, u32[]{:S(2)}) copy-start(bf16[32,16,1024]{2,1,0:T(8,128)(2,1)S(1)} %all-to-all-done) | copy-start | bytes 3145732
  43.1 43.9 %all-to-all-start.2 = ((bf16[32,16,1024]{2,1,0:T(8,128)(2,1)}), bf16[32,16,1024]{2,1,0:T(8,128)(2,1)}, u32[]{:S(2)}, u32[]{:S(2)}) async-start(bf16[32,16,1024]{2,1,0:T(8,128)(2,1)} %bitcast.11), calls=%async_computation.2 | async-start | bytes 2097152 | tf_op jit(solution)/shard_map/all_to_all | solution.py:264
  51.3 5.2 %copy-start.4 = (bf16[32,16,1024]{2,1,0:T(8,128)(2,1)S(1)}, bf16[32,16,1024]{2,1,0:T(8,128)(2,1)}, u32[]{:S(2)}) copy-start(bf16[32,16,1024]{2,1,0:T(8,128)(2,1)} %copy-done.3) | copy-start | bytes 3145732
  51.3 3.5 %collective-permute-start.1 = (bf16[512,768]{1,0:T(8,128)(2,1)S(1)}, bf16[512,768]{1,0:T(8,128)(2,1)S(1)}, u32[]{:S(2)}, u32[]{:S(2)}) collective-permute-start(bf16[512,768]{1,0:T(8,128)(2,1)S(1)} %dynamic-slice_bitcast_fusion.2), channel_id=1, source_target_pairs={{0,32},{32,0},{64,96},{96,64},{128,160},{160,128},{192,224},{224,1... | collective-permute-start | bytes 2359304 | tf_op jit(solution)/shard_map/ppermute | solution.py:257
  54.1 2.4 %collective-permute-start.2 = (bf16[512,768]{1,0:T(8,128)(2,1)S(1)}, bf16[512,768]{1,0:T(8,128)(2,1)S(1)}, u32[]{:S(2)}, u32[]{:S(2)}) collective-permute-start(bf16[512,768]{1,0:T(8,128)(2,1)S(1)} %dynamic-slice_bitcast_fusion.1), channel_id=1, source_target_pairs={{0,32},{32,0},{64,96},{96,64},{128,160},{160,128},{192,224},{224,1... | collective-permute-start | bytes 2359304 | tf_op jit(solution)/shard_map/ppermute | solution.py:257
  54.4 25.0 %collective-permute-start.9 = (bf16[768,512]{1,0:T(8,128)(2,1)S(1)}, bf16[768,512]{1,0:T(8,128)(2,1)S(1)}, u32[]{:S(2)}, u32[]{:S(2)}) collective-permute-start(bf16[768,512]{1,0:T(8,128)(2,1)S(1)} %dynamic-slice_bitcast_fusion), channel_id=1, source_target_pairs={{0,32},{32,0},{64,96},{96,64},{128,160},{160,128},{192,224},{224,1... | collective-permute-start | bytes 2359304 | tf_op jit(solution)/shard_map/ppermute | solution.py:257
  56.5 3.8 %copy-start.5 = (bf16[512,768]{1,0:T(8,128)(2,1)}, bf16[512,768]{1,0:T(8,128)(2,1)S(1)}, u32[]{:S(2)}) copy-start(bf16[512,768]{1,0:T(8,128)(2,1)S(1)} %collective-permute-done.2.wo_u_ref) | copy-start | bytes 2359300
  61.0 22.7 %copy-start.7 = (bf16[256,1024]{1,0:T(8,128)(2,1)}, bf16[256,1024]{1,0:T(8,128)(2,1)S(1)}, u32[]{:S(2)}) copy-start(bf16[256,1024]{1,0:T(8,128)(2,1)S(1)} %get-tuple-element.48) | copy-start | bytes 1572868
  61.0 22.7 %copy-start.9 = (bf16[512,256]{1,0:T(8,128)(2,1)}, bf16[512,256]{1,0:T(8,128)(2,1)S(1)}, u32[]{:S(2)}) copy-start(bf16[512,256]{1,0:T(8,128)(2,1)S(1)} %get-tuple-element.34.widen_ref) | copy-start | bytes 786436
  61.0 7.7 %collective-permute-start.3 = (bf16[64,1536]{1,0:T(8,128)(2,1)S(1)}, bf16[64,1536]{1,0:T(8,128)(2,1)S(1)}, u32[]{:S(2)}, u32[]{:S(2)}) collective-permute-start(bf16[64,1536]{1,0:T(8,128)(2,1)S(1)} %get-tuple-element.30), channel_id=1, source_target_pairs={{0,64},{32,96},{64,128},{96,160},{128,192},{160,224},{192,0},{224,... | collective-permute-start | bytes 589832 | tf_op jit(solution)/shard_map/ppermute | solution.py:260
  62.2 11.6 %collective-permute-start.4 = (bf16[64,1536]{1,0:T(8,128)(2,1)S(1)}, bf16[64,1536]{1,0:T(8,128)(2,1)S(1)}, u32[]{:S(2)}, u32[]{:S(2)}) collective-permute-start(bf16[64,1536]{1,0:T(8,128)(2,1)S(1)} %get-tuple-element.31), channel_id=1, source_target_pairs={{0,128},{32,160},{64,192},{96,224},{128,0},{160,32},{192,64},{224,... | collective-permute-start | bytes 589832 | tf_op jit(solution)/shard_map/ppermute | solution.py:260
  64.6 9.2 %collective-permute-start.5 = (bf16[64,1536]{1,0:T(8,128)(2,1)S(1)}, bf16[64,1536]{1,0:T(8,128)(2,1)S(1)}, u32[]{:S(2)}, u32[]{:S(2)}) collective-permute-start(bf16[64,1536]{1,0:T(8,128)(2,1)S(1)} %get-tuple-element.32), channel_id=1, source_target_pairs={{0,192},{32,224},{64,0},{96,32},{128,64},{160,96},{192,128},{224,1... | collective-permute-start | bytes 589832 | tf_op jit(solution)/shard_map/ppermute | solution.py:260
  75.3 5.1 %collective-permute-start.6 = (bf16[64,768]{1,0:T(8,128)(2,1)S(1)}, bf16[64,768]{1,0:T(8,128)(2,1)S(1)}, u32[]{:S(2)}, u32[]{:S(2)}) collective-permute-start(bf16[64,768]{1,0:T(8,128)(2,1)S(1)} %get-tuple-element.33.h0), channel_id=1, source_target_pairs={{0,64},{32,96},{64,128},{96,160},{128,192},{160,224},{192,0},{224,... | collective-permute-start | bytes 294920 | tf_op jit(solution)/shard_map/ppermute | solution.py:260
  76.1 7.4 %collective-permute-start.7 = (bf16[64,768]{1,0:T(8,128)(2,1)S(1)}, bf16[64,768]{1,0:T(8,128)(2,1)S(1)}, u32[]{:S(2)}, u32[]{:S(2)}) collective-permute-start(bf16[64,768]{1,0:T(8,128)(2,1)S(1)} %get-tuple-element.33.h0), channel_id=1, source_target_pairs={{0,128},{32,160},{64,192},{96,224},{128,0},{160,32},{192,64},{224,... | collective-permute-start | bytes 294920 | tf_op jit(solution)/shard_map/ppermute | solution.py:260
  78.9 4.8 %collective-permute-start.8 = (bf16[64,768]{1,0:T(8,128)(2,1)S(1)}, bf16[64,768]{1,0:T(8,128)(2,1)S(1)}, u32[]{:S(2)}, u32[]{:S(2)}) collective-permute-start(bf16[64,768]{1,0:T(8,128)(2,1)S(1)} %get-tuple-element.33.h0), channel_id=1, source_target_pairs={{0,192},{32,224},{64,0},{96,32},{128,64},{160,96},{192,128},{224,1... | collective-permute-start | bytes 294920 | tf_op jit(solution)/shard_map/ppermute | solution.py:260
  87.0 43.9 %all-to-all-start.1 = ((bf16[32,16,1024]{2,1,0:T(8,128)(2,1)}), bf16[32,16,1024]{2,1,0:T(8,128)(2,1)}, u32[]{:S(2)}, u32[]{:S(2)}) async-start(bf16[32,16,1024]{2,1,0:T(8,128)(2,1)} %bitcast.38), calls=%async_computation.1 | async-start | bytes 2097152 | tf_op jit(solution)/shard_map/all_to_all | solution.py:264
  98.4 10.0 %copy-start.17 = (f32[64,1536]{1,0:T(8,128)S(1)}, f32[64,1536]{1,0:T(8,128)}, u32[]{:S(2)}) copy-start(f32[64,1536]{1,0:T(8,128)} %copy-done.16) | copy-start | bytes 1179652
  98.4 21.1 %copy-start.2 = (bf16[2,512,768]{2,1,0:T(8,128)(2,1)S(1)}, bf16[2,512,768]{2,1,0:T(8,128)(2,1)}, u32[]{:S(2)}) copy-start(bf16[2,512,768]{2,1,0:T(8,128)(2,1)} %wg_ref.3) | copy-start | bytes 4718596
  98.4 21.1 %copy-start.6 = (bf16[512,768]{1,0:T(8,128)(2,1)S(1)}, bf16[512,768]{1,0:T(8,128)(2,1)}, u32[]{:S(2)}) copy-start(bf16[512,768]{1,0:T(8,128)(2,1)} %copy-done.5) | copy-start | bytes 2359300
  98.4 21.1 %copy-start.10 = (bf16[512,256]{1,0:T(8,128)(2,1)S(1)}, bf16[512,256]{1,0:T(8,128)(2,1)}, u32[]{:S(2)}) copy-start(bf16[512,256]{1,0:T(8,128)(2,1)} %copy-done.9) | copy-start | bytes 786436
  101.6 17.9 %copy-start.14 = (bf16[256,1024]{1,0:T(8,128)(2,1)}, bf16[256,1024]{1,0:T(8,128)(2,1)S(1)}, u32[]{:S(2)}) copy-start(bf16[256,1024]{1,0:T(8,128)(2,1)S(1)} %get-tuple-element.51) | copy-start | bytes 1572868
  101.6 5.2 %collective-permute-start.12 = (bf16[64,768]{1,0:T(8,128)(2,1)S(1)}, bf16[64,768]{1,0:T(8,128)(2,1)S(1)}, u32[]{:S(2)}, u32[]{:S(2)}) collective-permute-start(bf16[64,768]{1,0:T(8,128)(2,1)S(1)} %get-tuple-element.40), channel_id=1, source_target_pairs={{0,64},{32,96},{64,128},{96,160},{128,192},{160,224},{192,0},{224,... | collective-permute-start | bytes 294920 | tf_op jit(solution)/shard_map/ppermute | solution.py:260
  102.5 5.4 %collective-permute-start.13 = (bf16[64,768]{1,0:T(8,128)(2,1)S(1)}, bf16[64,768]{1,0:T(8,128)(2,1)S(1)}, u32[]{:S(2)}, u32[]{:S(2)}) collective-permute-start(bf16[64,768]{1,0:T(8,128)(2,1)S(1)} %get-tuple-element.41), channel_id=1, source_target_pairs={{0,128},{32,160},{64,192},{96,224},{128,0},{160,32},{192,64},{224,... | collective-permute-start | bytes 294920 | tf_op jit(solution)/shard_map/ppermute | solution.py:260
  104.4 4.0 %collective-permute-start.14 = (bf16[64,768]{1,0:T(8,128)(2,1)S(1)}, bf16[64,768]{1,0:T(8,128)(2,1)S(1)}, u32[]{:S(2)}, u32[]{:S(2)}) collective-permute-start(bf16[64,768]{1,0:T(8,128)(2,1)S(1)} %get-tuple-element.42), channel_id=1, source_target_pairs={{0,192},{32,224},{64,0},{96,32},{128,64},{160,96},{192,128},{224,1... | collective-permute-start | bytes 294920 | tf_op jit(solution)/shard_map/ppermute | solution.py:260
  109.0 14.6 %copy-start.8 = (bf16[256,1024]{1,0:T(8,128)(2,1)S(1)}, bf16[256,1024]{1,0:T(8,128)(2,1)}, u32[]{:S(2)}) copy-start(bf16[256,1024]{1,0:T(8,128)(2,1)} %copy-done.7) | copy-start | bytes 1572868
  109.0 6.2 %collective-permute-start.15 = (bf16[64,1536]{1,0:T(8,128)(2,1)S(1)}, bf16[64,1536]{1,0:T(8,128)(2,1)S(1)}, u32[]{:S(2)}, u32[]{:S(2)}) collective-permute-start(bf16[64,1536]{1,0:T(8,128)(2,1)S(1)} %shard_map.125.g0), channel_id=1, source_target_pairs={{0,64},{32,96},{64,128},{96,160},{128,192},{160,224},{192,0},{224,... | collective-permute-start | bytes 589832 | tf_op jit(solution)/shard_map/ppermute | solution.py:260
  109.8 9.7 %collective-permute-start.16 = (bf16[64,1536]{1,0:T(8,128)(2,1)S(1)}, bf16[64,1536]{1,0:T(8,128)(2,1)S(1)}, u32[]{:S(2)}, u32[]{:S(2)}) collective-permute-start(bf16[64,1536]{1,0:T(8,128)(2,1)S(1)} %shard_map.125.g0), channel_id=1, source_target_pairs={{0,128},{32,160},{64,192},{96,224},{128,0},{160,32},{192,64},{224,... | collective-permute-start | bytes 589832 | tf_op jit(solution)/shard_map/ppermute | solution.py:260
  112.7 6.8 %collective-permute-start.17 = (bf16[64,1536]{1,0:T(8,128)(2,1)S(1)}, bf16[64,1536]{1,0:T(8,128)(2,1)S(1)}, u32[]{:S(2)}, u32[]{:S(2)}) collective-permute-start(bf16[64,1536]{1,0:T(8,128)(2,1)S(1)} %shard_map.125.g0), channel_id=1, source_target_pairs={{0,192},{32,224},{64,0},{96,32},{128,64},{160,96},{192,128},{224,1... | collective-permute-start | bytes 589832 | tf_op jit(solution)/shard_map/ppermute | solution.py:260
  127.6 12.3 %copy-start.15 = (bf16[256,1024]{1,0:T(8,128)(2,1)S(1)}, bf16[256,1024]{1,0:T(8,128)(2,1)}, u32[]{:S(2)}) copy-start(bf16[256,1024]{1,0:T(8,128)(2,1)} %copy-done.14) | copy-start | bytes 1572868
  127.6 26.1 %collective-permute-start.23 = (bf16[512,1536]{1,0:T(8,128)(2,1)}, bf16[512,1536]{1,0:T(8,128)(2,1)}, u32[]{:S(2)}, u32[]{:S(2)}) collective-permute-start(bf16[512,1536]{1,0:T(8,128)(2,1)} %slice.32), channel_id=1, source_target_pairs={{0,32},{32,0},{64,96},{96,64},{128,160},{160,128},{192,224},{224,1... | collective-permute-start | bytes 4718600 | tf_op jit(solution)/shard_map/ppermute | solution.py:257
  130.9 34.3 %all-to-all-start.3 = ((bf16[32,16,1024]{2,1,0:T(8,128)(2,1)}), bf16[32,16,1024]{2,1,0:T(8,128)(2,1)S(1)}, u32[]{:S(2)}, u32[]{:S(2)}) async-start(bf16[32,16,1024]{2,1,0:T(8,128)(2,1)} %bitcast.13), calls=%async_computation.3 | async-start | bytes 2097152 | tf_op jit(solution)/shard_map/all_to_all | solution.py:264
  141.2 3.5 %collective-permute-start.24 = (bf16[768,512]{1,0:T(8,128)(2,1)}, bf16[768,512]{1,0:T(8,128)(2,1)}, u32[]{:S(2)}, u32[]{:S(2)}) collective-permute-start(bf16[768,512]{1,0:T(8,128)(2,1)} %convolution_convert_fusion.1), channel_id=1, source_target_pairs={{0,32},{32,0},{64,96},{96,64},{128,160},{160,128},{192,224},{224,1... | collective-permute-start | bytes 2359304 | tf_op jit(solution)/shard_map/ppermute | solution.py:257
  150.6 6.3 %collective-permute-start.21 = (f32[32,16]{1,0:T(8,128)S(1)}, f32[32,16]{1,0:T(8,128)S(1)}, u32[]{:S(2)}, u32[]{:S(2)}) collective-permute-start(f32[32,16]{1,0:T(8,128)S(1)} %get-tuple-element.47), channel_id=1, source_target_pairs={{0,192},{32,224},{64,0},{96,32},{128,64},{160,96},{192,128},{224,1... | collective-permute-start | bytes 6152 | tf_op jit(solution)/shard_map/ppermute | solution.py:260
  152.7 4.4 %collective-permute-start.20 = (f32[32,16]{1,0:T(8,128)S(1)}, f32[32,16]{1,0:T(8,128)S(1)}, u32[]{:S(2)}, u32[]{:S(2)}) collective-permute-start(f32[32,16]{1,0:T(8,128)S(1)} %get-tuple-element.47), channel_id=1, source_target_pairs={{0,128},{32,160},{64,192},{96,224},{128,0},{160,32},{192,64},{224,... | collective-permute-start | bytes 6152 | tf_op jit(solution)/shard_map/ppermute | solution.py:260
  153.6 4.1 %collective-permute-start.19 = (f32[32,16]{1,0:T(8,128)S(1)}, f32[32,16]{1,0:T(8,128)S(1)}, u32[]{:S(2)}, u32[]{:S(2)}) collective-permute-start(f32[32,16]{1,0:T(8,128)S(1)} %get-tuple-element.47), channel_id=1, source_target_pairs={{0,64},{32,96},{64,128},{96,160},{128,192},{160,224},{192,0},{224,... | collective-permute-start | bytes 6152 | tf_op jit(solution)/shard_map/ppermute | solution.py:260
  156.3 19.3 %collective-permute-start.11 = (f32[256,512]{1,0:T(8,128)S(1)}, f32[256,512]{1,0:T(8,128)}, u32[]{:S(2)}, u32[]{:S(2)}) collective-permute-start(f32[256,512]{1,0:T(8,128)S(1)} %get-tuple-element.37), channel_id=1, source_target_pairs={{0,32},{32,0},{64,96},{96,64},{128,160},{160,128},{192,224},{224,1... | collective-permute-start | bytes 1572872 | tf_op jit(solution)/shard_map/ppermute | solution.py:257
  157.7 17.1 %collective-permute-start.22 = (bf16[32,16]{1,0:T(8,128)(2,1)S(1)}, bf16[32,16]{1,0:T(8,128)(2,1)S(1)}, u32[]{:S(2)}, u32[]{:S(2)}) collective-permute-start(bf16[32,16]{1,0:T(8,128)(2,1)S(1)} %add_convert_fusion.2), channel_id=1, source_target_pairs={{0,32},{32,0},{64,96},{96,64},{128,160},{160,128},{192,224},{224,1... | collective-permute-start | bytes 3080 | tf_op jit(solution)/shard_map/ppermute | solution.py:257
  165.2 5.5 %copy-start.30 = (bf16[1,512,768]{2,1,0:T(8,128)(2,1)S(1)}, bf16[1,512,768]{2,1,0:T(8,128)(2,1)}, u32[]{:S(2)}) copy-start(bf16[1,512,768]{2,1,0:T(8,128)(2,1)} %get-tuple-element.60) | copy-start | bytes 2359300
  166.3 11.0 %collective-permute-start.18 = (f32[256,512]{1,0:T(8,128)S(1)}, f32[256,512]{1,0:T(8,128)S(1)}, u32[]{:S(2)}, u32[]{:S(2)}) collective-permute-start(f32[256,512]{1,0:T(8,128)S(1)} %get-tuple-element.46), channel_id=1, source_target_pairs={{0,32},{32,0},{64,96},{96,64},{128,160},{160,128},{192,224},{224,1... | collective-permute-start | bytes 1572872 | tf_op jit(solution)/shard_map/ppermute | solution.py:257
  (13 other events, 21.9 us)

commit v2 on v1

v2 whole, which is shorter than its diff:
```python
import functools

import jax
import jax.numpy as jnp
from jax import lax
from jax.experimental import pallas as pl
from jax.experimental.pallas import tpu as pltpu
from jax.sharding import PartitionSpec as P

BF = jnp.bfloat16
F32 = jnp.float32
LIVE = 256
EMPTY_MARK = 64.0
VMEM_LIMIT = 24 * 1024 * 1024


def dot(a, b):
    return jnp.dot(a, b, preferred_element_type=F32)


def dot_nt(a, b):
    return lax.dot_general(a, b, (((1,), (1,)), ((), ())), preferred_element_type=F32)


def dot_tn(a, b):
    return lax.dot_general(a, b, (((0,), (0,)), ((), ())), preferred_element_type=F32)


def iota(shape, dim):
    return lax.broadcasted_iota(jnp.int32, shape, dim)


IN_VMEM = pl.BlockSpec(memory_space=pltpu.VMEM)
IN_HBM = pl.BlockSpec(memory_space=pltpu.HBM)


def call(kernel, ids, args, outs, flops, scratch=(), placed=(), left=(), aliases=()):
    moved = sum(a.size * a.dtype.itemsize for a in args)
    moved += sum(functools.reduce(lambda p, q: p * q, s) * jnp.dtype(t).itemsize for s, t in outs)
    args = [
        pltpu.with_memory_space_constraint(a, pltpu.HBM) if n in left else a
        for n, a in enumerate(args)
    ]
    return pl.pallas_call(
        kernel,
        out_shape=[
            pltpu.HBM(s, t) if n in placed else jax.ShapeDtypeStruct(s, t)
            for n, (s, t) in enumerate(outs)
        ],
        in_specs=[pl.BlockSpec(memory_space=pltpu.SMEM)]
        + [IN_HBM if n in left else IN_VMEM for n in range(len(args))],
        out_specs=[IN_HBM if n in placed else IN_VMEM for n in range(len(outs))],
        scratch_shapes=list(scratch),
        input_output_aliases={n + 1: m for n, m in aliases},
        cost_estimate=pl.CostEstimate(flops=flops, bytes_accessed=moved, transcendentals=0),
        compiler_params=pltpu.CompilerParams(vmem_limit_bytes=VMEM_LIMIT),
    )(ids, *args)


def slot_column(table, core, slots):
    pair, experts = table.shape
    owner = 2 * (iota((slots, experts), 0) // pair) + core
    spread = dot_nt(
        jnp.where(iota((slots, experts), 1) == owner, 1.0, 0.0).astype(BF), table.astype(BF)
    )
    here = iota((slots, pair), 1) == iota((slots, pair), 0) % pair
    return jnp.sum(jnp.where(here, spread, 0.0), axis=1, keepdims=True)


def slot_row(table, core, slots):
    pair, experts = table.shape
    owner = 2 * (iota((experts, slots), 1) // pair) + core
    chosen = jnp.where(iota((experts, slots), 0) == owner, 1.0, 0.0).astype(BF)
    spread = dot(table.astype(BF), chosen)
    here = iota((pair, slots), 0) == iota((pair, slots), 1) % pair
    return jnp.sum(jnp.where(here, spread, 0.0), axis=0, keepdims=True)


def row_picker(slot_ref, ids, slots, count):
    token = slot_column(slot_ref[...].astype(F32), ids[0], slots)
    picker = jnp.where(iota((slots, count), 1).astype(F32) == token, 1.0, 0.0).astype(BF)
    return token, picker


def started(source, target, sem):
    copy = pltpu.make_async_copy(source, target, sem)
    copy.start()
    return copy


def leave_blocks(blocks, buffer, out_ref, sems):
    width = buffer.shape[1] // len(blocks)
    copies = []
    for n, half in enumerate(blocks):
        at = pl.ds(n * width, width)
        buffer[:, at] = half()
        copies.append(started(buffer.at[:, at], out_ref.at[:, at], sems.at[n]))
    for copy in copies:
        copy.wait()


def pick_tokens(ids, slot_hbm, own_hbm, other_ref, sent_ref, buffer, sems, slot_ref, own_ref, in_sems):
    slots, both = sent_ref.shape
    slot_in = started(slot_hbm, slot_ref, in_sems.at[0])
    own_in = started(own_hbm, own_ref, in_sems.at[1])
    slot_in.wait()
    token, picker = row_picker(slot_ref, ids, slots, own_ref.shape[0])
    empty = token < 0.0
    own_in.wait()
    leave_blocks(
        [
            lambda ref=ref: jnp.where(empty, EMPTY_MARK, dot(picker, ref[...])).astype(BF)
            for ref in (own_ref, other_ref)
        ],
        buffer, sent_ref, sems,
    )


def pick_grads(ids, slot_ref, gate_ref, own_ref, other_ref, sent_ref, buffer, sems):
    slots, both = sent_ref.shape
    token, picker = row_picker(slot_ref, ids, slots, own_ref.shape[0])
    gate = slot_column(gate_ref[...].astype(F32), ids[0], slots)
    leave_blocks(
        [
            lambda ref=ref: (gate * dot(picker, ref[...])).astype(BF)
            for ref in (own_ref, other_ref)
        ],
        buffer, sent_ref, sems,
    )


def send_chunks(ids, total_ref, own_ref, send_refs):
    chunk = own_ref.shape[0]
    parts = total_ref.shape[0] // chunk
    for k, ref in enumerate((own_ref, *send_refs)):
        at = pl.multiple_of(((ids[1] + k) % parts) * chunk, chunk)
        ref[...] = total_ref[pl.ds(at, chunk), :].astype(ref.dtype)


def join_chunks(ids, refs, whole_ref):
    chunk = refs[0].shape[0]
    parts = whole_ref.shape[0] // chunk
    for k, ref in enumerate(refs):
        at = pl.multiple_of(((ids[1] + parts - k) % parts) * chunk, chunk)
        whole_ref[pl.ds(at, chunk), :] = ref[...]


def forward_in(ids, got_hbm, wo_u_hbm, wg_ref, wu_ref, wo_g_ref,
               rows_hbm, narrow_hbm, widen_hbm, own_ref, s1, s2, s3,
               total_ref, got_ref, rows_ref, narrow_ref, widen_ref, wo_u_ref, sems):
    slots, both = got_ref.shape
    width, hidden = wg_ref.shape
    live_rows = rows_ref.shape[0]
    first, rest = pl.ds(0, 128), pl.ds(128, both - 128)
    first_in = started(got_hbm.at[:, first], got_ref.at[:, first], sems.at[0])
    rest_in = started(got_hbm.at[:, rest], got_ref.at[:, rest], sems.at[1])
    wo_u_in = started(wo_u_hbm, wo_u_ref, sems.at[5])
    first_in.wait()
    probe = got_ref[:, :128]
    lane0 = jnp.where(iota((8, 128), 1) == 0, 1.0, 0.0).astype(BF)
    live_row = dot_nt(lane0, probe) < EMPTY_MARK / 2
    before = iota((slots, slots), 0) <= iota((slots, slots), 1)
    place_row = dot(
        jnp.where(live_row, 1.0, 0.0).astype(BF), jnp.where(before, 1.0, 0.0).astype(BF)
    )
    place_row = jnp.where(live_row, place_row - 1.0, -1.0)[:1, :]
    narrow = jnp.where(iota((live_rows, slots), 0).astype(F32) == place_row, 1.0, 0.0).astype(BF)
    narrow_ref[...] = narrow
    narrow_out = started(narrow_ref, narrow_hbm, sems.at[2])
    rest_in.wait()
    rows_ref[...] = dot(narrow, got_ref[...]).astype(BF)
    rows_out = started(rows_ref, rows_hbm, sems.at[3])
    mine = rows_ref[:, :width]
    other = rows_ref[:, width:]
    total_ref[:, :hidden] = dot(mine, wg_ref[...]) + dot(other, wo_g_ref[...])
    wo_u_in.wait()
    total_ref[:, hidden:] = dot(mine, wu_ref[...]) + dot(other, wo_u_ref[...])
    send_chunks(ids, total_ref, own_ref, (s1, s2, s3))
    widen_ref[...] = narrow_ref[...].T
    widen_out = started(widen_ref, widen_hbm, sems.at[4])
    narrow_out.wait()
    rows_out.wait()
    widen_out.wait()


def activate(ids, own_ref, r1, r2, r3, pre_hbm, hidden_ref, pre_ref, sems):
    hidden = hidden_ref.shape[1]
    pre = own_ref[...] + r1[...].astype(F32) + r2[...].astype(F32) + r3[...].astype(F32)
    pre_ref[...] = pre
    pre_out = started(pre_ref, pre_hbm, sems.at[0])
    hidden_ref[...] = (jax.nn.silu(pre[:, :hidden]) * pre[:, hidden:]).astype(BF)
    pre_out.wait()


def forward_out(ids, h0, h1, h2, h3, wd_ref, wo_d_ref, widen_hbm, hidden_hbm, sent_ref, buffer,
                sems, hidden_ref, widen_ref, more_sems):
    widen_in = started(widen_hbm, widen_ref, more_sems.at[1])
    join_chunks(ids, (h0, h1, h2, h3), hidden_ref)
    hidden_out = started(hidden_ref, hidden_hbm, more_sems.at[0])
    width = wd_ref.shape[1]
    out = [dot(hidden_ref[...], ref[...]).astype(BF) for ref in (wd_ref, wo_d_ref)]
    widen_in.wait()
    leave_blocks(
        [
            lambda half=half, at=at: dot(widen_ref[...], half[:, at : at + width // 2]).astype(BF)
            for half in out
            for at in (0, width // 2)
        ],
        buffer, sent_ref, sems,
    )
    hidden_out.wait()


def backward_in(ids, got_hbm, narrow_hbm, wd_hbm, wo_d_hbm, rows_hbm, own_ref, s1, s2, s3,
                total_ref, got_ref, narrow_ref, wd_ref, wo_d_ref, rows_ref, sems):
    width = wd_ref.shape[1]
    narrow_in = started(narrow_hbm, narrow_ref, sems.at[0])
    mine, other = pl.ds(0, width), pl.ds(width, width)
    mine_in = started(got_hbm.at[:, mine], got_ref.at[:, mine], sems.at[1])
    other_in = started(got_hbm.at[:, other], got_ref.at[:, other], sems.at[2])
    wd_in = started(wd_hbm, wd_ref, sems.at[3])
    wo_d_in = started(wo_d_hbm, wo_d_ref, sems.at[4])
    narrow_in.wait()
    mine_in.wait()
    rows_ref[:, :width] = dot(narrow_ref[...], got_ref[:, :width]).astype(BF)
    other_in.wait()
    rows_ref[:, width:] = dot(narrow_ref[...], got_ref[:, width:]).astype(BF)
    rows_out = started(rows_ref, rows_hbm, sems.at[5])
    wd_in.wait()
    total_ref[...] = dot_nt(rows_ref[:, :width], wd_ref[...])
    wo_d_in.wait()
    total_ref[...] += dot_nt(rows_ref[:, width:], wo_d_ref[...])
    send_chunks(ids, total_ref, own_ref, (s1, s2, s3))
    rows_out.wait()


def deactivate(ids, own_ref, r1, r2, r3, pre_ref, out_ref):
    hidden = own_ref.shape[1]
    grad = own_ref[...] + r1[...].astype(F32) + r2[...].astype(F32) + r3[...].astype(F32)
    gate_pre = pre_ref[:, :hidden]
    up_pre = pre_ref[:, hidden:]
    sigma = jax.nn.sigmoid(gate_pre)
    slope = sigma * (1.0 + gate_pre * (1.0 - sigma))
    out_ref[:, :hidden] = (grad * up_pre * slope).astype(BF)
    out_ref[:, hidden:] = (grad * (gate_pre * sigma)).astype(BF)


def backward_out(ids, g0, g1, g2, g3, wg_ref, wu_ref, wo_g_ref, wo_u_ref, widen_ref,
                 grads_hbm, sent_ref, buffer, sems, grads_ref, grads_sems):
    join_chunks(ids, (g0, g1, g2, g3), grads_ref)
    grads_out = started(grads_ref, grads_hbm, grads_sems.at[0])
    hidden = wg_ref.shape[1]
    gate = grads_ref[:, :hidden]
    up = grads_ref[:, hidden:]
    widen = widen_ref[...]

    def half(gate_w, up_w):
        back = dot_nt(gate, gate_w[...]) + dot_nt(up, up_w[...])
        return dot(widen, back.astype(BF)).astype(BF)

    leave_blocks(
        [lambda: half(wg_ref, wu_ref), lambda: half(wo_g_ref, wo_u_ref)], buffer, sent_ref, sems
    )
    grads_out.wait()


def combine_out(ids, back_hbm, own_hbm, other_hbm, slot_ref, gate_ref, mine_ref, theirs_ref,
                dots_ref, back_ref, own_ref, other_ref, sems):
    slots, both = back_ref.shape
    count, width = own_ref.shape
    pair = slot_ref.shape[0]
    mine, other = pl.ds(0, width), pl.ds(width, width)
    back_mine = started(back_hbm.at[:, mine], back_ref.at[:, mine], sems.at[0])
    own_in = started(own_hbm, own_ref, sems.at[1])
    back_other = started(back_hbm.at[:, other], back_ref.at[:, other], sems.at[2])
    other_in = started(other_hbm, other_ref, sems.at[3])
    token_row = slot_row(slot_ref[...].astype(F32), ids[0], slots)
    gate_row = slot_row(gate_ref[...].astype(F32), ids[0], slots)
    adder = jnp.where(
        iota((count, slots), 0).astype(F32) == token_row, gate_row, 0.0
    ).astype(BF)
    token, picker = row_picker(slot_ref, ids, slots, count)
    back_mine.wait()
    mine_ref[...] = dot(adder, back_ref[:, :width])
    own_in.wait()
    sums = jnp.sum(
        dot(picker, own_ref[...]) * back_ref[:, :width].astype(F32), axis=1, keepdims=True
    )
    back_other.wait()
    theirs_ref[...] = dot(adder, back_ref[:, width:])
    other_in.wait()
    sums = sums + jnp.sum(
        dot(picker, other_ref[...]) * back_ref[:, width:].astype(F32), axis=1, keepdims=True
    )
    here = iota((slots, pair), 1) == iota((slots, pair), 0) % pair
    spread = jnp.where(here, sums, 0.0)
    dots_ref[...] = jnp.sum(spread.reshape(slots // pair, pair, pair), axis=1)


def adder_of(ids, slot_ref, count, slots):
    token_row = slot_row(slot_ref[...].astype(F32), ids[0], slots)
    return jnp.where(iota((count, slots), 0).astype(F32) == token_row, 1.0, 0.0).astype(BF)


def combine_theirs(ids, back_ref, slot_ref, theirs_ref):
    count, width = theirs_ref.shape
    adder = adder_of(ids, slot_ref, count, back_ref.shape[0])
    theirs_ref[...] = dot(adder, back_ref[:, width:])


def combine_mine(ids, back_ref, slot_ref, mine_ref):
    count, width = mine_ref.shape
    adder = adder_of(ids, slot_ref, count, back_ref.shape[0])
    mine_ref[...] = dot(adder, back_ref[:, :width])


def add_halves(ids, mine_ref, got_ref, out_ref):
    out_ref[...] = (mine_ref[...] + got_ref[...]).astype(BF)


def load_rows(rows_in_hbm, grads_hbm, hidden_hbm, rows_grad_hbm, at, refs, sems):
    sources = (rows_in_hbm.at[:, at], grads_hbm, rows_grad_hbm.at[:, at], hidden_hbm)
    return [started(source, ref, sems.at[n]) for n, (source, ref) in enumerate(zip(sources, refs))]


def weights_theirs(ids, rows_in_hbm, grads_hbm, hidden_hbm, rows_grad_hbm, in_ref, down_ref,
                   rows_in_ref, grads_ref, rows_grad_ref, hidden_ref, sems):
    width = in_ref.shape[0]
    loads = load_rows(rows_in_hbm, grads_hbm, hidden_hbm, rows_grad_hbm, pl.ds(width, width),
                      (rows_in_ref, grads_ref, rows_grad_ref, hidden_ref), sems)
    loads[0].wait()
    loads[1].wait()
    in_ref[...] = dot_tn(rows_in_ref[...], grads_ref[...]).astype(BF)
    loads[2].wait()
    loads[3].wait()
    down_ref[...] = dot_tn(hidden_ref[...], rows_grad_ref[...]).astype(BF)


def weights_mine(ids, rows_in_hbm, grads_hbm, hidden_hbm, rows_grad_hbm, gate_ref, up_ref, down_ref,
                 rows_in_ref, grads_ref, rows_grad_ref, hidden_ref, mine_in, mine_down, sems):
    width, hidden = gate_ref.shape[1:]
    core = ids[0]
    loads = load_rows(rows_in_hbm, grads_hbm, hidden_hbm, rows_grad_hbm, pl.ds(0, width),
                      (rows_in_ref, grads_ref, rows_grad_ref, hidden_ref), sems)
    loads[0].wait()
    loads[1].wait()
    mine_in[...] = dot_tn(rows_in_ref[...], grads_ref[...]).astype(BF)
    stores = [
        started(mine_in.at[:, pl.ds(0, hidden)], gate_ref.at[core], sems.at[4]),
        started(mine_in.at[:, pl.ds(hidden, hidden)], up_ref.at[core], sems.at[5]),
    ]
    loads[2].wait()
    loads[3].wait()
    mine_down[...] = dot_tn(hidden_ref[...], rows_grad_ref[...]).astype(BF)
    stores.append(started(mine_down, down_ref.at[core], sems.at[6]))
    for store in stores:
        store.wait()


def weights_got(ids, got_in_ref, got_down_ref, gate_in, up_in, down_in, gate_ref, up_ref, down_ref,
                sems):
    hidden = gate_ref.shape[2]
    there = 1 - ids[0]
    stores = [
        started(got_in_ref.at[:, pl.ds(0, hidden)], gate_ref.at[there], sems.at[0]),
        started(got_in_ref.at[:, pl.ds(hidden, hidden)], up_ref.at[there], sems.at[1]),
        started(got_down_ref, down_ref.at[there], sems.at[2]),
    ]
    for store in stores:
        store.wait()


def local(tokens, out_grad, slot_token, slot_gate, w_gate, w_up, w_down):
    senders = lax.axis_size("expert")
    devices = lax.axis_size("dp")
    parts = devices // 2
    count, width = tokens.shape
    both = 2 * width
    experts, pair = slot_token.shape[1:]
    hidden = w_gate.shape[2]
    slots = senders * pair
    chunk = LIVE // parts
    place = lax.axis_index("dp")
    core = place % 2
    ids = jnp.stack([core, place // 2]).astype(jnp.int32)
    slot_table = slot_token[0].T
    gate_table = slot_gate[0].T

    def swap(value):
        return lax.ppermute(value, "dp", [(i, i ^ 1) for i in range(devices)])

    def along(value, k):
        return lax.ppermute(value, "dp", [(i, (i + 2 * k) % devices) for i in range(devices)])

    def spread(values):
        return [along(value, k + 1) for k, value in enumerate(values)]

    def gather_x(value):
        return [value] + spread([value] * (parts - 1))

    def exchange(value):
        value = value.reshape(senders, pair, both)
        value = lax.all_to_all(value, "expert", split_axis=0, concat_axis=0, tiled=True)
        return value.reshape(slots, both)

    def pick_expert(value, which):
        return lax.dynamic_index_in_dim(value, which, 0, keepdims=False)

    tok_other = swap(tokens)
    grad_other = swap(out_grad)
    wg, wu, wd = (pick_expert(w, core) for w in (w_gate, w_up, w_down))
    wo_g, wo_u, wo_d = (swap(pick_expert(w, 1 - core)) for w in (w_gate, w_up, w_down))
    picks = 4 * slots * count * width
    move = 4 * LIVE * slots * width
    mm = 4 * LIVE * width * hidden
    sent = ((slots, both), BF)
    buffers = [pltpu.VMEM((slots, both), BF), pltpu.SemaphoreType.DMA((4,))]

    def room(*shapes):
        return [pltpu.VMEM(shape, dtype) for shape, dtype in shapes]

    def sems(n):
        return [pltpu.SemaphoreType.DMA((n,))]

    (sent_in,) = call(
        pick_tokens, ids, (slot_table, tokens, tok_other), [sent], picks,
        buffers + room((slot_table.shape, jnp.int32), (tokens.shape, BF)) + sems(2), (0,), (0, 1),
    )
    got_in = exchange(sent_in)
    (sent_grad,) = call(
        pick_grads, ids, (slot_table, gate_table, out_grad, grad_other), [sent], picks, buffers, (0,)
    )
    sent_grad, wg, wu, wd, wo_g, wo_u, wo_d = lax.optimization_barrier(
        (sent_grad, wg, wu, wd, wo_g, wo_u, wo_d)
    )
    got_grad = exchange(sent_grad)

    rows_in, narrow, widen, own, *sends = call(
        forward_in,
        ids,
        (got_in, wo_u, wg, wu, wo_g),
        [
            ((LIVE, both), BF),
            ((LIVE, slots), BF),
            ((slots, LIVE), BF),
            ((chunk, 2 * hidden), F32),
        ]
        + [((chunk, 2 * hidden), BF)] * (parts - 1),
        move + 2 * mm,
        room(
            ((LIVE, 2 * hidden), F32),
            ((slots, both), BF),
            ((LIVE, both), BF),
            ((LIVE, slots), BF),
            ((slots, LIVE), BF),
            ((width, hidden), BF),
        )
        + sems(6),
        (0, 1, 2),
        (0, 1),
    )
    pre, hidden_own = call(
        activate,
        ids,
        (own, *spread(sends)),
        [((chunk, 2 * hidden), F32), ((chunk, hidden), BF)],
        8 * chunk * hidden,
        room(((chunk, 2 * hidden), F32)) + sems(1),
        (0,),
    )
    hidden_all, sent_out = call(
        forward_out,
        ids,
        (*gather_x(hidden_own), wd, wo_d, widen),
        [((LIVE, hidden), BF), sent],
        move + mm,
        buffers + room(((LIVE, hidden), BF), ((slots, LIVE), BF)) + sems(2),
        (0, 1),
        (parts + 2,),
    )
    back_out = exchange(sent_out)

    rows_grad, own, *sends = call(
        backward_in,
        ids,
        (got_grad, narrow, wd, wo_d),
        [((LIVE, both), BF), ((chunk, hidden), F32)] + [((chunk, hidden), BF)] * (parts - 1),
        move + mm,
        room(
            ((LIVE, hidden), F32),
            ((slots, both), BF),
            ((LIVE, slots), BF),
            ((hidden, width), BF),
            ((hidden, width), BF),
            ((LIVE, both), BF),
        )
        + sems(6),
        (0,),
        (0, 1, 2, 3),
    )
    (pre_grads,) = call(
        deactivate,
        ids,
        (own, *spread(sends), pre),
        [((chunk, 2 * hidden), BF)],
        12 * chunk * hidden,
    )
    grads_all, sent_back = call(
        backward_out,
        ids,
        (*gather_x(pre_grads), wg, wu, wo_g, wo_u, widen),
        [((LIVE, 2 * hidden), BF), sent],
        move + 2 * mm,
        buffers + room(((LIVE, 2 * hidden), BF)) + sems(1),
        (0, 1),
    )
    back_grad = exchange(sent_back)

    out_mine, out_theirs, dots = call(
        combine_out,
        ids,
        (back_out, out_grad, grad_other, slot_table, gate_table),
        [((count, width), F32), ((count, width), F32), ((senders, pair), F32)],
        2 * picks,
        room(((slots, both), BF), ((count, width), BF), ((count, width), BF)) + sems(4),
        (),
        (0, 1, 2),
    )
    rows_in, grads_all, hidden_all, rows_grad, out_theirs, dots = lax.optimization_barrier(
        (rows_in, grads_all, hidden_all, rows_grad, out_theirs, dots)
    )
    rows = (rows_in, grads_all, hidden_all, rows_grad)
    rows_room = room(
        ((LIVE, width), BF), ((LIVE, 2 * hidden), BF), ((LIVE, width), BF), ((LIVE, hidden), BF)
    )
    theirs_in, theirs_down = call(
        weights_theirs,
        ids,
        rows,
        [((width, 2 * hidden), BF), ((hidden, width), BF)],
        3 * mm // 2,
        rows_room + sems(4),
        (),
        (0, 1, 2, 3),
    )
    weight_shapes = [(w_gate.shape, BF), (w_up.shape, BF), (w_down.shape, BF)]
    weight_grads = call(
        weights_mine,
        ids,
        rows,
        weight_shapes,
        3 * mm // 2,
        rows_room + room(((width, 2 * hidden), BF), ((hidden, width), BF)) + sems(7),
        (0, 1, 2),
        (0, 1, 2, 3),
    )
    moe_out = (out_mine + swap(out_theirs)).astype(BF)
    *dots, weight_grads = lax.optimization_barrier((*gather_x(dots), weight_grads))
    dots = sum(dots).astype(BF)
    dots_other = swap(dots)
    gate_grad = jnp.where(
        core == 0, jnp.stack([dots, dots_other], 1), jnp.stack([dots_other, dots], 1)
    ).reshape(1, experts, pair)
    grad_gate_w, grad_up_w, grad_down_w = call(
        weights_got,
        ids,
        (swap(theirs_in), swap(theirs_down), *weight_grads),
        weight_shapes,
        0,
        sems(3),
        (0, 1, 2),
        (2, 3, 4),
        ((2, 0), (3, 1), (4, 2)),
    )
    back_grad, moe_out, gate_grad, grad_gate_w, grad_up_w, grad_down_w = lax.optimization_barrier(
        (back_grad, moe_out, gate_grad, grad_gate_w, grad_up_w, grad_down_w)
    )
    half = [((count, width), F32)]
    (tok_theirs,) = call(combine_theirs, ids, (back_grad, slot_table), half, picks // 2)
    (tok_mine,) = call(combine_mine, ids, (back_grad, slot_table), half, picks // 2)
    (token_grad,) = call(
        add_halves, ids, (tok_mine, swap(tok_theirs)), [((count, width), BF)], count * width
    )
    return (moe_out, token_grad, gate_grad, grad_gate_w, grad_up_w, grad_down_w)


def solution(mesh):
    placed = (
        P("expert", "dp"),
        P("expert", "dp"),
        P("expert", None, None),
        P("expert", None, None),
        P("expert", "dp", None),
        P("expert", "dp", None),
        P("expert", None, "dp"),
    )
    return jax.shard_map(
        local,
        mesh=mesh,
        in_specs=placed,
        out_specs=(
            P("expert", "dp"),
            P("expert", "dp"),
            P("expert", None, None),
            P("expert", "dp", None),
            P("expert", "dp", None),
            P("expert", None, "dp"),
        ),
        check_vma=False,
    )
```

time: 179 us -> 157 us (0.88)
  Pallas kernels: 22.5 us -> 37.2 us
  local copies, waits for them, and re-layouts: 16.7 us -> 4.22 us
  waiting for transfers between devices: 52.8 us -> 44.6 us
  other arithmetic: 9.67 us -> 2.07 us
  starting transfers between devices: 72.8 us -> 67.4 us
  matrix products: 2.68 us -> 0 us
    pallas_call x10 -> x15, Pallas kernels: 22.5 us -> 37.2 us  [call(): pl.pallas_call(kernel, out_shape=[pltpu.HBM(s, t) if n in placed else jax...]
    all_to_all x4, waiting for transfers between devices: 27.1 us -> 16.2 us  [exchange(): lax.all_to_all(value, 'expert', split_axis=0, concat_axis=0, tiled=True)]
    select_n x2 -> x0, other arithmetic: 6.98 us -> none  [place_pair(): jnp.where(core == 0, jnp.stack([mine, other]), jnp.stack([other, mine]))]
    unnamed x67 -> x33, local copies, waits for them, and re-layouts: 8.9 us -> 2.99 us
    another operation x2 -> x0, local copies, waits for them, and re-layouts: 5.29 us -> none  [place_pair(): jnp.stack([mine, other])]
    dot_general x3 -> x0, matrix products: 2.68 us -> none  [dot_tn(): lax.dot_general(a, b, (((0,), (0,)), ((), ())), preferred_element_type=F32)]
    ppermute x15, starting transfers between devices: 19.8 us -> 17.3 us  [along(): lax.ppermute(value, 'dp', [(i, (i + 2 * k) % devices) for i in range(devi...]
    ppermute x10, starting transfers between devices: 16.7 us -> 14.4 us  [swap(): return lax.ppermute(value, 'dp', [(i, i ^ 1) for i in range(devices)])]
  transfers between devices with their start and end apart: 29 -> 29, of which waited for: 17 -> 16; matrix products, arithmetic and copies ran while one was open for 12% -> 3% of each run, Pallas kernels for 11% -> 21%
where the time goes in v2:
time: 157 us
  starting transfers between devices  67.4 us (43%)
  waiting for transfers between devices  44.6 us (28%)
  Pallas kernels  37.2 us (24%)
  local copies, waits for them, and re-layouts  4.22 us (3%)
  other arithmetic  2.07 us (1%)
    pallas_call x15, Pallas kernels, call(): pl.pallas_call(kernel, out_shape=[pltpu.HBM(s, t) if n in placed else jax...  37.2 us
    all_to_all x4, starting transfers between devices, exchange(): lax.all_to_all(value, 'expert', split_axis=0, concat_axis=0, tiled=True)  35.7 us
    ppermute x15, waiting for transfers between devices, along(): lax.ppermute(value, 'dp', [(i, (i + 2 * k) % devices) for i in range(devi...  24.1 us
    ppermute x15, starting transfers between devices, along(): lax.ppermute(value, 'dp', [(i, (i + 2 * k) % devices) for i in range(devi...  17.3 us
    all_to_all x4, waiting for transfers between devices, exchange(): lax.all_to_all(value, 'expert', split_axis=0, concat_axis=0, tiled=True)  16.2 us
    ppermute x10, starting transfers between devices, swap(): return lax.ppermute(value, 'dp', [(i, i ^ 1) for i in range(devices)])  14.4 us
    ppermute x10, waiting for transfers between devices, swap(): return lax.ppermute(value, 'dp', [(i, i ^ 1) for i in range(devices)])  4.29 us
  transfers between devices with their start and end apart: 29, of which 16 were waited for; matrix products, arithmetic and copies ran while one was open for 3% of the time, Pallas kernels for 21%

profile of v2, /device:TPU:1, one launch (start us, length us, event | category | flops | bytes accessed | tf_op | source)
XLA Modules:
  0.0 156.5 jit_solution(3282732963670455737)
XLA Ops:
  0.6 3.3 %collective-permute-start.4 = (bf16[256,512]{1,0:T(8,128)(2,1)}, bf16[256,512]{1,0:T(8,128)(2,1)S(1)}, u32[]{:S(2)}, u32[]{:S(2)}) collective-permute-start(bf16[256,512]{1,0:T(8,128)(2,1)} %own_hbm.2), channel_id=1, source_target_pairs={{0,32},{32,0},{64,96},{96,64},{128,160},{160,128},{192,224},{224,1... | collective-permute-start | bytes 786440 | tf_op jit(solution)/shard_map/ppermute | solution.py:390
  4.0 1.3 collective-permute-done.4.other_ref
  5.3 2.8 %shard_map.119 = bf16[512,1024]{1,0:T(8,128)(2,1)} custom-call(s32[2]{0:T(128)S(1)} %pad_add_fusion.ids, s32[16,64]{1,0:T(8,128)} %bitcast.33, bf16[256,512]{1,0:T(8,128)(2,1)} %own_hbm.2, bf16[256,512]{1,0:T(8,128)(2,1)S(1)} %collective-permute-done.4.other_ref), custom_call_target="tpu_custom_call" | custom-call | flops 268435456 | bytes 1576960 | tf_op jit(solution)/shard_map/pallas_call | solution.py:44
  8.2 9.6 %all-to-all-start.1 = ((bf16[32,16,1024]{2,1,0:T(8,128)(2,1)}), bf16[32,16,1024]{2,1,0:T(8,128)(2,1)}, u32[]{:S(2)}, u32[]{:S(2)}) async-start(bf16[32,16,1024]{2,1,0:T(8,128)(2,1)} %bitcast.41), calls=%async_computation.1 | async-start | bytes 2097152 | tf_op jit(solution)/shard_map/all_to_all | solution.py:403
  20.1 1.0 dynamic-slice_bitcast_fusion
  21.6 2.1 %collective-permute-done.other_ref.other_hbm = bf16[256,512]{1,0:T(8,128)(2,1)S(1)} collective-permute-done((bf16[256,512]{1,0:T(8,128)(2,1)S(1)}, bf16[256,512]{1,0:T(8,128)(2,1)S(1)}, u32[]{:S(2)}, u32[]{:S(2)}) %collective-permute-start) | collective-permute-done | bytes 262176 | tf_op jit(solution)/shard_map/ppermute | solution.py:390
  23.8 2.0 %shard_map.118 = bf16[512,1024]{1,0:T(8,128)(2,1)} custom-call(s32[2]{0:T(128)S(1)} %pad_add_fusion.ids, s32[16,64]{1,0:T(8,128)S(1)} %bitcast.34, bf16[16,64]{1,0:T(8,128)(2,1)S(1)} %bitcast.38, bf16[256,512]{1,0:T(8,128)(2,1)S(1)} %copy-done.8, bf16[256,512]{1,0:T(8,128)(2,1)S(1)} %collective-permute-done.other_ref.other_hbm), custom_call_target="tpu_custom_call" | custom-call | flops 268435456 | bytes 1579008 | tf_op jit(solution)/shard_map/pallas_call | solution.py:44
  25.9 0.9 copy-done.3
  26.8 16.2 %all-to-all-done.1 = bf16[32,16,1024]{2,1,0:T(8,128)(2,1)} async-done(((bf16[32,16,1024]{2,1,0:T(8,128)(2,1)}), bf16[32,16,1024]{2,1,0:T(8,128)(2,1)}, u32[]{:S(2)}, u32[]{:S(2)}) %all-to-all-start.1) | async-done | bytes 1048608 | tf_op jit(solution)/shard_map/all_to_all | solution.py:403
  43.0 8.1 %all-to-all-start = ((bf16[32,16,1024]{2,1,0:T(8,128)(2,1)}), bf16[32,16,1024]{2,1,0:T(8,128)(2,1)}, u32[]{:S(2)}, u32[]{:S(2)}) async-start(bf16[32,16,1024]{2,1,0:T(8,128)(2,1)} %bitcast.40), calls=%async_computation | async-start | bytes 2097152 | tf_op jit(solution)/shard_map/all_to_all | solution.py:403
  51.1 4.2 %shard_map.120 = (bf16[256,1024]{1,0:T(8,128)(2,1)}, bf16[256,512]{1,0:T(8,128)(2,1)}, bf16[512,256]{1,0:T(8,128)(2,1)}, f32[64,1536]{1,0:T(8,128)S(1)}, bf16[64...) custom-call(s32[2]{0:T(128)S(1)} %pad_add_fusion.ids, ...), custom_call_target="tpu_custom_call" | custom-call | flops 1073741824 | bytes 6225920 | tf_op jit(solution)/shard_map/pallas_call | solution.py:44
  55.3 1.3 collective-permute-start.8
  56.6 2.4 %collective-permute-start.9 = (bf16[64,1536]{1,0:T(8,128)(2,1)S(1)}, bf16[64,1536]{1,0:T(8,128)(2,1)S(1)}, u32[]{:S(2)}, u32[]{:S(2)}) collective-permute-start(bf16[64,1536]{1,0:T(8,128)(2,1)S(1)} %get-tuple-element.75), channel_id=1, source_target_pairs={{0,128},{32,160},{64,192},{96,224},{128,0},{160,32},{192,64},{224,... | collective-permute-start | bytes 589832 | tf_op jit(solution)/shard_map/ppermute | solution.py:393
  59.1 1.2 collective-permute-start.10
  60.2 1.4 collective-permute-done.8.r1
  61.6 5.2 %collective-permute-done.9.r2 = bf16[64,1536]{1,0:T(8,128)(2,1)S(1)} collective-permute-done((bf16[64,1536]{1,0:T(8,128)(2,1)S(1)}, bf16[64,1536]{1,0:T(8,128)(2,1)S(1)}, u32[]{:S(2)}, u32[]{:S(2)}) %collective-permute-start.9) | collective-permute-done | bytes 196640 | tf_op jit(solution)/shard_map/ppermute | solution.py:393
  66.8 1.4 shard_map.122
  68.2 2.8 %collective-permute-start.16 = (bf16[64,768]{1,0:T(8,128)(2,1)S(1)}, bf16[64,768]{1,0:T(8,128)(2,1)S(1)}, u32[]{:S(2)}, u32[]{:S(2)}) collective-permute-start(bf16[64,768]{1,0:T(8,128)(2,1)S(1)} %get-tuple-element.80.h0), channel_id=1, source_target_pairs={{0,192},{32,224},{64,0},{96,32},{128,64},{160,96},{192,128},{224,1... | collective-permute-start | bytes 294920 | tf_op jit(solution)/shard_map/ppermute | solution.py:393
  71.0 1.3 collective-permute-start.15
  72.3 1.3 collective-permute-done.16.h3
  73.6 2.8 %collective-permute-done.15.h2 = bf16[64,768]{1,0:T(8,128)(2,1)S(1)} collective-permute-done((bf16[64,768]{1,0:T(8,128)(2,1)S(1)}, bf16[64,768]{1,0:T(8,128)(2,1)S(1)}, u32[]{:S(2)}, u32[]{:S(2)}) %collective-permute-start.15) | collective-permute-done | bytes 98336 | tf_op jit(solution)/shard_map/ppermute | solution.py:393
  76.4 1.1 collective-permute-done.14.h1
  77.4 3.3 %shard_map.125 = (bf16[256,768]{1,0:T(8,128)(2,1)}, bf16[512,1024]{1,0:T(8,128)(2,1)}) custom-call(s32[2]{0:T(128)S(1)} %pad_add_fusion.ids, bf16[64,768]{1,0:T(8,128)(2,1)S(1)} %get-tuple-element.80.h0, bf16[64,768]{1,0:T(8,128)(2,1)S(1)} %collective-permute-done.14.h1, bf16[64,768]{1,0:T(8,128)(2,1)S(1)} %collective-permute-done.15.h2, ...), custom_call_target="tpu_custom_call" | custom-call | flops 671088640 | bytes 3670016 | tf_op jit(solution)/shard_map/pallas_call | solution.py:44
  80.8 8.8 %all-to-all-start.3 = ((bf16[32,16,1024]{2,1,0:T(8,128)(2,1)}), bf16[32,16,1024]{2,1,0:T(8,128)(2,1)S(1)}, u32[]{:S(2)}, u32[]{:S(2)}) async-start(bf16[32,16,1024]{2,1,0:T(8,128)(2,1)} %bitcast.44), calls=%async_computation.3 | async-start | bytes 2097152 | tf_op jit(solution)/shard_map/all_to_all | solution.py:403
  89.6 3.3 %shard_map.121 = (bf16[256,1024]{1,0:T(8,128)(2,1)}, f32[64,768]{1,0:T(8,128)S(1)}, bf16[64,768]{1,0:T(8,128)(2,1)S(1)}, bf16[64,768]{1,0:T(8,128)(2,1)S(1)}, bf16[64,768]{1,0:T(8,128)(2,1)S(1)}) custom-call(s32[2]{0:T(128)S(1)} %pad_add_fusion.ids, bf16[512,1024]{1,0:T(8,128)(2,1)} %bitcast.13.got_hbm, bf16[256,512]{1,0:T(8,128)(2,1)} %get-tuple-element.66.narrow_hbm, ...), custom_call_target="tpu_custom_call" | custom-call | flops 671088640 | bytes 3899392 | tf_op jit(solution)/shard_map/pallas_call | solution.py:44
  93.3 1.2 collective-permute-start.6
  94.5 2.0 %collective-permute-start.7 = (bf16[64,768]{1,0:T(8,128)(2,1)S(1)}, bf16[64,768]{1,0:T(8,128)(2,1)S(1)}, u32[]{:S(2)}, u32[]{:S(2)}) collective-permute-start(bf16[64,768]{1,0:T(8,128)(2,1)S(1)} %get-tuple-element.72), channel_id=1, source_target_pairs={{0,192},{32,224},{64,0},{96,32},{128,64},{160,96},{192,128},{224,1... | collective-permute-start | bytes 294920 | tf_op jit(solution)/shard_map/ppermute | solution.py:393
  96.5 2.3 %collective-permute-done.5.r1 = bf16[64,768]{1,0:T(8,128)(2,1)S(1)} collective-permute-done((bf16[64,768]{1,0:T(8,128)(2,1)S(1)}, bf16[64,768]{1,0:T(8,128)(2,1)S(1)}, u32[]{:S(2)}, u32[]{:S(2)}) %collective-permute-start.5) | collective-permute-done | bytes 98336 | tf_op jit(solution)/shard_map/ppermute | solution.py:393
  99.9 2.8 %collective-permute-start.13 = (bf16[64,1536]{1,0:T(8,128)(2,1)S(1)}, bf16[64,1536]{1,0:T(8,128)(2,1)S(1)}, u32[]{:S(2)}, u32[]{:S(2)}) collective-permute-start(bf16[64,1536]{1,0:T(8,128)(2,1)S(1)} %shard_map.123.g0), channel_id=1, source_target_pairs={{0,192},{32,224},{64,0},{96,32},{128,64},{160,96},{192,128},{224,1... | collective-permute-start | bytes 589832 | tf_op jit(solution)/shard_map/ppermute | solution.py:393
  103.4 4.0 %collective-permute-done.13.g3 = bf16[64,1536]{1,0:T(8,128)(2,1)S(1)} collective-permute-done((bf16[64,1536]{1,0:T(8,128)(2,1)S(1)}, bf16[64,1536]{1,0:T(8,128)(2,1)S(1)}, u32[]{:S(2)}, u32[]{:S(2)}) %collective-permute-start.13) | collective-permute-done | bytes 196640 | tf_op jit(solution)/shard_map/ppermute | solution.py:393
  107.4 1.6 %collective-permute-done.12.g2 = bf16[64,1536]{1,0:T(8,128)(2,1)S(1)} collective-permute-done((bf16[64,1536]{1,0:T(8,128)(2,1)S(1)}, bf16[64,1536]{1,0:T(8,128)(2,1)S(1)}, u32[]{:S(2)}, u32[]{:S(2)}) %collective-permute-start.12) | collective-permute-done | bytes 196640 | tf_op jit(solution)/shard_map/ppermute | solution.py:393
  109.1 2.1 %collective-permute-done.11.g1 = bf16[64,1536]{1,0:T(8,128)(2,1)S(1)} collective-permute-done((bf16[64,1536]{1,0:T(8,128)(2,1)S(1)}, bf16[64,1536]{1,0:T(8,128)(2,1)S(1)}, u32[]{:S(2)}, u32[]{:S(2)}) %collective-permute-start.11) | collective-permute-done | bytes 196640 | tf_op jit(solution)/shard_map/ppermute | solution.py:393
  111.1 3.1 %shard_map.124 = (bf16[256,1536]{1,0:T(8,128)(2,1)}, bf16[512,1024]{1,0:T(8,128)(2,1)}) custom-call(s32[2]{0:T(128)S(1)} %pad_add_fusion.ids, bf16[64,1536]{1,0:T(8,128)(2,1)S(1)} %shard_map.123.g0, bf16[64,1536]{1,0:T(8,128)(2,1)S(1)} %collective-permute-done.11.g1, bf16[64,1536]{1,0:T(8,128)(2,1)S(1)} %collective-permute-done.12.g2, ...), custom_call_target="tpu_custom_call" | custom-call | flops 1073741824 | bytes 6029312 | tf_op jit(solution)/shard_map/pallas_call | solution.py:44
  114.2 9.2 %all-to-all-start.2 = ((bf16[32,16,1024]{2,1,0:T(8,128)(2,1)}), bf16[32,16,1024]{2,1,0:T(8,128)(2,1)S(1)}, u32[]{:S(2)}, u32[]{:S(2)}) async-start(bf16[32,16,1024]{2,1,0:T(8,128)(2,1)} %bitcast.42), calls=%async_computation.2 | async-start | bytes 2097152 | tf_op jit(solution)/shard_map/all_to_all | solution.py:403
  123.5 3.5 %shard_map.126 = (f32[256,512]{1,0:T(8,128)S(1)}, f32[256,512]{1,0:T(8,128)}, f32[32,16]{1,0:T(8,128)S(1)}) custom-call(s32[2]{0:T(128)S(1)} %pad_add_fusion.ids, bf16[512,1024]{1,0:T(8,128)(2,1)} %bitcast.43, bf16[256,512]{1,0:T(8,128)(2,1)} %own_hbm.3, bf16[256,512]{1,0:T(8,128)(2,1)} %copy-done.9, s32[16,64]{1,0:T(8,128)S(1)} %bitcast.35, ...), custom_call_target="tpu_custom_call" | custom-call | flops 536870912 | bytes 2629632 | tf_op jit(solution)/shard_map/pallas_call | solution.py:44
  126.9 0.8 copy-done.5
  127.8 3.9 %shard_map.128 = (bf16[512,1536]{1,0:T(8,128)(2,1)}, bf16[768,512]{1,0:T(8,128)(2,1)}) custom-call(s32[2]{0:T(128)S(1)} %pad_add_fusion.ids, bf16[256,1024]{1,0:T(8,128)(2,1)} %get-tuple-element.91.rows_in_hbm, bf16[256,1536]{1,0:T(8,128)(2,1)} %get-tuple-element.92.grads_hbm, bf16[256,768]{1,0:T(8,128)(2,1)} %get-tuple-element.93.hidden_hbm, ...), custom_call_target="tpu_custom_call" | custom-call | flops 603979776 | bytes 4587520 | tf_op jit(solution)/shard_map/pallas_call | solution.py:44
  131.7 6.3 %collective-permute-start.22 = (bf16[512,1536]{1,0:T(8,128)(2,1)}, bf16[512,1536]{1,0:T(8,128)(2,1)S(1)}, u32[]{:S(2)}, u32[]{:S(2)}) collective-permute-start(bf16[512,1536]{1,0:T(8,128)(2,1)} %get-tuple-element.102), channel_id=1, source_target_pairs={{0,32},{32,0},{64,96},{96,64},{128,160},{160,128},{192,224},{224,1... | collective-permute-start | bytes 4718600 | tf_op jit(solution)/shard_map/ppermute | solution.py:390
  138.7 0.9 collective-permute-start.19
  139.6 1.7 %collective-permute-done.20 = f32[32,16]{1,0:T(8,128)S(1)} collective-permute-done((f32[32,16]{1,0:T(8,128)S(1)}, f32[32,16]{1,0:T(8,128)S(1)}, u32[]{:S(2)}, u32[]{:S(2)}) %collective-permute-start.20) | collective-permute-done | bytes 2080 | tf_op jit(solution)/shard_map/ppermute | solution.py:393
  141.3 3.8 %shard_map.127 = (bf16[2,512,768]{2,1,0:T(8,128)(2,1)}, bf16[2,512,768]{2,1,0:T(8,128)(2,1)}, bf16[2,768,512]{2,1,0:T(8,128)(2,1)}) custom-call(s32[2]{0:T(128)S(1)} %pad_add_fusion.ids, bf16[256,1024]{1,0:T(8,128)(2,1)} %get-tuple-element.91.rows_in_hbm, bf16[256,1536]{1,0:T(8,128)(2,1)} %get-tuple-element.92.grads_hbm, ...), custom_call_target="tpu_custom_call" | custom-call | flops 603979776 | bytes 6946816 | tf_op jit(solution)/shard_map/pallas_call | solution.py:44
  145.4 1.9 %collective-permute-start.21 = (bf16[32,16]{1,0:T(8,128)(2,1)S(1)}, bf16[32,16]{1,0:T(8,128)(2,1)S(1)}, u32[]{:S(2)}, u32[]{:S(2)}) collective-permute-start(bf16[32,16]{1,0:T(8,128)(2,1)S(1)} %add_convert_fusion.1), channel_id=1, source_target_pairs={{0,32},{32,0},{64,96},{96,64},{128,160},{160,128},{192,224},{224,1... | collective-permute-start | bytes 3080 | tf_op jit(solution)/shard_map/ppermute | solution.py:390
  147.3 0.8 collective-permute-done.21
  148.2 2.0 %add_convert_fusion = bf16[256,512]{1,0:T(8,128)(2,1)} fusion(f32[256,512]{1,0:T(8,128)} %copy-done.5, f32[256,512]{1,0:T(8,128)} %collective-permute-done.17), kind=kLoop, calls=%fused_computation.6 | loop fusion | flops 262144 | bytes 1310720 | tf_op jit(solution)/shard_map/convert_element_type | solution.py:557
  150.2 2.0 %shard_map.129 = (bf16[2,512,768]{2,1,0:T(8,128)(2,1)}, bf16[2,512,768]{2,1,0:T(8,128)(2,1)}, bf16[2,768,512]{2,1,0:T(8,128)(2,1)}) custom-call(s32[2]{0:T(128)S(1)} %pad_add_fusion.ids, bf16[512,1536]{1,0:T(8,128)(2,1)S(1)} %collective-permute-done.22.got_in_ref, ...), custom_call_target="tpu_custom_call", output_to_operand_aliasing={{0}: (3, {}), {1}: (4, {}), {2}: (5, {})} | custom-call | bytes 11796480 | tf_op jit(solution)/shard_map/pallas_call | solution.py:44
  152.2 0.9 shard_map.131
  154.2 0.9 shard_map.130.mine_ref
  155.2 1.3 shard_map.132
  (66 shorter events, 7.3 us)
Async XLA Ops:
  0.6 4.7 %collective-permute-start.4 = (bf16[256,512]{1,0:T(8,128)(2,1)}, bf16[256,512]{1,0:T(8,128)(2,1)S(1)}, u32[]{:S(2)}, u32[]{:S(2)}) collective-permute-start(bf16[256,512]{1,0:T(8,128)(2,1)} %own_hbm.2), channel_id=1, source_target_pairs={{0,32},{32,0},{64,96},{96,64},{128,160},{160,128},{192,224},{224,1... | collective-permute-start | bytes 786440 | tf_op jit(solution)/shard_map/ppermute | solution.py:390
  5.3 12.5 %copy-start.12 = (bf16[2,512,768]{2,1,0:T(8,128)(2,1)S(1)}, bf16[2,512,768]{2,1,0:T(8,128)(2,1)}, u32[]{:S(2)}) copy-start(bf16[2,512,768]{2,1,0:T(8,128)(2,1)} %param.11) | copy-start | bytes 4718596
  8.2 34.8 %all-to-all-start.1 = ((bf16[32,16,1024]{2,1,0:T(8,128)(2,1)}), bf16[32,16,1024]{2,1,0:T(8,128)(2,1)}, u32[]{:S(2)}, u32[]{:S(2)}) async-start(bf16[32,16,1024]{2,1,0:T(8,128)(2,1)} %bitcast.41), calls=%async_computation.1 | async-start | bytes 2097152 | tf_op jit(solution)/shard_map/all_to_all | solution.py:403
  17.8 1.4 copy-start.13
  17.9 2.2 %copy-start.14 = (bf16[2,768,512]{2,1,0:T(8,128)(2,1)S(1)}, bf16[2,768,512]{2,1,0:T(8,128)(2,1)}, u32[]{:S(2)}) copy-start(bf16[2,768,512]{2,1,0:T(8,128)(2,1)} %param.13) | copy-start | bytes 4718596
  18.0 7.9 %collective-permute-start.1 = (bf16[512,768]{1,0:T(8,128)(2,1)S(1)}, bf16[512,768]{1,0:T(8,128)(2,1)S(1)}, u32[]{:S(2)}, u32[]{:S(2)}) collective-permute-start(bf16[512,768]{1,0:T(8,128)(2,1)S(1)} %get-tuple-element.126), channel_id=1, source_target_pairs={{0,32},{32,0},{64,96},{96,64},{128,160},{160,128},{192,224},{224,1... | collective-permute-start | bytes 2359304 | tf_op jit(solution)/shard_map/ppermute | solution.py:390
  19.3 2.1 %copy-start.8 = (bf16[256,512]{1,0:T(8,128)(2,1)S(1)}, bf16[256,512]{1,0:T(8,128)(2,1)}, u32[]{:S(2)}) copy-start(bf16[256,512]{1,0:T(8,128)(2,1)} %own_hbm.3) | copy-start | bytes 786436
  19.3 4.4 %copy-start.10 = (s32[1,64,16]{1,2,0:T(8,128)S(1)}, s32[1,64,16]{1,2,0:T(8,128)}, u32[]{:S(2)}) copy-start(s32[1,64,16]{1,2,0:T(8,128)} %param.9) | copy-start | bytes 12292
  19.4 4.4 %copy-start.11 = (bf16[1,64,16]{1,2,0:T(8,128)(2,1)S(1)}, bf16[1,64,16]{1,2,0:T(8,128)(2,1)}, u32[]{:S(2)}) copy-start(bf16[1,64,16]{1,2,0:T(8,128)(2,1)} %param.10) | copy-start | bytes 6148
  19.4 6.5 %collective-permute-start.2 = (bf16[512,768]{1,0:T(8,128)(2,1)S(1)}, bf16[512,768]{1,0:T(8,128)(2,1)S(1)}, u32[]{:S(2)}, u32[]{:S(2)}) collective-permute-start(bf16[512,768]{1,0:T(8,128)(2,1)S(1)} %get-tuple-element.124), channel_id=1, source_target_pairs={{0,32},{32,0},{64,96},{96,64},{128,160},{160,128},{192,224},{224,1... | collective-permute-start | bytes 2359304 | tf_op jit(solution)/shard_map/ppermute | solution.py:390
  21.1 4.7 %collective-permute-start.3 = (bf16[768,512]{1,0:T(8,128)(2,1)S(1)}, bf16[768,512]{1,0:T(8,128)(2,1)S(1)}, u32[]{:S(2)}, u32[]{:S(2)}) collective-permute-start(bf16[768,512]{1,0:T(8,128)(2,1)S(1)} %get-tuple-element.122), channel_id=1, source_target_pairs={{0,32},{32,0},{64,96},{96,64},{128,160},{160,128},{192,224},{224,1... | collective-permute-start | bytes 2359304 | tf_op jit(solution)/shard_map/ppermute | solution.py:390
  21.4 2.4 %collective-permute-start = (bf16[256,512]{1,0:T(8,128)(2,1)S(1)}, bf16[256,512]{1,0:T(8,128)(2,1)S(1)}, u32[]{:S(2)}, u32[]{:S(2)}) collective-permute-start(bf16[256,512]{1,0:T(8,128)(2,1)S(1)} %copy-done.8), channel_id=1, source_target_pairs={{0,32},{32,0},{64,96},{96,64},{128,160},{160,128},{192,224},{224,1... | collective-permute-start | bytes 786440 | tf_op jit(solution)/shard_map/ppermute | solution.py:390
  23.8 2.1 %copy-start.9 = (bf16[256,512]{1,0:T(8,128)(2,1)}, bf16[256,512]{1,0:T(8,128)(2,1)S(1)}, u32[]{:S(2)}) copy-start(bf16[256,512]{1,0:T(8,128)(2,1)S(1)} %collective-permute-done.other_ref.other_hbm) | copy-start | bytes 786436
  25.8 25.2 %copy-start = (bf16[512,768]{1,0:T(8,128)(2,1)}, bf16[512,768]{1,0:T(8,128)(2,1)S(1)}, u32[]{:S(2)}) copy-start(bf16[512,768]{1,0:T(8,128)(2,1)S(1)} %collective-permute-done.2.wo_u_hbm.wo_u_ref) | copy-start | bytes 2359300
  25.9 0.9 copy-start.3
  43.0 37.8 %all-to-all-start = ((bf16[32,16,1024]{2,1,0:T(8,128)(2,1)}), bf16[32,16,1024]{2,1,0:T(8,128)(2,1)}, u32[]{:S(2)}, u32[]{:S(2)}) async-start(bf16[32,16,1024]{2,1,0:T(8,128)(2,1)} %bitcast.40), calls=%async_computation | async-start | bytes 2097152 | tf_op jit(solution)/shard_map/all_to_all | solution.py:403
  51.1 26.3 %copy-start.2 = (bf16[768,512]{1,0:T(8,128)(2,1)S(1)}, bf16[768,512]{1,0:T(8,128)(2,1)}, u32[]{:S(2)}) copy-start(bf16[768,512]{1,0:T(8,128)(2,1)} %get-tuple-element.67.wd_hbm.wd_ref) | copy-start | bytes 2359300
  51.1 26.3 %copy-start.4 = (bf16[768,512]{1,0:T(8,128)(2,1)S(1)}, bf16[768,512]{1,0:T(8,128)(2,1)}, u32[]{:S(2)}) copy-start(bf16[768,512]{1,0:T(8,128)(2,1)} %copy-done.3) | copy-start | bytes 2359300
  55.3 6.3 %collective-permute-start.8 = (bf16[64,1536]{1,0:T(8,128)(2,1)S(1)}, bf16[64,1536]{1,0:T(8,128)(2,1)S(1)}, u32[]{:S(2)}, u32[]{:S(2)}) collective-permute-start(bf16[64,1536]{1,0:T(8,128)(2,1)S(1)} %get-tuple-element.74), channel_id=1, source_target_pairs={{0,64},{32,96},{64,128},{96,160},{128,192},{160,224},{192,0},{224,... | collective-permute-start | bytes 589832 | tf_op jit(solution)/shard_map/ppermute | solution.py:393
  56.6 10.2 %collective-permute-start.9 = (bf16[64,1536]{1,0:T(8,128)(2,1)S(1)}, bf16[64,1536]{1,0:T(8,128)(2,1)S(1)}, u32[]{:S(2)}, u32[]{:S(2)}) collective-permute-start(bf16[64,1536]{1,0:T(8,128)(2,1)S(1)} %get-tuple-element.75), channel_id=1, source_target_pairs={{0,128},{32,160},{64,192},{96,224},{128,0},{160,32},{192,64},{224,... | collective-permute-start | bytes 589832 | tf_op jit(solution)/shard_map/ppermute | solution.py:393
  59.1 7.7 %collective-permute-start.10 = (bf16[64,1536]{1,0:T(8,128)(2,1)S(1)}, bf16[64,1536]{1,0:T(8,128)(2,1)S(1)}, u32[]{:S(2)}, u32[]{:S(2)}) collective-permute-start(bf16[64,1536]{1,0:T(8,128)(2,1)S(1)} %get-tuple-element.76), channel_id=1, source_target_pairs={{0,192},{32,224},{64,0},{96,32},{128,64},{160,96},{192,128},{224,1... | collective-permute-start | bytes 589832 | tf_op jit(solution)/shard_map/ppermute | solution.py:393
  68.2 5.4 %collective-permute-start.16 = (bf16[64,768]{1,0:T(8,128)(2,1)S(1)}, bf16[64,768]{1,0:T(8,128)(2,1)S(1)}, u32[]{:S(2)}, u32[]{:S(2)}) collective-permute-start(bf16[64,768]{1,0:T(8,128)(2,1)S(1)} %get-tuple-element.80.h0), channel_id=1, source_target_pairs={{0,192},{32,224},{64,0},{96,32},{128,64},{160,96},{192,128},{224,1... | collective-permute-start | bytes 294920 | tf_op jit(solution)/shard_map/ppermute | solution.py:393
  71.0 5.4 %collective-permute-start.15 = (bf16[64,768]{1,0:T(8,128)(2,1)S(1)}, bf16[64,768]{1,0:T(8,128)(2,1)S(1)}, u32[]{:S(2)}, u32[]{:S(2)}) collective-permute-start(bf16[64,768]{1,0:T(8,128)(2,1)S(1)} %get-tuple-element.80.h0), channel_id=1, source_target_pairs={{0,128},{32,160},{64,192},{96,224},{128,0},{160,32},{192,64},{224,... | collective-permute-start | bytes 294920 | tf_op jit(solution)/shard_map/ppermute | solution.py:393
  72.3 5.1 %collective-permute-start.14 = (bf16[64,768]{1,0:T(8,128)(2,1)S(1)}, bf16[64,768]{1,0:T(8,128)(2,1)S(1)}, u32[]{:S(2)}, u32[]{:S(2)}) collective-permute-start(bf16[64,768]{1,0:T(8,128)(2,1)S(1)} %get-tuple-element.80.h0), channel_id=1, source_target_pairs={{0,64},{32,96},{64,128},{96,160},{128,192},{160,224},{192,0},{224,... | collective-permute-start | bytes 294920 | tf_op jit(solution)/shard_map/ppermute | solution.py:393
  80.8 33.4 %all-to-all-start.3 = ((bf16[32,16,1024]{2,1,0:T(8,128)(2,1)}), bf16[32,16,1024]{2,1,0:T(8,128)(2,1)S(1)}, u32[]{:S(2)}, u32[]{:S(2)}) async-start(bf16[32,16,1024]{2,1,0:T(8,128)(2,1)} %bitcast.44), calls=%async_computation.3 | async-start | bytes 2097152 | tf_op jit(solution)/shard_map/all_to_all | solution.py:403
  89.5 9.7 %copy-start.6 = (f32[64,1536]{1,0:T(8,128)S(1)}, f32[64,1536]{1,0:T(8,128)}, u32[]{:S(2)}) copy-start(f32[64,1536]{1,0:T(8,128)} %get-tuple-element.77.pre_ref) | copy-start | bytes 1179652
  89.5 21.6 %copy-start.1 = (bf16[512,768]{1,0:T(8,128)(2,1)S(1)}, bf16[512,768]{1,0:T(8,128)(2,1)}, u32[]{:S(2)}) copy-start(bf16[512,768]{1,0:T(8,128)(2,1)} %copy-done) | copy-start | bytes 2359300
  89.5 21.6 %copy-start.7 = (bf16[512,256]{1,0:T(8,128)(2,1)S(1)}, bf16[512,256]{1,0:T(8,128)(2,1)}, u32[]{:S(2)}) copy-start(bf16[512,256]{1,0:T(8,128)(2,1)} %get-tuple-element.78.widen_ref.widen_hbm) | copy-start | bytes 786436
  92.9 6.0 %collective-permute-start.5 = (bf16[64,768]{1,0:T(8,128)(2,1)S(1)}, bf16[64,768]{1,0:T(8,128)(2,1)S(1)}, u32[]{:S(2)}, u32[]{:S(2)}) collective-permute-start(bf16[64,768]{1,0:T(8,128)(2,1)S(1)} %get-tuple-element.70), channel_id=1, source_target_pairs={{0,64},{32,96},{64,128},{96,160},{128,192},{160,224},{192,0},{224,... | collective-permute-start | bytes 294920 | tf_op jit(solution)/shard_map/ppermute | solution.py:393
  93.3 5.5 %collective-permute-start.6 = (bf16[64,768]{1,0:T(8,128)(2,1)S(1)}, bf16[64,768]{1,0:T(8,128)(2,1)S(1)}, u32[]{:S(2)}, u32[]{:S(2)}) collective-permute-start(bf16[64,768]{1,0:T(8,128)(2,1)S(1)} %get-tuple-element.71), channel_id=1, source_target_pairs={{0,128},{32,160},{64,192},{96,224},{128,0},{160,32},{192,64},{224,... | collective-permute-start | bytes 294920 | tf_op jit(solution)/shard_map/ppermute | solution.py:393
  94.5 4.7 %collective-permute-start.7 = (bf16[64,768]{1,0:T(8,128)(2,1)S(1)}, bf16[64,768]{1,0:T(8,128)(2,1)S(1)}, u32[]{:S(2)}, u32[]{:S(2)}) collective-permute-start(bf16[64,768]{1,0:T(8,128)(2,1)S(1)} %get-tuple-element.72), channel_id=1, source_target_pairs={{0,192},{32,224},{64,0},{96,32},{128,64},{160,96},{192,128},{224,1... | collective-permute-start | bytes 294920 | tf_op jit(solution)/shard_map/ppermute | solution.py:393
  99.9 7.5 %collective-permute-start.13 = (bf16[64,1536]{1,0:T(8,128)(2,1)S(1)}, bf16[64,1536]{1,0:T(8,128)(2,1)S(1)}, u32[]{:S(2)}, u32[]{:S(2)}) collective-permute-start(bf16[64,1536]{1,0:T(8,128)(2,1)S(1)} %shard_map.123.g0), channel_id=1, source_target_pairs={{0,192},{32,224},{64,0},{96,32},{128,64},{160,96},{192,128},{224,1... | collective-permute-start | bytes 589832 | tf_op jit(solution)/shard_map/ppermute | solution.py:393
  102.7 6.4 %collective-permute-start.12 = (bf16[64,1536]{1,0:T(8,128)(2,1)S(1)}, bf16[64,1536]{1,0:T(8,128)(2,1)S(1)}, u32[]{:S(2)}, u32[]{:S(2)}) collective-permute-start(bf16[64,1536]{1,0:T(8,128)(2,1)S(1)} %shard_map.123.g0), channel_id=1, source_target_pairs={{0,128},{32,160},{64,192},{96,224},{128,0},{160,32},{192,64},{224,... | collective-permute-start | bytes 589832 | tf_op jit(solution)/shard_map/ppermute | solution.py:393
  103.0 8.1 %collective-permute-start.11 = (bf16[64,1536]{1,0:T(8,128)(2,1)S(1)}, bf16[64,1536]{1,0:T(8,128)(2,1)S(1)}, u32[]{:S(2)}, u32[]{:S(2)}) collective-permute-start(bf16[64,1536]{1,0:T(8,128)(2,1)S(1)} %shard_map.123.g0), channel_id=1, source_target_pairs={{0,64},{32,96},{64,128},{96,160},{128,192},{160,224},{192,0},{224,... | collective-permute-start | bytes 589832 | tf_op jit(solution)/shard_map/ppermute | solution.py:393
  114.2 9.3 %copy-start.15 = (bf16[32,16,1024]{2,1,0:T(8,128)(2,1)}, bf16[32,16,1024]{2,1,0:T(8,128)(2,1)S(1)}, u32[]{:S(2)}) copy-start(bf16[32,16,1024]{2,1,0:T(8,128)(2,1)S(1)} %all-to-all-done.3) | copy-start | bytes 3145732
  114.2 37.9 %all-to-all-start.2 = ((bf16[32,16,1024]{2,1,0:T(8,128)(2,1)}), bf16[32,16,1024]{2,1,0:T(8,128)(2,1)S(1)}, u32[]{:S(2)}, u32[]{:S(2)}) async-start(bf16[32,16,1024]{2,1,0:T(8,128)(2,1)} %bitcast.42), calls=%async_computation.2 | async-start | bytes 2097152 | tf_op jit(solution)/shard_map/all_to_all | solution.py:403
  126.9 0.8 copy-start.5
  131.7 18.5 %collective-permute-start.22 = (bf16[512,1536]{1,0:T(8,128)(2,1)}, bf16[512,1536]{1,0:T(8,128)(2,1)S(1)}, u32[]{:S(2)}, u32[]{:S(2)}) collective-permute-start(bf16[512,1536]{1,0:T(8,128)(2,1)} %get-tuple-element.102), channel_id=1, source_target_pairs={{0,32},{32,0},{64,96},{96,64},{128,160},{160,128},{192,224},{224,1... | collective-permute-start | bytes 4718600 | tf_op jit(solution)/shard_map/ppermute | solution.py:390
  137.9 12.2 %collective-permute-start.23 = (bf16[768,512]{1,0:T(8,128)(2,1)}, bf16[768,512]{1,0:T(8,128)(2,1)S(1)}, u32[]{:S(2)}, u32[]{:S(2)}) collective-permute-start(bf16[768,512]{1,0:T(8,128)(2,1)} %get-tuple-element.103), channel_id=1, source_target_pairs={{0,32},{32,0},{64,96},{96,64},{128,160},{160,128},{192,224},{224,1... | collective-permute-start | bytes 2359304 | tf_op jit(solution)/shard_map/ppermute | solution.py:390
  138.0 10.2 %collective-permute-start.17 = (f32[256,512]{1,0:T(8,128)}, f32[256,512]{1,0:T(8,128)}, u32[]{:S(2)}, u32[]{:S(2)}) collective-permute-start(f32[256,512]{1,0:T(8,128)} %get-tuple-element.89), channel_id=1, source_target_pairs={{0,32},{32,0},{64,96},{96,64},{128,160},{160,128},{192,224},{224,1... | collective-permute-start | bytes 1572872 | tf_op jit(solution)/shard_map/ppermute | solution.py:390
  138.4 2.9 %collective-permute-start.20 = (f32[32,16]{1,0:T(8,128)S(1)}, f32[32,16]{1,0:T(8,128)S(1)}, u32[]{:S(2)}, u32[]{:S(2)}) collective-permute-start(f32[32,16]{1,0:T(8,128)S(1)} %get-tuple-element.98), channel_id=1, source_target_pairs={{0,192},{32,224},{64,0},{96,32},{128,64},{160,96},{192,128},{224,1... | collective-permute-start | bytes 6152 | tf_op jit(solution)/shard_map/ppermute | solution.py:393
  138.7 6.4 %collective-permute-start.19 = (f32[32,16]{1,0:T(8,128)S(1)}, f32[32,16]{1,0:T(8,128)S(1)}, u32[]{:S(2)}, u32[]{:S(2)}) collective-permute-start(f32[32,16]{1,0:T(8,128)S(1)} %get-tuple-element.98), channel_id=1, source_target_pairs={{0,128},{32,160},{64,192},{96,224},{128,0},{160,32},{192,64},{224,... | collective-permute-start | bytes 6152 | tf_op jit(solution)/shard_map/ppermute | solution.py:393
  141.3 4.1 %collective-permute-start.18 = (f32[32,16]{1,0:T(8,128)S(1)}, f32[32,16]{1,0:T(8,128)S(1)}, u32[]{:S(2)}, u32[]{:S(2)}) collective-permute-start(f32[32,16]{1,0:T(8,128)S(1)} %get-tuple-element.98), channel_id=1, source_target_pairs={{0,64},{32,96},{64,128},{96,160},{128,192},{160,224},{192,0},{224,... | collective-permute-start | bytes 6152 | tf_op jit(solution)/shard_map/ppermute | solution.py:393
  145.4 2.7 %collective-permute-start.21 = (bf16[32,16]{1,0:T(8,128)(2,1)S(1)}, bf16[32,16]{1,0:T(8,128)(2,1)S(1)}, u32[]{:S(2)}, u32[]{:S(2)}) collective-permute-start(bf16[32,16]{1,0:T(8,128)(2,1)S(1)} %add_convert_fusion.1), channel_id=1, source_target_pairs={{0,32},{32,0},{64,96},{96,64},{128,160},{160,128},{192,224},{224,1... | collective-permute-start | bytes 3080 | tf_op jit(solution)/shard_map/ppermute | solution.py:390
  153.1 2.1 %collective-permute-start.24 = (f32[256,512]{1,0:T(8,128)S(1)}, f32[256,512]{1,0:T(8,128)S(1)}, u32[]{:S(2)}, u32[]{:S(2)}) collective-permute-start(f32[256,512]{1,0:T(8,128)S(1)} %shard_map.131), channel_id=1, source_target_pairs={{0,32},{32,0},{64,96},{96,64},{128,160},{160,128},{192,224},{224,1... | collective-permute-start | bytes 1572872 | tf_op jit(solution)/shard_map/ppermute | solution.py:390

commit v3 on v2

--- a/solution.py
+++ b/solution.py
@@ -99,21 +99,31 @@
         copy.wait()
 
 
-def pick_tokens(ids, slot_hbm, own_hbm, other_ref, sent_ref, buffer, sems, slot_ref, own_ref, in_sems):
-    slots, both = sent_ref.shape
-    slot_in = started(slot_hbm, slot_ref, in_sems.at[0])
-    own_in = started(own_hbm, own_ref, in_sems.at[1])
+def pick_own(ids, slot_hbm, tokens_hbm, half_ref, picker_ref, slot_ref, tokens_ref, sems):
+    slots = half_ref.shape[0]
+    slot_in = started(slot_hbm, slot_ref, sems.at[0])
+    tokens_in = started(tokens_hbm, tokens_ref, sems.at[1])
     slot_in.wait()
-    token, picker = row_picker(slot_ref, ids, slots, own_ref.shape[0])
-    empty = token < 0.0
-    own_in.wait()
-    leave_blocks(
-        [
-            lambda ref=ref: jnp.where(empty, EMPTY_MARK, dot(picker, ref[...])).astype(BF)
-            for ref in (own_ref, other_ref)
-        ],
-        buffer, sent_ref, sems,
-    )
+    token, picker = row_picker(slot_ref, ids, slots, tokens_ref.shape[0])
+    picker_ref[...] = picker
+    tokens_in.wait()
+    half_ref[...] = jnp.where(token < 0.0, EMPTY_MARK, dot(picker, tokens_ref[...])).astype(BF)
+
+
+def pick_other(ids, half_ref, picker_ref, tokens_ref, sent_hbm, buffer, sems):
+    slots, width = half_ref.shape
+    stores = [started(half_ref, sent_hbm.at[:, pl.ds(0, width)], sems.at[0])]
+    chunk = slots // 2
+    for n in range(2):
+        at = pl.ds(n * chunk, chunk)
+        picker = picker_ref[at, :]
+        empty = jnp.sum(picker.astype(F32), axis=1, keepdims=True) < 0.5
+        buffer[at, :] = jnp.where(empty, EMPTY_MARK, dot(picker, tokens_ref[...])).astype(BF)
+        stores.append(
+            started(buffer.at[at, :], sent_hbm.at[at, pl.ds(width, width)], sems.at[1 + n])
+        )
+    for store in stores:
+        store.wait()
 
 
 def pick_grads(ids, slot_ref, gate_ref, own_ref, other_ref, sent_ref, buffer, sems):
@@ -146,27 +156,26 @@
 
 
 def forward_in(ids, got_hbm, wo_u_hbm, wg_ref, wu_ref, wo_g_ref,
-               rows_hbm, narrow_hbm, widen_hbm, own_ref, s1, s2, s3,
-               total_ref, got_ref, rows_ref, narrow_ref, widen_ref, wo_u_ref, sems):
+               rows_hbm, narrow_hbm, widen_ref, own_ref, s1, s2, s3,
+               total_ref, got_ref, rows_ref, narrow_ref, wo_u_ref, before_ref, sems):
     slots, both = got_ref.shape
     width, hidden = wg_ref.shape
     live_rows = rows_ref.shape[0]
     first, rest = pl.ds(0, 128), pl.ds(128, both - 128)
     first_in = started(got_hbm.at[:, first], got_ref.at[:, first], sems.at[0])
     rest_in = started(got_hbm.at[:, rest], got_ref.at[:, rest], sems.at[1])
-    wo_u_in = started(wo_u_hbm, wo_u_ref, sems.at[5])
+    wo_u_in = started(wo_u_hbm, wo_u_ref, sems.at[4])
+    before = iota((slots, slots), 0) <= iota((slots, slots), 1)
+    before_ref[...] = jnp.where(before, 1.0, 0.0).astype(BF)
+    lane0 = jnp.where(iota((8, 128), 1) == 0, 1.0, 0.0).astype(BF)
     first_in.wait()
-    probe = got_ref[:, :128]
-    lane0 = jnp.where(iota((8, 128), 1) == 0, 1.0, 0.0).astype(BF)
-    live_row = dot_nt(lane0, probe) < EMPTY_MARK / 2
-    before = iota((slots, slots), 0) <= iota((slots, slots), 1)
-    place_row = dot(
-        jnp.where(live_row, 1.0, 0.0).astype(BF), jnp.where(before, 1.0, 0.0).astype(BF)
-    )
+    live_row = dot_nt(lane0, got_ref[:, :128]) < EMPTY_MARK / 2
+    place_row = dot(jnp.where(live_row, 1.0, 0.0).astype(BF), before_ref[...])
     place_row = jnp.where(live_row, place_row - 1.0, -1.0)[:1, :]
     narrow = jnp.where(iota((live_rows, slots), 0).astype(F32) == place_row, 1.0, 0.0).astype(BF)
     narrow_ref[...] = narrow
     narrow_out = started(narrow_ref, narrow_hbm, sems.at[2])
+    widen_ref[...] = narrow_ref[...].T
     rest_in.wait()
     rows_ref[...] = dot(narrow, got_ref[...]).astype(BF)
     rows_out = started(rows_ref, rows_hbm, sems.at[3])
@@ -176,39 +185,38 @@
     wo_u_in.wait()
     total_ref[:, hidden:] = dot(mine, wu_ref[...]) + dot(other, wo_u_ref[...])
     send_chunks(ids, total_ref, own_ref, (s1, s2, s3))
-    widen_ref[...] = narrow_ref[...].T
-    widen_out = started(widen_ref, widen_hbm, sems.at[4])
     narrow_out.wait()
     rows_out.wait()
-    widen_out.wait()
-
-
-def activate(ids, own_ref, r1, r2, r3, pre_hbm, hidden_ref, pre_ref, sems):
+
+
+def activate(ids, own_ref, r1, r2, r3, pre_ref, hidden_ref):
     hidden = hidden_ref.shape[1]
     pre = own_ref[...] + r1[...].astype(F32) + r2[...].astype(F32) + r3[...].astype(F32)
     pre_ref[...] = pre
-    pre_out = started(pre_ref, pre_hbm, sems.at[0])
     hidden_ref[...] = (jax.nn.silu(pre[:, :hidden]) * pre[:, hidden:]).astype(BF)
-    pre_out.wait()
-
-
-def forward_out(ids, h0, h1, h2, h3, wd_ref, wo_d_ref, widen_hbm, hidden_hbm, sent_ref, buffer,
-                sems, hidden_ref, widen_ref, more_sems):
-    widen_in = started(widen_hbm, widen_ref, more_sems.at[1])
+
+
+def forward_out(ids, h0, h1, h2, h3, wd_ref, wo_d_ref, widen_ref, pre_ref, hidden_hbm, sent_ref,
+                widen_hbm, pre_hbm, buffer, sems, hidden_ref, more_sems):
+    kept = [
+        started(widen_ref, widen_hbm, more_sems.at[0]),
+        started(pre_ref, pre_hbm, more_sems.at[1]),
+    ]
     join_chunks(ids, (h0, h1, h2, h3), hidden_ref)
-    hidden_out = started(hidden_ref, hidden_hbm, more_sems.at[0])
-    width = wd_ref.shape[1]
-    out = [dot(hidden_ref[...], ref[...]).astype(BF) for ref in (wd_ref, wo_d_ref)]
-    widen_in.wait()
+    kept.append(started(hidden_ref, hidden_hbm, more_sems.at[2]))
+    half = wd_ref.shape[1] // 2
     leave_blocks(
         [
-            lambda half=half, at=at: dot(widen_ref[...], half[:, at : at + width // 2]).astype(BF)
-            for half in out
-            for at in (0, width // 2)
+            lambda ref=ref, at=at: dot(
+                widen_ref[...], dot(hidden_ref[...], ref[:, at : at + half]).astype(BF)
+            ).astype(BF)
+            for ref in (wd_ref, wo_d_ref)
+            for at in (0, half)
         ],
         buffer, sent_ref, sems,
     )
-    hidden_out.wait()
+    for copy in kept:
+        copy.wait()
 
 
 def backward_in(ids, got_hbm, narrow_hbm, wd_hbm, wo_d_hbm, rows_hbm, own_ref, s1, s2, s3,
@@ -264,8 +272,12 @@
     grads_out.wait()
 
 
-def combine_out(ids, back_hbm, own_hbm, other_hbm, slot_ref, gate_ref, mine_ref, theirs_ref,
-                dots_ref, back_ref, own_ref, other_ref, sems):
+def fetch(ids, source_hbm, out_ref, sems):
+    started(source_hbm, out_ref, sems.at[0]).wait()
+
+
+def combine_out(ids, back_hbm, own_hbm, other_hbm, slot_ref, gate_ref, mine_hbm, theirs_ref,
+                dots_ref, back_ref, own_ref, other_ref, mine_ref, sems):
     slots, both = back_ref.shape
     count, width = own_ref.shape
     pair = slot_ref.shape[0]
@@ -282,6 +294,7 @@
     token, picker = row_picker(slot_ref, ids, slots, count)
     back_mine.wait()
     mine_ref[...] = dot(adder, back_ref[:, :width])
+    mine_out = started(mine_ref, mine_hbm, sems.at[4])
     own_in.wait()
     sums = jnp.sum(
         dot(picker, own_ref[...]) * back_ref[:, :width].astype(F32), axis=1, keepdims=True
@@ -295,6 +308,7 @@
     here = iota((slots, pair), 1) == iota((slots, pair), 0) % pair
     spread = jnp.where(here, sums, 0.0)
     dots_ref[...] = jnp.sum(spread.reshape(slots // pair, pair, pair), axis=1)
+    mine_out.wait()
 
 
 def adder_of(ids, slot_ref, count, slots):
@@ -312,10 +326,6 @@
     count, width = mine_ref.shape
     adder = adder_of(ids, slot_ref, count, back_ref.shape[0])
     mine_ref[...] = dot(adder, back_ref[:, :width])
-
-
-def add_halves(ids, mine_ref, got_ref, out_ref):
-    out_ref[...] = (mine_ref[...] + got_ref[...]).astype(BF)
 
 
 def load_rows(rows_in_hbm, grads_hbm, hidden_hbm, rows_grad_hbm, at, refs, sems):
@@ -422,9 +432,13 @@
     def sems(n):
         return [pltpu.SemaphoreType.DMA((n,))]
 
+    own_half, picker = call(
+        pick_own, ids, (slot_table, tokens), [((slots, width), BF), ((slots, count), BF)],
+        picks // 2, room((slot_table.shape, jnp.int32), (tokens.shape, BF)) + sems(2), (), (0, 1),
+    )
     (sent_in,) = call(
-        pick_tokens, ids, (slot_table, tokens, tok_other), [sent], picks,
-        buffers + room((slot_table.shape, jnp.int32), (tokens.shape, BF)) + sems(2), (0,), (0, 1),
+        pick_other, ids, (own_half, picker, tok_other), [sent], picks // 2,
+        room(((slots, width), BF)) + sems(3), (0,),
     )
     got_in = exchange(sent_in)
     (sent_grad,) = call(
@@ -452,11 +466,11 @@
             ((slots, both), BF),
             ((LIVE, both), BF),
             ((LIVE, slots), BF),
-            ((slots, LIVE), BF),
             ((width, hidden), BF),
+            ((slots, slots), BF),
         )
-        + sems(6),
-        (0, 1, 2),
+        + sems(5),
+        (0, 1),
         (0, 1),
     )
     pre, hidden_own = call(
@@ -465,18 +479,15 @@
         (own, *spread(sends)),
         [((chunk, 2 * hidden), F32), ((chunk, hidden), BF)],
         8 * chunk * hidden,
-        room(((chunk, 2 * hidden), F32)) + sems(1),
-        (0,),
-    )
-    hidden_all, sent_out = call(
+    )
+    hidden_all, sent_out, widen, pre = call(
         forward_out,
         ids,
-        (*gather_x(hidden_own), wd, wo_d, widen),
-        [((LIVE, hidden), BF), sent],
+        (*gather_x(hidden_own), wd, wo_d, widen, pre),
+        [((LIVE, hidden), BF), sent, ((slots, LIVE), BF), ((chunk, 2 * hidden), F32)],
         move + mm,
-        buffers + room(((LIVE, hidden), BF), ((slots, LIVE), BF)) + sems(2),
-        (0, 1),
-        (parts + 2,),
+        buffers + room(((LIVE, hidden), BF)) + sems(3),
+        (0, 1, 2, 3),
     )
     back_out = exchange(sent_out)
 
@@ -505,6 +516,8 @@
         [((chunk, 2 * hidden), BF)],
         12 * chunk * hidden,
     )
+    wo_u, pre_grads = lax.optimization_barrier((wo_u, pre_grads))
+    (wo_u,) = call(fetch, ids, (wo_u,), [(wo_u.shape, BF)], 0, sems(1), (), (0,))
     grads_all, sent_back = call(
         backward_out,
         ids,
@@ -522,8 +535,11 @@
         (back_out, out_grad, grad_other, slot_table, gate_table),
         [((count, width), F32), ((count, width), F32), ((senders, pair), F32)],
         2 * picks,
-        room(((slots, both), BF), ((count, width), BF), ((count, width), BF)) + sems(4),
-        (),
+        room(
+            ((slots, both), BF), ((count, width), BF), ((count, width), BF), ((count, width), F32)
+        )
+        + sems(5),
+        (0,),
         (0, 1, 2),
     )
     rows_in, grads_all, hidden_all, rows_grad, out_theirs, dots = lax.optimization_barrier(
@@ -560,7 +576,8 @@
     dots_other = swap(dots)
     gate_grad = jnp.where(
         core == 0, jnp.stack([dots, dots_other], 1), jnp.stack([dots_other, dots], 1)
-    ).reshape(1, experts, pair)
+    )
+    gate_grad = gate_grad.reshape(experts, pair).T
     grad_gate_w, grad_up_w, grad_down_w = call(
         weights_got,
         ids,
@@ -578,9 +595,8 @@
     half = [((count, width), F32)]
     (tok_theirs,) = call(combine_theirs, ids, (back_grad, slot_table), half, picks // 2)
     (tok_mine,) = call(combine_mine, ids, (back_grad, slot_table), half, picks // 2)
-    (token_grad,) = call(
-        add_halves, ids, (tok_mine, swap(tok_theirs)), [((count, width), BF)], count * width
-    )
+    token_grad = (tok_mine + swap(tok_theirs)).astype(BF)
+    gate_grad = gate_grad.T.reshape(1, experts, pair)
     return (moe_out, token_grad, gate_grad, grad_gate_w, grad_up_w, grad_down_w)
 
 

time: 157 us -> 155 us (0.987)
    pallas_call x15 -> x16, Pallas kernels: 37.2 us -> 37.3 us  [call(): pl.pallas_call(kernel, out_shape=[pltpu.HBM(s, t) if n in placed else jax...]
  transfers between devices with their start and end apart: 29 -> 29, of which waited for: 16 -> 15; matrix products, arithmetic and copies ran while one was open for 3% -> 2% of each run, Pallas kernels for 21% -> 23%
where the time goes in v3:
time: 155 us; the launch traced here: 154 us
  starting transfers between devices  66.6 us (43%)
  waiting for transfers between devices  43.2 us (28%)
  Pallas kernels  37.3 us (24%)
  local copies, waits for them, and re-layouts  3.15 us (2%)
  other arithmetic  2.85 us (2%)
    pallas_call x16, Pallas kernels, call(): pl.pallas_call(kernel, out_shape=[pltpu.HBM(s, t) if n in placed else jax...  37.3 us
    all_to_all x4, starting transfers between devices, exchange(): lax.all_to_all(value, 'expert', split_axis=0, concat_axis=0, tiled=True)  35.6 us
    ppermute x15, waiting for transfers between devices, along(): lax.ppermute(value, 'dp', [(i, (i + 2 * k) % devices) for i in range(devi...  23.1 us
    ppermute x15, starting transfers between devices, along(): lax.ppermute(value, 'dp', [(i, (i + 2 * k) % devices) for i in range(devi...  16.9 us
    all_to_all x4, waiting for transfers between devices, exchange(): lax.all_to_all(value, 'expert', split_axis=0, concat_axis=0, tiled=True)  16.7 us
    ppermute x10, starting transfers between devices, swap(): return lax.ppermute(value, 'dp', [(i, i ^ 1) for i in range(devices)])  14 us
    ppermute x10, waiting for transfers between devices, swap(): return lax.ppermute(value, 'dp', [(i, i ^ 1) for i in range(devices)])  3.39 us
  transfers between devices with their start and end apart: 29, of which 15 were waited for; matrix products, arithmetic and copies ran while one was open for 2% of the time, Pallas kernels for 23%

profile of v3, /device:TPU:1, one launch (start us, length us, event | category | flops | bytes accessed | tf_op | source)
XLA Modules:
  0.0 154.1 jit_solution(17089524403208421147)
XLA Ops:
  0.6 3.3 %collective-permute-start.4 = (bf16[256,512]{1,0:T(8,128)(2,1)}, bf16[256,512]{1,0:T(8,128)(2,1)S(1)}, u32[]{:S(2)}, u32[]{:S(2)}) collective-permute-start(bf16[256,512]{1,0:T(8,128)(2,1)} %tokens_hbm.1), channel_id=1, source_target_pairs={{0,32},{32,0},{64,96},{96,64},{128,160},{160,128},{192,224},{224,1... | collective-permute-start | bytes 786440 | tf_op jit(solution)/shard_map/ppermute | solution.py:400
  4.0 1.8 %shard_map.119 = (bf16[512,512]{1,0:T(8,128)(2,1)S(1)}, bf16[512,256]{1,0:T(8,128)(2,1)S(1)}) custom-call(s32[2]{0:T(128)S(1)} %pad_add_fusion.ids, s32[16,64]{1,0:T(8,128)} %bitcast.38, bf16[256,512]{1,0:T(8,128)(2,1)} %tokens_hbm.1), custom_call_target="tpu_custom_call" | custom-call | flops 134217728 | bytes 1052672 | tf_op jit(solution)/shard_map/pallas_call | solution.py:44
  5.9 1.6 %shard_map.120 = bf16[512,1024]{1,0:T(8,128)(2,1)} custom-call(s32[2]{0:T(128)S(1)} %pad_add_fusion.ids, bf16[512,512]{1,0:T(8,128)(2,1)S(1)} %get-tuple-element.69.half_ref, bf16[512,256]{1,0:T(8,128)(2,1)S(1)} %get-tuple-element.70.picker_ref, bf16[256,512]{1,0:T(8,128)(2,1)S(1)} %collective-permute-done.4.tokens_ref), custom_call_target="tpu_custom_call" | custom-call | flops 134217728 | bytes 2097152 | tf_op jit(solution)/shard_map/pallas_call | solution.py:44
  7.5 9.7 %all-to-all-start.1 = ((bf16[32,16,1024]{2,1,0:T(8,128)(2,1)}), bf16[32,16,1024]{2,1,0:T(8,128)(2,1)}, u32[]{:S(2)}, u32[]{:S(2)}) async-start(bf16[32,16,1024]{2,1,0:T(8,128)(2,1)} %bitcast.45), calls=%async_computation.1 | async-start | bytes 2097152 | tf_op jit(solution)/shard_map/all_to_all | solution.py:413
  17.8 0.9 copy-done.11
  20.2 2.5 %collective-permute-done.other_ref.other_hbm = bf16[256,512]{1,0:T(8,128)(2,1)S(1)} collective-permute-done((bf16[256,512]{1,0:T(8,128)(2,1)S(1)}, bf16[256,512]{1,0:T(8,128)(2,1)S(1)}, u32[]{:S(2)}, u32[]{:S(2)}) %collective-permute-start) | collective-permute-done | bytes 262176 | tf_op jit(solution)/shard_map/ppermute | solution.py:400
  22.7 2.0 %shard_map.118 = bf16[512,1024]{1,0:T(8,128)(2,1)} custom-call(s32[2]{0:T(128)S(1)} %pad_add_fusion.ids, s32[16,64]{1,0:T(8,128)S(1)} %bitcast.39, bf16[16,64]{1,0:T(8,128)(2,1)S(1)} %bitcast.43, bf16[256,512]{1,0:T(8,128)(2,1)S(1)} %copy-done.5, bf16[256,512]{1,0:T(8,128)(2,1)S(1)} %collective-permute-done.other_ref.other_hbm), custom_call_target="tpu_custom_call" | custom-call | flops 268435456 | bytes 1579008 | tf_op jit(solution)/shard_map/pallas_call | solution.py:44
  24.8 0.9 copy-done.1
  25.9 16.7 %all-to-all-done.1 = bf16[32,16,1024]{2,1,0:T(8,128)(2,1)} async-done(((bf16[32,16,1024]{2,1,0:T(8,128)(2,1)}), bf16[32,16,1024]{2,1,0:T(8,128)(2,1)}, u32[]{:S(2)}, u32[]{:S(2)}) %all-to-all-start.1) | async-done | bytes 1048608 | tf_op jit(solution)/shard_map/all_to_all | solution.py:413
  42.6 8.1 %all-to-all-start = ((bf16[32,16,1024]{2,1,0:T(8,128)(2,1)}), bf16[32,16,1024]{2,1,0:T(8,128)(2,1)}, u32[]{:S(2)}, u32[]{:S(2)}) async-start(bf16[32,16,1024]{2,1,0:T(8,128)(2,1)} %bitcast.46), calls=%async_computation | async-start | bytes 2097152 | tf_op jit(solution)/shard_map/all_to_all | solution.py:413
  50.8 3.8 %shard_map.121 = (bf16[256,1024]{1,0:T(8,128)(2,1)}, bf16[256,512]{1,0:T(8,128)(2,1)}, bf16[512,256]{1,0:T(8,128)(2,1)S(1)}, f32[64,1536]{1,0:T(8,128)S(1)}, bf1...) custom-call(s32[2]{0:T(128)S(1)} %pad_add_fusion.ids, ...), custom_call_target="tpu_custom_call" | custom-call | flops 1073741824 | bytes 6225920 | tf_op jit(solution)/shard_map/pallas_call | solution.py:44
  54.6 1.3 collective-permute-start.8
  55.8 2.5 %collective-permute-start.9 = (bf16[64,1536]{1,0:T(8,128)(2,1)S(1)}, bf16[64,1536]{1,0:T(8,128)(2,1)S(1)}, u32[]{:S(2)}, u32[]{:S(2)}) collective-permute-start(bf16[64,1536]{1,0:T(8,128)(2,1)S(1)} %get-tuple-element.83), channel_id=1, source_target_pairs={{0,128},{32,160},{64,192},{96,224},{128,0},{160,32},{192,64},{224,... | collective-permute-start | bytes 589832 | tf_op jit(solution)/shard_map/ppermute | solution.py:403
  58.3 1.2 collective-permute-start.10
  59.4 1.6 %collective-permute-done.8.r1 = bf16[64,1536]{1,0:T(8,128)(2,1)S(1)} collective-permute-done((bf16[64,1536]{1,0:T(8,128)(2,1)S(1)}, bf16[64,1536]{1,0:T(8,128)(2,1)S(1)}, u32[]{:S(2)}, u32[]{:S(2)}) %collective-permute-start.8) | collective-permute-done | bytes 196640 | tf_op jit(solution)/shard_map/ppermute | solution.py:403
  61.1 5.2 %collective-permute-done.9.r2 = bf16[64,1536]{1,0:T(8,128)(2,1)S(1)} collective-permute-done((bf16[64,1536]{1,0:T(8,128)(2,1)S(1)}, bf16[64,1536]{1,0:T(8,128)(2,1)S(1)}, u32[]{:S(2)}, u32[]{:S(2)}) %collective-permute-start.9) | collective-permute-done | bytes 196640 | tf_op jit(solution)/shard_map/ppermute | solution.py:403
  67.0 2.8 %collective-permute-start.13 = (bf16[64,768]{1,0:T(8,128)(2,1)S(1)}, bf16[64,768]{1,0:T(8,128)(2,1)S(1)}, u32[]{:S(2)}, u32[]{:S(2)}) collective-permute-start(bf16[64,768]{1,0:T(8,128)(2,1)S(1)} %get-tuple-element.85.h0), channel_id=1, source_target_pairs={{0,192},{32,224},{64,0},{96,32},{128,64},{160,96},{192,128},{224,1... | collective-permute-start | bytes 294920 | tf_op jit(solution)/shard_map/ppermute | solution.py:403
  69.7 1.1 collective-permute-start.12
  70.8 1.6 %collective-permute-done.13.h3 = bf16[64,768]{1,0:T(8,128)(2,1)S(1)} collective-permute-done((bf16[64,768]{1,0:T(8,128)(2,1)S(1)}, bf16[64,768]{1,0:T(8,128)(2,1)S(1)}, u32[]{:S(2)}, u32[]{:S(2)}) %collective-permute-start.13) | collective-permute-done | bytes 98336 | tf_op jit(solution)/shard_map/ppermute | solution.py:403
  72.4 2.8 %collective-permute-done.12.h2 = bf16[64,768]{1,0:T(8,128)(2,1)S(1)} collective-permute-done((bf16[64,768]{1,0:T(8,128)(2,1)S(1)}, bf16[64,768]{1,0:T(8,128)(2,1)S(1)}, u32[]{:S(2)}, u32[]{:S(2)}) %collective-permute-start.12) | collective-permute-done | bytes 98336 | tf_op jit(solution)/shard_map/ppermute | solution.py:403
  75.1 1.1 collective-permute-done.11.h1
  76.2 3.3 %shard_map.124 = (bf16[256,768]{1,0:T(8,128)(2,1)}, bf16[512,1024]{1,0:T(8,128)(2,1)}, bf16[512,256]{1,0:T(8,128)(2,1)}, f32[64,1536]{1,0:T(8,128)}) custom-call(s32[2]{0:T(128)S(1)} %pad_add_fusion.ids, bf16[64,768]{1,0:T(8,128)(2,1)S(1)} %get-tuple-element.85.h0, bf16[64,768]{1,0:T(8,128)(2,1)S(1)} %collective-permute-done.11.h1, ...), custom_call_target="tpu_custom_call" | custom-call | flops 671088640 | bytes 4718592 | tf_op jit(solution)/shard_map/pallas_call | solution.py:44
  79.5 8.5 %all-to-all-start.3 = ((bf16[32,16,1024]{2,1,0:T(8,128)(2,1)}), bf16[32,16,1024]{2,1,0:T(8,128)(2,1)S(1)}, u32[]{:S(2)}, u32[]{:S(2)}) async-start(bf16[32,16,1024]{2,1,0:T(8,128)(2,1)} %bitcast.49), calls=%async_computation.3 | async-start | bytes 2097152 | tf_op jit(solution)/shard_map/all_to_all | solution.py:413
  88.0 3.3 %shard_map.122 = (bf16[256,1024]{1,0:T(8,128)(2,1)}, f32[64,768]{1,0:T(8,128)S(1)}, bf16[64,768]{1,0:T(8,128)(2,1)S(1)}, bf16[64,768]{1,0:T(8,128)(2,1)S(1)}, bf16[64,768]{1,0:T(8,128)(2,1)S(1)}) custom-call(s32[2]{0:T(128)S(1)} %pad_add_fusion.ids, bf16[512,1024]{1,0:T(8,128)(2,1)} %bitcast.13.got_hbm, bf16[256,512]{1,0:T(8,128)(2,1)} %get-tuple-element.74.narrow_hbm, ...), custom_call_target="tpu_custom_call" | custom-call | flops 671088640 | bytes 3899392 | tf_op jit(solution)/shard_map/pallas_call | solution.py:44
  91.8 1.6 %collective-permute-start.6 = (bf16[64,768]{1,0:T(8,128)(2,1)S(1)}, bf16[64,768]{1,0:T(8,128)(2,1)S(1)}, u32[]{:S(2)}, u32[]{:S(2)}) collective-permute-start(bf16[64,768]{1,0:T(8,128)(2,1)S(1)} %get-tuple-element.79), channel_id=1, source_target_pairs={{0,128},{32,160},{64,192},{96,224},{128,0},{160,32},{192,64},{224,... | collective-permute-start | bytes 294920 | tf_op jit(solution)/shard_map/ppermute | solution.py:403
  93.4 2.0 %collective-permute-start.7 = (bf16[64,768]{1,0:T(8,128)(2,1)S(1)}, bf16[64,768]{1,0:T(8,128)(2,1)S(1)}, u32[]{:S(2)}, u32[]{:S(2)}) collective-permute-start(bf16[64,768]{1,0:T(8,128)(2,1)S(1)} %get-tuple-element.80), channel_id=1, source_target_pairs={{0,192},{32,224},{64,0},{96,32},{128,64},{160,96},{192,128},{224,1... | collective-permute-start | bytes 294920 | tf_op jit(solution)/shard_map/ppermute | solution.py:403
  95.4 2.0 %collective-permute-done.5.r1 = bf16[64,768]{1,0:T(8,128)(2,1)S(1)} collective-permute-done((bf16[64,768]{1,0:T(8,128)(2,1)S(1)}, bf16[64,768]{1,0:T(8,128)(2,1)S(1)}, u32[]{:S(2)}, u32[]{:S(2)}) %collective-permute-start.5) | collective-permute-done | bytes 98336 | tf_op jit(solution)/shard_map/ppermute | solution.py:403
  98.4 2.8 %collective-permute-start.16 = (bf16[64,1536]{1,0:T(8,128)(2,1)S(1)}, bf16[64,1536]{1,0:T(8,128)(2,1)S(1)}, u32[]{:S(2)}, u32[]{:S(2)}) collective-permute-start(bf16[64,1536]{1,0:T(8,128)(2,1)S(1)} %shard_map.125.g0), channel_id=1, source_target_pairs={{0,192},{32,224},{64,0},{96,32},{128,64},{160,96},{192,128},{224,1... | collective-permute-start | bytes 589832 | tf_op jit(solution)/shard_map/ppermute | solution.py:403
  101.1 0.7 collective-permute-start.15
  101.8 1.7 %shard_map.126.wo_u_ref = bf16[512,768]{1,0:T(8,128)(2,1)S(1)} custom-call(s32[2]{0:T(128)S(1)} %pad_add_fusion.ids, bf16[512,768]{1,0:T(8,128)(2,1)} %copy-done.9), custom_call_target="tpu_custom_call" | custom-call | bytes 1572864 | tf_op jit(solution)/shard_map/pallas_call | solution.py:44
  103.5 2.3 %collective-permute-done.16.g3 = bf16[64,1536]{1,0:T(8,128)(2,1)S(1)} collective-permute-done((bf16[64,1536]{1,0:T(8,128)(2,1)S(1)}, bf16[64,1536]{1,0:T(8,128)(2,1)S(1)}, u32[]{:S(2)}, u32[]{:S(2)}) %collective-permute-start.16) | collective-permute-done | bytes 196640 | tf_op jit(solution)/shard_map/ppermute | solution.py:403
  105.9 1.6 %collective-permute-done.15.g2 = bf16[64,1536]{1,0:T(8,128)(2,1)S(1)} collective-permute-done((bf16[64,1536]{1,0:T(8,128)(2,1)S(1)}, bf16[64,1536]{1,0:T(8,128)(2,1)S(1)}, u32[]{:S(2)}, u32[]{:S(2)}) %collective-permute-start.15) | collective-permute-done | bytes 196640 | tf_op jit(solution)/shard_map/ppermute | solution.py:403
  107.5 2.1 %collective-permute-done.14.g1 = bf16[64,1536]{1,0:T(8,128)(2,1)S(1)} collective-permute-done((bf16[64,1536]{1,0:T(8,128)(2,1)S(1)}, bf16[64,1536]{1,0:T(8,128)(2,1)S(1)}, u32[]{:S(2)}, u32[]{:S(2)}) %collective-permute-start.14) | collective-permute-done | bytes 196640 | tf_op jit(solution)/shard_map/ppermute | solution.py:403
  109.6 3.1 %shard_map.127 = (bf16[256,1536]{1,0:T(8,128)(2,1)}, bf16[512,1024]{1,0:T(8,128)(2,1)}) custom-call(s32[2]{0:T(128)S(1)} %pad_add_fusion.ids, bf16[64,1536]{1,0:T(8,128)(2,1)S(1)} %shard_map.125.g0, bf16[64,1536]{1,0:T(8,128)(2,1)S(1)} %collective-permute-done.14.g1, bf16[64,1536]{1,0:T(8,128)(2,1)S(1)} %collective-permute-done.15.g2, ...), custom_call_target="tpu_custom_call" | custom-call | flops 1073741824 | bytes 6029312 | tf_op jit(solution)/shard_map/pallas_call | solution.py:44
  112.7 9.2 %all-to-all-start.2 = ((bf16[32,16,1024]{2,1,0:T(8,128)(2,1)}), bf16[32,16,1024]{2,1,0:T(8,128)(2,1)S(1)}, u32[]{:S(2)}, u32[]{:S(2)}) async-start(bf16[32,16,1024]{2,1,0:T(8,128)(2,1)} %bitcast.47), calls=%async_computation.2 | async-start | bytes 2097152 | tf_op jit(solution)/shard_map/all_to_all | solution.py:413
  121.9 3.8 %shard_map.128 = (f32[256,512]{1,0:T(8,128)}, f32[256,512]{1,0:T(8,128)}, f32[32,16]{1,0:T(8,128)S(1)}) custom-call(s32[2]{0:T(128)S(1)} %pad_add_fusion.ids, bf16[512,1024]{1,0:T(8,128)(2,1)} %bitcast.48, bf16[256,512]{1,0:T(8,128)(2,1)} %own_hbm.1, bf16[256,512]{1,0:T(8,128)(2,1)} %copy-done.6, s32[16,64]{1,0:T(8,128)S(1)} %bitcast.40, ...), custom_call_target="tpu_custom_call" | custom-call | flops 536870912 | bytes 2629632 | tf_op jit(solution)/shard_map/pallas_call | solution.py:44
  125.8 3.9 %shard_map.130 = (bf16[512,1536]{1,0:T(8,128)(2,1)}, bf16[768,512]{1,0:T(8,128)(2,1)}) custom-call(s32[2]{0:T(128)S(1)} %pad_add_fusion.ids, bf16[256,1024]{1,0:T(8,128)(2,1)} %get-tuple-element.103.rows_in_hbm, bf16[256,1536]{1,0:T(8,128)(2,1)} %get-tuple-element.104.grads_hbm, bf16[256,768]{1,0:T(8,128)(2,1)} %get-tuple-element.105.hidden_hbm, ...), custom_call_target="tpu_custom_call" | custom-call | flops 603979776 | bytes 4587520 | tf_op jit(solution)/shard_map/pallas_call | solution.py:44
  129.7 6.2 %collective-permute-start.22 = (bf16[512,1536]{1,0:T(8,128)(2,1)}, bf16[512,1536]{1,0:T(8,128)(2,1)S(1)}, u32[]{:S(2)}, u32[]{:S(2)}) collective-permute-start(bf16[512,1536]{1,0:T(8,128)(2,1)} %get-tuple-element.114), channel_id=1, source_target_pairs={{0,32},{32,0},{64,96},{96,64},{128,160},{160,128},{192,224},{224,1... | collective-permute-start | bytes 4718600 | tf_op jit(solution)/shard_map/ppermute | solution.py:400
  137.1 2.2 %collective-permute-done.20 = f32[32,16]{1,0:T(8,128)S(1)} collective-permute-done((f32[32,16]{1,0:T(8,128)S(1)}, f32[32,16]{1,0:T(8,128)S(1)}, u32[]{:S(2)}, u32[]{:S(2)}) %collective-permute-start.20) | collective-permute-done | bytes 2080 | tf_op jit(solution)/shard_map/ppermute | solution.py:403
  139.3 3.8 %shard_map.129 = (bf16[2,512,768]{2,1,0:T(8,128)(2,1)}, bf16[2,512,768]{2,1,0:T(8,128)(2,1)}, bf16[2,768,512]{2,1,0:T(8,128)(2,1)}) custom-call(s32[2]{0:T(128)S(1)} %pad_add_fusion.ids, bf16[256,1024]{1,0:T(8,128)(2,1)} %get-tuple-element.103.rows_in_hbm, bf16[256,1536]{1,0:T(8,128)(2,1)} %get-tuple-element.104.grads_hbm, ...), custom_call_target="tpu_custom_call" | custom-call | flops 603979776 | bytes 6946816 | tf_op jit(solution)/shard_map/pallas_call | solution.py:44
  143.4 1.9 %collective-permute-start.21 = (bf16[32,16]{1,0:T(8,128)(2,1)S(1)}, bf16[32,16]{1,0:T(8,128)(2,1)S(1)}, u32[]{:S(2)}, u32[]{:S(2)}) collective-permute-start(bf16[32,16]{1,0:T(8,128)(2,1)S(1)} %add_convert_fusion.2), channel_id=1, source_target_pairs={{0,32},{32,0},{64,96},{96,64},{128,160},{160,128},{192,224},{224,1... | collective-permute-start | bytes 3080 | tf_op jit(solution)/shard_map/ppermute | solution.py:400
  145.3 0.8 collective-permute-done.21
  146.2 2.0 %add_convert_fusion.1 = bf16[256,512]{1,0:T(8,128)(2,1)} fusion(f32[256,512]{1,0:T(8,128)} %get-tuple-element.94, f32[256,512]{1,0:T(8,128)} %collective-permute-done.17), kind=kLoop, calls=%fused_computation.7 | loop fusion | flops 262144 | bytes 1310720 | tf_op jit(solution)/shard_map/convert_element_type | solution.py:573
  148.2 2.0 %shard_map.131 = (bf16[2,512,768]{2,1,0:T(8,128)(2,1)}, bf16[2,512,768]{2,1,0:T(8,128)(2,1)}, bf16[2,768,512]{2,1,0:T(8,128)(2,1)}) custom-call(s32[2]{0:T(128)S(1)} %pad_add_fusion.ids, bf16[512,1536]{1,0:T(8,128)(2,1)S(1)} %collective-permute-done.22.got_in_ref, ...), custom_call_target="tpu_custom_call", output_to_operand_aliasing={{0}: (3, {}), {1}: (4, {}), {2}: (5, {})} | custom-call | bytes 11796480 | tf_op jit(solution)/shard_map/pallas_call | solution.py:44
  150.1 0.9 shard_map.133
  151.7 0.7 copy.17
  152.4 0.9 shard_map.132
  153.3 0.8 add_convert_fusion
  (64 shorter events, 6.6 us)
Async XLA Ops:
  0.6 5.2 %collective-permute-start.4 = (bf16[256,512]{1,0:T(8,128)(2,1)}, bf16[256,512]{1,0:T(8,128)(2,1)S(1)}, u32[]{:S(2)}, u32[]{:S(2)}) collective-permute-start(bf16[256,512]{1,0:T(8,128)(2,1)} %tokens_hbm.1), channel_id=1, source_target_pairs={{0,32},{32,0},{64,96},{96,64},{128,160},{160,128},{192,224},{224,1... | collective-permute-start | bytes 786440 | tf_op jit(solution)/shard_map/ppermute | solution.py:400
  7.5 9.8 %copy-start.10 = (bf16[2,512,768]{2,1,0:T(8,128)(2,1)S(1)}, bf16[2,512,768]{2,1,0:T(8,128)(2,1)}, u32[]{:S(2)}) copy-start(bf16[2,512,768]{2,1,0:T(8,128)(2,1)} %param.11) | copy-start | bytes 4718596
  7.5 35.1 %all-to-all-start.1 = ((bf16[32,16,1024]{2,1,0:T(8,128)(2,1)}), bf16[32,16,1024]{2,1,0:T(8,128)(2,1)}, u32[]{:S(2)}, u32[]{:S(2)}) async-start(bf16[32,16,1024]{2,1,0:T(8,128)(2,1)} %bitcast.45), calls=%async_computation.1 | async-start | bytes 2097152 | tf_op jit(solution)/shard_map/all_to_all | solution.py:413
  17.3 1.4 copy-start.11
  17.4 1.8 %copy-start.12 = (bf16[2,768,512]{2,1,0:T(8,128)(2,1)S(1)}, bf16[2,768,512]{2,1,0:T(8,128)(2,1)}, u32[]{:S(2)}) copy-start(bf16[2,768,512]{2,1,0:T(8,128)(2,1)} %param.13) | copy-start | bytes 4718596
  17.4 7.3 %collective-permute-start.1 = (bf16[512,768]{1,0:T(8,128)(2,1)S(1)}, bf16[512,768]{1,0:T(8,128)(2,1)S(1)}, u32[]{:S(2)}, u32[]{:S(2)}) collective-permute-start(bf16[512,768]{1,0:T(8,128)(2,1)S(1)} %get-tuple-element.138), channel_id=1, source_target_pairs={{0,32},{32,0},{64,96},{96,64},{128,160},{160,128},{192,224},{224,1... | collective-permute-start | bytes 2359304 | tf_op jit(solution)/shard_map/ppermute | solution.py:400
  18.8 1.1 copy-start.5
  18.8 3.9 %copy-start.7 = (s32[1,64,16]{1,2,0:T(8,128)S(1)}, s32[1,64,16]{1,2,0:T(8,128)}, u32[]{:S(2)}) copy-start(s32[1,64,16]{1,2,0:T(8,128)} %param.9) | copy-start | bytes 12292
  18.8 3.9 %copy-start.8 = (bf16[1,64,16]{1,2,0:T(8,128)(2,1)S(1)}, bf16[1,64,16]{1,2,0:T(8,128)(2,1)}, u32[]{:S(2)}) copy-start(bf16[1,64,16]{1,2,0:T(8,128)(2,1)} %param.10) | copy-start | bytes 6148
  18.8 5.9 %collective-permute-start.2 = (bf16[512,768]{1,0:T(8,128)(2,1)S(1)}, bf16[512,768]{1,0:T(8,128)(2,1)S(1)}, u32[]{:S(2)}, u32[]{:S(2)}) collective-permute-start(bf16[512,768]{1,0:T(8,128)(2,1)S(1)} %get-tuple-element.136), channel_id=1, source_target_pairs={{0,32},{32,0},{64,96},{96,64},{128,160},{160,128},{192,224},{224,1... | collective-permute-start | bytes 2359304 | tf_op jit(solution)/shard_map/ppermute | solution.py:400
  19.3 56.8 %copy-start = (bf16[768,512]{1,0:T(8,128)(2,1)}, bf16[768,512]{1,0:T(8,128)(2,1)S(1)}, u32[]{:S(2)}) copy-start(bf16[768,512]{1,0:T(8,128)(2,1)S(1)} %get-tuple-element.75.wd_hbm.wd_ref) | copy-start | bytes 2359300
  19.3 5.4 %collective-permute-start.3 = (bf16[768,512]{1,0:T(8,128)(2,1)S(1)}, bf16[768,512]{1,0:T(8,128)(2,1)S(1)}, u32[]{:S(2)}, u32[]{:S(2)}) collective-permute-start(bf16[768,512]{1,0:T(8,128)(2,1)S(1)} %get-tuple-element.134), channel_id=1, source_target_pairs={{0,32},{32,0},{64,96},{96,64},{128,160},{160,128},{192,224},{224,1... | collective-permute-start | bytes 2359304 | tf_op jit(solution)/shard_map/ppermute | solution.py:400
  19.8 2.9 %collective-permute-start = (bf16[256,512]{1,0:T(8,128)(2,1)S(1)}, bf16[256,512]{1,0:T(8,128)(2,1)S(1)}, u32[]{:S(2)}, u32[]{:S(2)}) collective-permute-start(bf16[256,512]{1,0:T(8,128)(2,1)S(1)} %copy-done.5), channel_id=1, source_target_pairs={{0,32},{32,0},{64,96},{96,64},{128,160},{160,128},{192,224},{224,1... | collective-permute-start | bytes 786440 | tf_op jit(solution)/shard_map/ppermute | solution.py:400
  22.7 2.1 %copy-start.6 = (bf16[256,512]{1,0:T(8,128)(2,1)}, bf16[256,512]{1,0:T(8,128)(2,1)S(1)}, u32[]{:S(2)}) copy-start(bf16[256,512]{1,0:T(8,128)(2,1)S(1)} %collective-permute-done.other_ref.other_hbm) | copy-start | bytes 786436
  24.8 1.1 copy-start.9
  24.8 0.9 copy-start.1
  42.6 36.8 %all-to-all-start = ((bf16[32,16,1024]{2,1,0:T(8,128)(2,1)}), bf16[32,16,1024]{2,1,0:T(8,128)(2,1)}, u32[]{:S(2)}, u32[]{:S(2)}) async-start(bf16[32,16,1024]{2,1,0:T(8,128)(2,1)} %bitcast.46), calls=%async_computation | async-start | bytes 2097152 | tf_op jit(solution)/shard_map/all_to_all | solution.py:413
  50.8 25.4 %copy-start.2 = (bf16[768,512]{1,0:T(8,128)(2,1)S(1)}, bf16[768,512]{1,0:T(8,128)(2,1)}, u32[]{:S(2)}) copy-start(bf16[768,512]{1,0:T(8,128)(2,1)} %copy-done.1) | copy-start | bytes 2359300
  54.6 6.5 %collective-permute-start.8 = (bf16[64,1536]{1,0:T(8,128)(2,1)S(1)}, bf16[64,1536]{1,0:T(8,128)(2,1)S(1)}, u32[]{:S(2)}, u32[]{:S(2)}) collective-permute-start(bf16[64,1536]{1,0:T(8,128)(2,1)S(1)} %get-tuple-element.82), channel_id=1, source_target_pairs={{0,64},{32,96},{64,128},{96,160},{128,192},{160,224},{192,0},{224,... | collective-permute-start | bytes 589832 | tf_op jit(solution)/shard_map/ppermute | solution.py:403
  55.8 10.5 %collective-permute-start.9 = (bf16[64,1536]{1,0:T(8,128)(2,1)S(1)}, bf16[64,1536]{1,0:T(8,128)(2,1)S(1)}, u32[]{:S(2)}, u32[]{:S(2)}) collective-permute-start(bf16[64,1536]{1,0:T(8,128)(2,1)S(1)} %get-tuple-element.83), channel_id=1, source_target_pairs={{0,128},{32,160},{64,192},{96,224},{128,0},{160,32},{192,64},{224,... | collective-permute-start | bytes 589832 | tf_op jit(solution)/shard_map/ppermute | solution.py:403
  58.3 8.0 %collective-permute-start.10 = (bf16[64,1536]{1,0:T(8,128)(2,1)S(1)}, bf16[64,1536]{1,0:T(8,128)(2,1)S(1)}, u32[]{:S(2)}, u32[]{:S(2)}) collective-permute-start(bf16[64,1536]{1,0:T(8,128)(2,1)S(1)} %get-tuple-element.84), channel_id=1, source_target_pairs={{0,192},{32,224},{64,0},{96,32},{128,64},{160,96},{192,128},{224,1... | collective-permute-start | bytes 589832 | tf_op jit(solution)/shard_map/ppermute | solution.py:403
  67.0 5.4 %collective-permute-start.13 = (bf16[64,768]{1,0:T(8,128)(2,1)S(1)}, bf16[64,768]{1,0:T(8,128)(2,1)S(1)}, u32[]{:S(2)}, u32[]{:S(2)}) collective-permute-start(bf16[64,768]{1,0:T(8,128)(2,1)S(1)} %get-tuple-element.85.h0), channel_id=1, source_target_pairs={{0,192},{32,224},{64,0},{96,32},{128,64},{160,96},{192,128},{224,1... | collective-permute-start | bytes 294920 | tf_op jit(solution)/shard_map/ppermute | solution.py:403
  69.7 5.4 %collective-permute-start.12 = (bf16[64,768]{1,0:T(8,128)(2,1)S(1)}, bf16[64,768]{1,0:T(8,128)(2,1)S(1)}, u32[]{:S(2)}, u32[]{:S(2)}) collective-permute-start(bf16[64,768]{1,0:T(8,128)(2,1)S(1)} %get-tuple-element.85.h0), channel_id=1, source_target_pairs={{0,128},{32,160},{64,192},{96,224},{128,0},{160,32},{192,64},{224,... | collective-permute-start | bytes 294920 | tf_op jit(solution)/shard_map/ppermute | solution.py:403
  70.8 5.4 %collective-permute-start.11 = (bf16[64,768]{1,0:T(8,128)(2,1)S(1)}, bf16[64,768]{1,0:T(8,128)(2,1)S(1)}, u32[]{:S(2)}, u32[]{:S(2)}) collective-permute-start(bf16[64,768]{1,0:T(8,128)(2,1)S(1)} %get-tuple-element.85.h0), channel_id=1, source_target_pairs={{0,64},{32,96},{64,128},{96,160},{128,192},{160,224},{192,0},{224,... | collective-permute-start | bytes 294920 | tf_op jit(solution)/shard_map/ppermute | solution.py:403
  79.5 33.2 %all-to-all-start.3 = ((bf16[32,16,1024]{2,1,0:T(8,128)(2,1)}), bf16[32,16,1024]{2,1,0:T(8,128)(2,1)S(1)}, u32[]{:S(2)}, u32[]{:S(2)}) async-start(bf16[32,16,1024]{2,1,0:T(8,128)(2,1)} %bitcast.49), calls=%async_computation.3 | async-start | bytes 2097152 | tf_op jit(solution)/shard_map/all_to_all | solution.py:413
  88.0 9.7 %copy-start.3 = (f32[64,1536]{1,0:T(8,128)S(1)}, f32[64,1536]{1,0:T(8,128)}, u32[]{:S(2)}) copy-start(f32[64,1536]{1,0:T(8,128)} %get-tuple-element.88.pre_ref) | copy-start | bytes 1179652
  91.3 18.3 %copy-start.4 = (bf16[512,256]{1,0:T(8,128)(2,1)S(1)}, bf16[512,256]{1,0:T(8,128)(2,1)}, u32[]{:S(2)}) copy-start(bf16[512,256]{1,0:T(8,128)(2,1)} %get-tuple-element.91.widen_ref) | copy-start | bytes 786436
  91.3 6.0 %collective-permute-start.5 = (bf16[64,768]{1,0:T(8,128)(2,1)S(1)}, bf16[64,768]{1,0:T(8,128)(2,1)S(1)}, u32[]{:S(2)}, u32[]{:S(2)}) collective-permute-start(bf16[64,768]{1,0:T(8,128)(2,1)S(1)} %get-tuple-element.78), channel_id=1, source_target_pairs={{0,64},{32,96},{64,128},{96,160},{128,192},{160,224},{192,0},{224,... | collective-permute-start | bytes 294920 | tf_op jit(solution)/shard_map/ppermute | solution.py:403
  91.8 5.5 %collective-permute-start.6 = (bf16[64,768]{1,0:T(8,128)(2,1)S(1)}, bf16[64,768]{1,0:T(8,128)(2,1)S(1)}, u32[]{:S(2)}, u32[]{:S(2)}) collective-permute-start(bf16[64,768]{1,0:T(8,128)(2,1)S(1)} %get-tuple-element.79), channel_id=1, source_target_pairs={{0,128},{32,160},{64,192},{96,224},{128,0},{160,32},{192,64},{224,... | collective-permute-start | bytes 294920 | tf_op jit(solution)/shard_map/ppermute | solution.py:403
  93.4 4.3 %collective-permute-start.7 = (bf16[64,768]{1,0:T(8,128)(2,1)S(1)}, bf16[64,768]{1,0:T(8,128)(2,1)S(1)}, u32[]{:S(2)}, u32[]{:S(2)}) collective-permute-start(bf16[64,768]{1,0:T(8,128)(2,1)S(1)} %get-tuple-element.80), channel_id=1, source_target_pairs={{0,192},{32,224},{64,0},{96,32},{128,64},{160,96},{192,128},{224,1... | collective-permute-start | bytes 294920 | tf_op jit(solution)/shard_map/ppermute | solution.py:403
  98.4 7.5 %collective-permute-start.16 = (bf16[64,1536]{1,0:T(8,128)(2,1)S(1)}, bf16[64,1536]{1,0:T(8,128)(2,1)S(1)}, u32[]{:S(2)}, u32[]{:S(2)}) collective-permute-start(bf16[64,1536]{1,0:T(8,128)(2,1)S(1)} %shard_map.125.g0), channel_id=1, source_target_pairs={{0,192},{32,224},{64,0},{96,32},{128,64},{160,96},{192,128},{224,1... | collective-permute-start | bytes 589832 | tf_op jit(solution)/shard_map/ppermute | solution.py:403
  101.1 6.3 %collective-permute-start.15 = (bf16[64,1536]{1,0:T(8,128)(2,1)S(1)}, bf16[64,1536]{1,0:T(8,128)(2,1)S(1)}, u32[]{:S(2)}, u32[]{:S(2)}) collective-permute-start(bf16[64,1536]{1,0:T(8,128)(2,1)S(1)} %shard_map.125.g0), channel_id=1, source_target_pairs={{0,128},{32,160},{64,192},{96,224},{128,0},{160,32},{192,64},{224,... | collective-permute-start | bytes 589832 | tf_op jit(solution)/shard_map/ppermute | solution.py:403
  101.8 7.7 %collective-permute-start.14 = (bf16[64,1536]{1,0:T(8,128)(2,1)S(1)}, bf16[64,1536]{1,0:T(8,128)(2,1)S(1)}, u32[]{:S(2)}, u32[]{:S(2)}) collective-permute-start(bf16[64,1536]{1,0:T(8,128)(2,1)S(1)} %shard_map.125.g0), channel_id=1, source_target_pairs={{0,64},{32,96},{64,128},{96,160},{128,192},{160,224},{192,0},{224,... | collective-permute-start | bytes 589832 | tf_op jit(solution)/shard_map/ppermute | solution.py:403
  112.7 9.3 %copy-start.13 = (bf16[32,16,1024]{2,1,0:T(8,128)(2,1)}, bf16[32,16,1024]{2,1,0:T(8,128)(2,1)S(1)}, u32[]{:S(2)}) copy-start(bf16[32,16,1024]{2,1,0:T(8,128)(2,1)S(1)} %all-to-all-done.3) | copy-start | bytes 3145732
  112.7 37.5 %all-to-all-start.2 = ((bf16[32,16,1024]{2,1,0:T(8,128)(2,1)}), bf16[32,16,1024]{2,1,0:T(8,128)(2,1)S(1)}, u32[]{:S(2)}, u32[]{:S(2)}) async-start(bf16[32,16,1024]{2,1,0:T(8,128)(2,1)} %bitcast.47), calls=%async_computation.2 | async-start | bytes 2097152 | tf_op jit(solution)/shard_map/all_to_all | solution.py:413
  129.7 18.5 %collective-permute-start.22 = (bf16[512,1536]{1,0:T(8,128)(2,1)}, bf16[512,1536]{1,0:T(8,128)(2,1)S(1)}, u32[]{:S(2)}, u32[]{:S(2)}) collective-permute-start(bf16[512,1536]{1,0:T(8,128)(2,1)} %get-tuple-element.114), channel_id=1, source_target_pairs={{0,32},{32,0},{64,96},{96,64},{128,160},{160,128},{192,224},{224,1... | collective-permute-start | bytes 4718600 | tf_op jit(solution)/shard_map/ppermute | solution.py:400
  135.9 12.2 %collective-permute-start.23 = (bf16[768,512]{1,0:T(8,128)(2,1)}, bf16[768,512]{1,0:T(8,128)(2,1)S(1)}, u32[]{:S(2)}, u32[]{:S(2)}) collective-permute-start(bf16[768,512]{1,0:T(8,128)(2,1)} %get-tuple-element.115), channel_id=1, source_target_pairs={{0,32},{32,0},{64,96},{96,64},{128,160},{160,128},{192,224},{224,1... | collective-permute-start | bytes 2359304 | tf_op jit(solution)/shard_map/ppermute | solution.py:400
  136.0 10.2 %collective-permute-start.17 = (f32[256,512]{1,0:T(8,128)}, f32[256,512]{1,0:T(8,128)}, u32[]{:S(2)}, u32[]{:S(2)}) collective-permute-start(f32[256,512]{1,0:T(8,128)} %get-tuple-element.101), channel_id=1, source_target_pairs={{0,32},{32,0},{64,96},{96,64},{128,160},{160,128},{192,224},{224,1... | collective-permute-start | bytes 1572872 | tf_op jit(solution)/shard_map/ppermute | solution.py:400
  136.4 2.9 %collective-permute-start.20 = (f32[32,16]{1,0:T(8,128)S(1)}, f32[32,16]{1,0:T(8,128)S(1)}, u32[]{:S(2)}, u32[]{:S(2)}) collective-permute-start(f32[32,16]{1,0:T(8,128)S(1)} %get-tuple-element.110), channel_id=1, source_target_pairs={{0,192},{32,224},{64,0},{96,32},{128,64},{160,96},{192,128},{224,1... | collective-permute-start | bytes 6152 | tf_op jit(solution)/shard_map/ppermute | solution.py:403
  136.7 6.4 %collective-permute-start.19 = (f32[32,16]{1,0:T(8,128)S(1)}, f32[32,16]{1,0:T(8,128)S(1)}, u32[]{:S(2)}, u32[]{:S(2)}) collective-permute-start(f32[32,16]{1,0:T(8,128)S(1)} %get-tuple-element.110), channel_id=1, source_target_pairs={{0,128},{32,160},{64,192},{96,224},{128,0},{160,32},{192,64},{224,... | collective-permute-start | bytes 6152 | tf_op jit(solution)/shard_map/ppermute | solution.py:403
  139.3 4.1 %collective-permute-start.18 = (f32[32,16]{1,0:T(8,128)S(1)}, f32[32,16]{1,0:T(8,128)S(1)}, u32[]{:S(2)}, u32[]{:S(2)}) collective-permute-start(f32[32,16]{1,0:T(8,128)S(1)} %get-tuple-element.110), channel_id=1, source_target_pairs={{0,64},{32,96},{64,128},{96,160},{128,192},{160,224},{192,0},{224,... | collective-permute-start | bytes 6152 | tf_op jit(solution)/shard_map/ppermute | solution.py:403
  143.4 2.7 %collective-permute-start.21 = (bf16[32,16]{1,0:T(8,128)(2,1)S(1)}, bf16[32,16]{1,0:T(8,128)(2,1)S(1)}, u32[]{:S(2)}, u32[]{:S(2)}) collective-permute-start(bf16[32,16]{1,0:T(8,128)(2,1)S(1)} %add_convert_fusion.2), channel_id=1, source_target_pairs={{0,32},{32,0},{64,96},{96,64},{128,160},{160,128},{192,224},{224,1... | collective-permute-start | bytes 3080 | tf_op jit(solution)/shard_map/ppermute | solution.py:400
  151.1 2.2 %collective-permute-start.24 = (f32[256,512]{1,0:T(8,128)S(1)}, f32[256,512]{1,0:T(8,128)S(1)}, u32[]{:S(2)}, u32[]{:S(2)}) collective-permute-start(f32[256,512]{1,0:T(8,128)S(1)} %shard_map.133), channel_id=1, source_target_pairs={{0,32},{32,0},{64,96},{96,64},{128,160},{160,128},{192,224},{224,1... | collective-permute-start | bytes 1572872 | tf_op jit(solution)/shard_map/ppermute | solution.py:400

commit v4 on v3

--- a/solution.py
+++ b/solution.py
@@ -207,10 +207,11 @@
     half = wd_ref.shape[1] // 2
     leave_blocks(
         [
-            lambda ref=ref, at=at: dot(
-                widen_ref[...], dot(hidden_ref[...], ref[:, at : at + half]).astype(BF)
-            ).astype(BF)
-            for ref in (wd_ref, wo_d_ref)
+            lambda out=out, at=at: dot(widen_ref[...], out[:, at : at + half]).astype(BF)
+            for out in (
+                dot(hidden_ref[...], wd_ref[...]).astype(BF),
+                dot(hidden_ref[...], wo_d_ref[...]).astype(BF),
+            )
             for at in (0, half)
         ],
         buffer, sent_ref, sems,

time: 155 us -> 154 us (level)
  transfers between devices with their start and end apart: 29 -> 29, of which waited for: 15 -> 15; matrix products, arithmetic and copies ran while one was open for 2% -> 2% of each run, Pallas kernels for 23% -> 22%
where the time goes in v4:
time: 154 us; the launch traced here: 153 us
  starting transfers between devices  66.7 us (43%)
  waiting for transfers between devices  43.2 us (28%)
  Pallas kernels  36.3 us (24%)
  local copies, waits for them, and re-layouts  3.15 us (2%)
  other arithmetic  2.85 us (2%)
    pallas_call x16, Pallas kernels, call(): pl.pallas_call(kernel, out_shape=[pltpu.HBM(s, t) if n in placed else jax...  36.3 us
    all_to_all x4, starting transfers between devices, exchange(): lax.all_to_all(value, 'expert', split_axis=0, concat_axis=0, tiled=True)  35.8 us
    ppermute x15, waiting for transfers between devices, along(): lax.ppermute(value, 'dp', [(i, (i + 2 * k) % devices) for i in range(devi...  23.1 us
    ppermute x15, starting transfers between devices, along(): lax.ppermute(value, 'dp', [(i, (i + 2 * k) % devices) for i in range(devi...  16.9 us
    all_to_all x4, waiting for transfers between devices, exchange(): lax.all_to_all(value, 'expert', split_axis=0, concat_axis=0, tiled=True)  16.7 us
    ppermute x10, starting transfers between devices, swap(): return lax.ppermute(value, 'dp', [(i, i ^ 1) for i in range(devices)])  14 us
    ppermute x10, waiting for transfers between devices, swap(): return lax.ppermute(value, 'dp', [(i, i ^ 1) for i in range(devices)])  3.39 us
  transfers between devices with their start and end apart: 29, of which 15 were waited for; matrix products, arithmetic and copies ran while one was open for 2% of the time, Pallas kernels for 22%

profile of v4, /device:TPU:1, one launch (start us, length us, event | category | flops | bytes accessed | tf_op | source)
XLA Modules:
  0.0 153.3 jit_solution(15045450766342203525)
XLA Ops:
  0.6 3.3 %collective-permute-start.4 = (bf16[256,512]{1,0:T(8,128)(2,1)}, bf16[256,512]{1,0:T(8,128)(2,1)S(1)}, u32[]{:S(2)}, u32[]{:S(2)}) collective-permute-start(bf16[256,512]{1,0:T(8,128)(2,1)} %tokens_hbm.1), channel_id=1, source_target_pairs={{0,32},{32,0},{64,96},{96,64},{128,160},{160,128},{192,224},{224,1... | collective-permute-start | bytes 786440 | tf_op jit(solution)/shard_map/ppermute | solution.py:401
  4.0 1.8 %shard_map.119 = (bf16[512,512]{1,0:T(8,128)(2,1)S(1)}, bf16[512,256]{1,0:T(8,128)(2,1)S(1)}) custom-call(s32[2]{0:T(128)S(1)} %pad_add_fusion.ids, s32[16,64]{1,0:T(8,128)} %bitcast.38, bf16[256,512]{1,0:T(8,128)(2,1)} %tokens_hbm.1), custom_call_target="tpu_custom_call" | custom-call | flops 134217728 | bytes 1052672 | tf_op jit(solution)/shard_map/pallas_call | solution.py:44
  5.9 1.6 %shard_map.120 = bf16[512,1024]{1,0:T(8,128)(2,1)} custom-call(s32[2]{0:T(128)S(1)} %pad_add_fusion.ids, bf16[512,512]{1,0:T(8,128)(2,1)S(1)} %get-tuple-element.69.half_ref, bf16[512,256]{1,0:T(8,128)(2,1)S(1)} %get-tuple-element.70.picker_ref, bf16[256,512]{1,0:T(8,128)(2,1)S(1)} %collective-permute-done.4.tokens_ref), custom_call_target="tpu_custom_call" | custom-call | flops 134217728 | bytes 2097152 | tf_op jit(solution)/shard_map/pallas_call | solution.py:44
  7.5 9.7 %all-to-all-start.1 = ((bf16[32,16,1024]{2,1,0:T(8,128)(2,1)}), bf16[32,16,1024]{2,1,0:T(8,128)(2,1)}, u32[]{:S(2)}, u32[]{:S(2)}) async-start(bf16[32,16,1024]{2,1,0:T(8,128)(2,1)} %bitcast.45), calls=%async_computation.1 | async-start | bytes 2097152 | tf_op jit(solution)/shard_map/all_to_all | solution.py:414
  17.8 0.9 copy-done.11
  20.2 2.5 %collective-permute-done.other_ref.other_hbm = bf16[256,512]{1,0:T(8,128)(2,1)S(1)} collective-permute-done((bf16[256,512]{1,0:T(8,128)(2,1)S(1)}, bf16[256,512]{1,0:T(8,128)(2,1)S(1)}, u32[]{:S(2)}, u32[]{:S(2)}) %collective-permute-start) | collective-permute-done | bytes 262176 | tf_op jit(solution)/shard_map/ppermute | solution.py:401
  22.7 2.0 %shard_map.118 = bf16[512,1024]{1,0:T(8,128)(2,1)} custom-call(s32[2]{0:T(128)S(1)} %pad_add_fusion.ids, s32[16,64]{1,0:T(8,128)S(1)} %bitcast.39, bf16[16,64]{1,0:T(8,128)(2,1)S(1)} %bitcast.43, bf16[256,512]{1,0:T(8,128)(2,1)S(1)} %copy-done.5, bf16[256,512]{1,0:T(8,128)(2,1)S(1)} %collective-permute-done.other_ref.other_hbm), custom_call_target="tpu_custom_call" | custom-call | flops 268435456 | bytes 1579008 | tf_op jit(solution)/shard_map/pallas_call | solution.py:44
  24.8 0.9 copy-done.1
  25.9 16.7 %all-to-all-done.1 = bf16[32,16,1024]{2,1,0:T(8,128)(2,1)} async-done(((bf16[32,16,1024]{2,1,0:T(8,128)(2,1)}), bf16[32,16,1024]{2,1,0:T(8,128)(2,1)}, u32[]{:S(2)}, u32[]{:S(2)}) %all-to-all-start.1) | async-done | bytes 1048608 | tf_op jit(solution)/shard_map/all_to_all | solution.py:414
  42.6 8.1 %all-to-all-start = ((bf16[32,16,1024]{2,1,0:T(8,128)(2,1)}), bf16[32,16,1024]{2,1,0:T(8,128)(2,1)}, u32[]{:S(2)}, u32[]{:S(2)}) async-start(bf16[32,16,1024]{2,1,0:T(8,128)(2,1)} %bitcast.46), calls=%async_computation | async-start | bytes 2097152 | tf_op jit(solution)/shard_map/all_to_all | solution.py:414
  50.8 3.8 %shard_map.121 = (bf16[256,1024]{1,0:T(8,128)(2,1)}, bf16[256,512]{1,0:T(8,128)(2,1)}, bf16[512,256]{1,0:T(8,128)(2,1)S(1)}, f32[64,1536]{1,0:T(8,128)S(1)}, bf1...) custom-call(s32[2]{0:T(128)S(1)} %pad_add_fusion.ids, ...), custom_call_target="tpu_custom_call" | custom-call | flops 1073741824 | bytes 6225920 | tf_op jit(solution)/shard_map/pallas_call | solution.py:44
  54.6 1.3 collective-permute-start.8
  55.8 2.5 %collective-permute-start.9 = (bf16[64,1536]{1,0:T(8,128)(2,1)S(1)}, bf16[64,1536]{1,0:T(8,128)(2,1)S(1)}, u32[]{:S(2)}, u32[]{:S(2)}) collective-permute-start(bf16[64,1536]{1,0:T(8,128)(2,1)S(1)} %get-tuple-element.83), channel_id=1, source_target_pairs={{0,128},{32,160},{64,192},{96,224},{128,0},{160,32},{192,64},{224,... | collective-permute-start | bytes 589832 | tf_op jit(solution)/shard_map/ppermute | solution.py:404
  58.3 1.2 collective-permute-start.10
  59.4 1.6 %collective-permute-done.8.r1 = bf16[64,1536]{1,0:T(8,128)(2,1)S(1)} collective-permute-done((bf16[64,1536]{1,0:T(8,128)(2,1)S(1)}, bf16[64,1536]{1,0:T(8,128)(2,1)S(1)}, u32[]{:S(2)}, u32[]{:S(2)}) %collective-permute-start.8) | collective-permute-done | bytes 196640 | tf_op jit(solution)/shard_map/ppermute | solution.py:404
  61.1 5.2 %collective-permute-done.9.r2 = bf16[64,1536]{1,0:T(8,128)(2,1)S(1)} collective-permute-done((bf16[64,1536]{1,0:T(8,128)(2,1)S(1)}, bf16[64,1536]{1,0:T(8,128)(2,1)S(1)}, u32[]{:S(2)}, u32[]{:S(2)}) %collective-permute-start.9) | collective-permute-done | bytes 196640 | tf_op jit(solution)/shard_map/ppermute | solution.py:404
  67.0 2.8 %collective-permute-start.13 = (bf16[64,768]{1,0:T(8,128)(2,1)S(1)}, bf16[64,768]{1,0:T(8,128)(2,1)S(1)}, u32[]{:S(2)}, u32[]{:S(2)}) collective-permute-start(bf16[64,768]{1,0:T(8,128)(2,1)S(1)} %get-tuple-element.85.h0), channel_id=1, source_target_pairs={{0,192},{32,224},{64,0},{96,32},{128,64},{160,96},{192,128},{224,1... | collective-permute-start | bytes 294920 | tf_op jit(solution)/shard_map/ppermute | solution.py:404
  69.7 1.1 collective-permute-start.12
  70.8 1.6 %collective-permute-done.13.h3 = bf16[64,768]{1,0:T(8,128)(2,1)S(1)} collective-permute-done((bf16[64,768]{1,0:T(8,128)(2,1)S(1)}, bf16[64,768]{1,0:T(8,128)(2,1)S(1)}, u32[]{:S(2)}, u32[]{:S(2)}) %collective-permute-start.13) | collective-permute-done | bytes 98336 | tf_op jit(solution)/shard_map/ppermute | solution.py:404
  72.4 2.8 %collective-permute-done.12.h2 = bf16[64,768]{1,0:T(8,128)(2,1)S(1)} collective-permute-done((bf16[64,768]{1,0:T(8,128)(2,1)S(1)}, bf16[64,768]{1,0:T(8,128)(2,1)S(1)}, u32[]{:S(2)}, u32[]{:S(2)}) %collective-permute-start.12) | collective-permute-done | bytes 98336 | tf_op jit(solution)/shard_map/ppermute | solution.py:404
  75.1 1.1 collective-permute-done.11.h1
  76.2 2.3 %shard_map.124 = (bf16[256,768]{1,0:T(8,128)(2,1)}, bf16[512,1024]{1,0:T(8,128)(2,1)}, bf16[512,256]{1,0:T(8,128)(2,1)}, f32[64,1536]{1,0:T(8,128)}) custom-call(s32[2]{0:T(128)S(1)} %pad_add_fusion.ids, bf16[64,768]{1,0:T(8,128)(2,1)S(1)} %get-tuple-element.85.h0, bf16[64,768]{1,0:T(8,128)(2,1)S(1)} %collective-permute-done.11.h1, ...), custom_call_target="tpu_custom_call" | custom-call | flops 671088640 | bytes 4718592 | tf_op jit(solution)/shard_map/pallas_call | solution.py:44
  78.5 8.7 %all-to-all-start.3 = ((bf16[32,16,1024]{2,1,0:T(8,128)(2,1)}), bf16[32,16,1024]{2,1,0:T(8,128)(2,1)S(1)}, u32[]{:S(2)}, u32[]{:S(2)}) async-start(bf16[32,16,1024]{2,1,0:T(8,128)(2,1)} %bitcast.49), calls=%async_computation.3 | async-start | bytes 2097152 | tf_op jit(solution)/shard_map/all_to_all | solution.py:414
  87.2 3.3 %shard_map.122 = (bf16[256,1024]{1,0:T(8,128)(2,1)}, f32[64,768]{1,0:T(8,128)S(1)}, bf16[64,768]{1,0:T(8,128)(2,1)S(1)}, bf16[64,768]{1,0:T(8,128)(2,1)S(1)}, bf16[64,768]{1,0:T(8,128)(2,1)S(1)}) custom-call(s32[2]{0:T(128)S(1)} %pad_add_fusion.ids, bf16[512,1024]{1,0:T(8,128)(2,1)} %bitcast.13.got_hbm, bf16[256,512]{1,0:T(8,128)(2,1)} %get-tuple-element.74.narrow_hbm, ...), custom_call_target="tpu_custom_call" | custom-call | flops 671088640 | bytes 3899392 | tf_op jit(solution)/shard_map/pallas_call | solution.py:44
  91.0 1.6 %collective-permute-start.6 = (bf16[64,768]{1,0:T(8,128)(2,1)S(1)}, bf16[64,768]{1,0:T(8,128)(2,1)S(1)}, u32[]{:S(2)}, u32[]{:S(2)}) collective-permute-start(bf16[64,768]{1,0:T(8,128)(2,1)S(1)} %get-tuple-element.79), channel_id=1, source_target_pairs={{0,128},{32,160},{64,192},{96,224},{128,0},{160,32},{192,64},{224,... | collective-permute-start | bytes 294920 | tf_op jit(solution)/shard_map/ppermute | solution.py:404
  92.6 2.0 %collective-permute-start.7 = (bf16[64,768]{1,0:T(8,128)(2,1)S(1)}, bf16[64,768]{1,0:T(8,128)(2,1)S(1)}, u32[]{:S(2)}, u32[]{:S(2)}) collective-permute-start(bf16[64,768]{1,0:T(8,128)(2,1)S(1)} %get-tuple-element.80), channel_id=1, source_target_pairs={{0,192},{32,224},{64,0},{96,32},{128,64},{160,96},{192,128},{224,1... | collective-permute-start | bytes 294920 | tf_op jit(solution)/shard_map/ppermute | solution.py:404
  94.5 2.0 %collective-permute-done.5.r1 = bf16[64,768]{1,0:T(8,128)(2,1)S(1)} collective-permute-done((bf16[64,768]{1,0:T(8,128)(2,1)S(1)}, bf16[64,768]{1,0:T(8,128)(2,1)S(1)}, u32[]{:S(2)}, u32[]{:S(2)}) %collective-permute-start.5) | collective-permute-done | bytes 98336 | tf_op jit(solution)/shard_map/ppermute | solution.py:404
  97.6 2.8 %collective-permute-start.16 = (bf16[64,1536]{1,0:T(8,128)(2,1)S(1)}, bf16[64,1536]{1,0:T(8,128)(2,1)S(1)}, u32[]{:S(2)}, u32[]{:S(2)}) collective-permute-start(bf16[64,1536]{1,0:T(8,128)(2,1)S(1)} %shard_map.125.g0), channel_id=1, source_target_pairs={{0,192},{32,224},{64,0},{96,32},{128,64},{160,96},{192,128},{224,1... | collective-permute-start | bytes 589832 | tf_op jit(solution)/shard_map/ppermute | solution.py:404
  100.3 0.7 collective-permute-start.15
  101.0 1.7 %shard_map.126.wo_u_ref = bf16[512,768]{1,0:T(8,128)(2,1)S(1)} custom-call(s32[2]{0:T(128)S(1)} %pad_add_fusion.ids, bf16[512,768]{1,0:T(8,128)(2,1)} %copy-done.9), custom_call_target="tpu_custom_call" | custom-call | bytes 1572864 | tf_op jit(solution)/shard_map/pallas_call | solution.py:44
  102.7 2.3 %collective-permute-done.16.g3 = bf16[64,1536]{1,0:T(8,128)(2,1)S(1)} collective-permute-done((bf16[64,1536]{1,0:T(8,128)(2,1)S(1)}, bf16[64,1536]{1,0:T(8,128)(2,1)S(1)}, u32[]{:S(2)}, u32[]{:S(2)}) %collective-permute-start.16) | collective-permute-done | bytes 196640 | tf_op jit(solution)/shard_map/ppermute | solution.py:404
  105.0 1.6 %collective-permute-done.15.g2 = bf16[64,1536]{1,0:T(8,128)(2,1)S(1)} collective-permute-done((bf16[64,1536]{1,0:T(8,128)(2,1)S(1)}, bf16[64,1536]{1,0:T(8,128)(2,1)S(1)}, u32[]{:S(2)}, u32[]{:S(2)}) %collective-permute-start.15) | collective-permute-done | bytes 196640 | tf_op jit(solution)/shard_map/ppermute | solution.py:404
  106.7 2.1 %collective-permute-done.14.g1 = bf16[64,1536]{1,0:T(8,128)(2,1)S(1)} collective-permute-done((bf16[64,1536]{1,0:T(8,128)(2,1)S(1)}, bf16[64,1536]{1,0:T(8,128)(2,1)S(1)}, u32[]{:S(2)}, u32[]{:S(2)}) %collective-permute-start.14) | collective-permute-done | bytes 196640 | tf_op jit(solution)/shard_map/ppermute | solution.py:404
  108.7 3.1 %shard_map.127 = (bf16[256,1536]{1,0:T(8,128)(2,1)}, bf16[512,1024]{1,0:T(8,128)(2,1)}) custom-call(s32[2]{0:T(128)S(1)} %pad_add_fusion.ids, bf16[64,1536]{1,0:T(8,128)(2,1)S(1)} %shard_map.125.g0, bf16[64,1536]{1,0:T(8,128)(2,1)S(1)} %collective-permute-done.14.g1, bf16[64,1536]{1,0:T(8,128)(2,1)S(1)} %collective-permute-done.15.g2, ...), custom_call_target="tpu_custom_call" | custom-call | flops 1073741824 | bytes 6029312 | tf_op jit(solution)/shard_map/pallas_call | solution.py:44
  111.9 9.2 %all-to-all-start.2 = ((bf16[32,16,1024]{2,1,0:T(8,128)(2,1)}), bf16[32,16,1024]{2,1,0:T(8,128)(2,1)S(1)}, u32[]{:S(2)}, u32[]{:S(2)}) async-start(bf16[32,16,1024]{2,1,0:T(8,128)(2,1)} %bitcast.47), calls=%async_computation.2 | async-start | bytes 2097152 | tf_op jit(solution)/shard_map/all_to_all | solution.py:414
  121.1 3.8 %shard_map.128 = (f32[256,512]{1,0:T(8,128)}, f32[256,512]{1,0:T(8,128)}, f32[32,16]{1,0:T(8,128)S(1)}) custom-call(s32[2]{0:T(128)S(1)} %pad_add_fusion.ids, bf16[512,1024]{1,0:T(8,128)(2,1)} %bitcast.48, bf16[256,512]{1,0:T(8,128)(2,1)} %own_hbm.1, bf16[256,512]{1,0:T(8,128)(2,1)} %copy-done.6, s32[16,64]{1,0:T(8,128)S(1)} %bitcast.40, ...), custom_call_target="tpu_custom_call" | custom-call | flops 536870912 | bytes 2629632 | tf_op jit(solution)/shard_map/pallas_call | solution.py:44
  125.0 3.9 %shard_map.130 = (bf16[512,1536]{1,0:T(8,128)(2,1)}, bf16[768,512]{1,0:T(8,128)(2,1)}) custom-call(s32[2]{0:T(128)S(1)} %pad_add_fusion.ids, bf16[256,1024]{1,0:T(8,128)(2,1)} %get-tuple-element.103.rows_in_hbm, bf16[256,1536]{1,0:T(8,128)(2,1)} %get-tuple-element.104.grads_hbm, bf16[256,768]{1,0:T(8,128)(2,1)} %get-tuple-element.105.hidden_hbm, ...), custom_call_target="tpu_custom_call" | custom-call | flops 603979776 | bytes 4587520 | tf_op jit(solution)/shard_map/pallas_call | solution.py:44
  128.9 6.2 %collective-permute-start.22 = (bf16[512,1536]{1,0:T(8,128)(2,1)}, bf16[512,1536]{1,0:T(8,128)(2,1)S(1)}, u32[]{:S(2)}, u32[]{:S(2)}) collective-permute-start(bf16[512,1536]{1,0:T(8,128)(2,1)} %get-tuple-element.114), channel_id=1, source_target_pairs={{0,32},{32,0},{64,96},{96,64},{128,160},{160,128},{192,224},{224,1... | collective-permute-start | bytes 4718600 | tf_op jit(solution)/shard_map/ppermute | solution.py:401
  136.3 2.2 %collective-permute-done.20 = f32[32,16]{1,0:T(8,128)S(1)} collective-permute-done((f32[32,16]{1,0:T(8,128)S(1)}, f32[32,16]{1,0:T(8,128)S(1)}, u32[]{:S(2)}, u32[]{:S(2)}) %collective-permute-start.20) | collective-permute-done | bytes 2080 | tf_op jit(solution)/shard_map/ppermute | solution.py:404
  138.5 3.8 %shard_map.129 = (bf16[2,512,768]{2,1,0:T(8,128)(2,1)}, bf16[2,512,768]{2,1,0:T(8,128)(2,1)}, bf16[2,768,512]{2,1,0:T(8,128)(2,1)}) custom-call(s32[2]{0:T(128)S(1)} %pad_add_fusion.ids, bf16[256,1024]{1,0:T(8,128)(2,1)} %get-tuple-element.103.rows_in_hbm, bf16[256,1536]{1,0:T(8,128)(2,1)} %get-tuple-element.104.grads_hbm, ...), custom_call_target="tpu_custom_call" | custom-call | flops 603979776 | bytes 6946816 | tf_op jit(solution)/shard_map/pallas_call | solution.py:44
  142.6 1.9 %collective-permute-start.21 = (bf16[32,16]{1,0:T(8,128)(2,1)S(1)}, bf16[32,16]{1,0:T(8,128)(2,1)S(1)}, u32[]{:S(2)}, u32[]{:S(2)}) collective-permute-start(bf16[32,16]{1,0:T(8,128)(2,1)S(1)} %add_convert_fusion.2), channel_id=1, source_target_pairs={{0,32},{32,0},{64,96},{96,64},{128,160},{160,128},{192,224},{224,1... | collective-permute-start | bytes 3080 | tf_op jit(solution)/shard_map/ppermute | solution.py:401
  144.5 0.8 collective-permute-done.21
  145.4 2.0 %add_convert_fusion.1 = bf16[256,512]{1,0:T(8,128)(2,1)} fusion(f32[256,512]{1,0:T(8,128)} %get-tuple-element.94, f32[256,512]{1,0:T(8,128)} %collective-permute-done.17), kind=kLoop, calls=%fused_computation.7 | loop fusion | flops 262144 | bytes 1310720 | tf_op jit(solution)/shard_map/convert_element_type | solution.py:574
  147.3 2.0 %shard_map.131 = (bf16[2,512,768]{2,1,0:T(8,128)(2,1)}, bf16[2,512,768]{2,1,0:T(8,128)(2,1)}, bf16[2,768,512]{2,1,0:T(8,128)(2,1)}) custom-call(s32[2]{0:T(128)S(1)} %pad_add_fusion.ids, bf16[512,1536]{1,0:T(8,128)(2,1)S(1)} %collective-permute-done.22.got_in_ref, ...), custom_call_target="tpu_custom_call", output_to_operand_aliasing={{0}: (3, {}), {1}: (4, {}), {2}: (5, {})} | custom-call | bytes 11796480 | tf_op jit(solution)/shard_map/pallas_call | solution.py:44
  149.3 0.9 shard_map.133
  150.9 0.7 copy.17
  151.5 0.9 shard_map.132
  152.5 0.8 add_convert_fusion
  (64 shorter events, 6.6 us)
Async XLA Ops:
  0.6 5.2 %collective-permute-start.4 = (bf16[256,512]{1,0:T(8,128)(2,1)}, bf16[256,512]{1,0:T(8,128)(2,1)S(1)}, u32[]{:S(2)}, u32[]{:S(2)}) collective-permute-start(bf16[256,512]{1,0:T(8,128)(2,1)} %tokens_hbm.1), channel_id=1, source_target_pairs={{0,32},{32,0},{64,96},{96,64},{128,160},{160,128},{192,224},{224,1... | collective-permute-start | bytes 786440 | tf_op jit(solution)/shard_map/ppermute | solution.py:401
  7.5 9.8 %copy-start.10 = (bf16[2,512,768]{2,1,0:T(8,128)(2,1)S(1)}, bf16[2,512,768]{2,1,0:T(8,128)(2,1)}, u32[]{:S(2)}) copy-start(bf16[2,512,768]{2,1,0:T(8,128)(2,1)} %param.11) | copy-start | bytes 4718596
  7.5 35.1 %all-to-all-start.1 = ((bf16[32,16,1024]{2,1,0:T(8,128)(2,1)}), bf16[32,16,1024]{2,1,0:T(8,128)(2,1)}, u32[]{:S(2)}, u32[]{:S(2)}) async-start(bf16[32,16,1024]{2,1,0:T(8,128)(2,1)} %bitcast.45), calls=%async_computation.1 | async-start | bytes 2097152 | tf_op jit(solution)/shard_map/all_to_all | solution.py:414
  17.3 1.4 copy-start.11
  17.4 1.8 %copy-start.12 = (bf16[2,768,512]{2,1,0:T(8,128)(2,1)S(1)}, bf16[2,768,512]{2,1,0:T(8,128)(2,1)}, u32[]{:S(2)}) copy-start(bf16[2,768,512]{2,1,0:T(8,128)(2,1)} %param.13) | copy-start | bytes 4718596
  17.4 7.3 %collective-permute-start.1 = (bf16[512,768]{1,0:T(8,128)(2,1)S(1)}, bf16[512,768]{1,0:T(8,128)(2,1)S(1)}, u32[]{:S(2)}, u32[]{:S(2)}) collective-permute-start(bf16[512,768]{1,0:T(8,128)(2,1)S(1)} %get-tuple-element.138), channel_id=1, source_target_pairs={{0,32},{32,0},{64,96},{96,64},{128,160},{160,128},{192,224},{224,1... | collective-permute-start | bytes 2359304 | tf_op jit(solution)/shard_map/ppermute | solution.py:401
  18.8 1.1 copy-start.5
  18.8 3.9 %copy-start.7 = (s32[1,64,16]{1,2,0:T(8,128)S(1)}, s32[1,64,16]{1,2,0:T(8,128)}, u32[]{:S(2)}) copy-start(s32[1,64,16]{1,2,0:T(8,128)} %param.9) | copy-start | bytes 12292
  18.8 3.9 %copy-start.8 = (bf16[1,64,16]{1,2,0:T(8,128)(2,1)S(1)}, bf16[1,64,16]{1,2,0:T(8,128)(2,1)}, u32[]{:S(2)}) copy-start(bf16[1,64,16]{1,2,0:T(8,128)(2,1)} %param.10) | copy-start | bytes 6148
  18.8 5.9 %collective-permute-start.2 = (bf16[512,768]{1,0:T(8,128)(2,1)S(1)}, bf16[512,768]{1,0:T(8,128)(2,1)S(1)}, u32[]{:S(2)}, u32[]{:S(2)}) collective-permute-start(bf16[512,768]{1,0:T(8,128)(2,1)S(1)} %get-tuple-element.136), channel_id=1, source_target_pairs={{0,32},{32,0},{64,96},{96,64},{128,160},{160,128},{192,224},{224,1... | collective-permute-start | bytes 2359304 | tf_op jit(solution)/shard_map/ppermute | solution.py:401
  19.3 56.8 %copy-start = (bf16[768,512]{1,0:T(8,128)(2,1)}, bf16[768,512]{1,0:T(8,128)(2,1)S(1)}, u32[]{:S(2)}) copy-start(bf16[768,512]{1,0:T(8,128)(2,1)S(1)} %get-tuple-element.75.wd_hbm.wd_ref) | copy-start | bytes 2359300
  19.3 5.4 %collective-permute-start.3 = (bf16[768,512]{1,0:T(8,128)(2,1)S(1)}, bf16[768,512]{1,0:T(8,128)(2,1)S(1)}, u32[]{:S(2)}, u32[]{:S(2)}) collective-permute-start(bf16[768,512]{1,0:T(8,128)(2,1)S(1)} %get-tuple-element.134), channel_id=1, source_target_pairs={{0,32},{32,0},{64,96},{96,64},{128,160},{160,128},{192,224},{224,1... | collective-permute-start | bytes 2359304 | tf_op jit(solution)/shard_map/ppermute | solution.py:401
  19.8 2.9 %collective-permute-start = (bf16[256,512]{1,0:T(8,128)(2,1)S(1)}, bf16[256,512]{1,0:T(8,128)(2,1)S(1)}, u32[]{:S(2)}, u32[]{:S(2)}) collective-permute-start(bf16[256,512]{1,0:T(8,128)(2,1)S(1)} %copy-done.5), channel_id=1, source_target_pairs={{0,32},{32,0},{64,96},{96,64},{128,160},{160,128},{192,224},{224,1... | collective-permute-start | bytes 786440 | tf_op jit(solution)/shard_map/ppermute | solution.py:401
  22.7 2.1 %copy-start.6 = (bf16[256,512]{1,0:T(8,128)(2,1)}, bf16[256,512]{1,0:T(8,128)(2,1)S(1)}, u32[]{:S(2)}) copy-start(bf16[256,512]{1,0:T(8,128)(2,1)S(1)} %collective-permute-done.other_ref.other_hbm) | copy-start | bytes 786436
  24.8 1.1 copy-start.9
  24.8 0.9 copy-start.1
  42.6 35.8 %all-to-all-start = ((bf16[32,16,1024]{2,1,0:T(8,128)(2,1)}), bf16[32,16,1024]{2,1,0:T(8,128)(2,1)}, u32[]{:S(2)}, u32[]{:S(2)}) async-start(bf16[32,16,1024]{2,1,0:T(8,128)(2,1)} %bitcast.46), calls=%async_computation | async-start | bytes 2097152 | tf_op jit(solution)/shard_map/all_to_all | solution.py:414
  50.8 25.4 %copy-start.2 = (bf16[768,512]{1,0:T(8,128)(2,1)S(1)}, bf16[768,512]{1,0:T(8,128)(2,1)}, u32[]{:S(2)}) copy-start(bf16[768,512]{1,0:T(8,128)(2,1)} %copy-done.1) | copy-start | bytes 2359300
  54.6 6.5 %collective-permute-start.8 = (bf16[64,1536]{1,0:T(8,128)(2,1)S(1)}, bf16[64,1536]{1,0:T(8,128)(2,1)S(1)}, u32[]{:S(2)}, u32[]{:S(2)}) collective-permute-start(bf16[64,1536]{1,0:T(8,128)(2,1)S(1)} %get-tuple-element.82), channel_id=1, source_target_pairs={{0,64},{32,96},{64,128},{96,160},{128,192},{160,224},{192,0},{224,... | collective-permute-start | bytes 589832 | tf_op jit(solution)/shard_map/ppermute | solution.py:404
  55.8 10.5 %collective-permute-start.9 = (bf16[64,1536]{1,0:T(8,128)(2,1)S(1)}, bf16[64,1536]{1,0:T(8,128)(2,1)S(1)}, u32[]{:S(2)}, u32[]{:S(2)}) collective-permute-start(bf16[64,1536]{1,0:T(8,128)(2,1)S(1)} %get-tuple-element.83), channel_id=1, source_target_pairs={{0,128},{32,160},{64,192},{96,224},{128,0},{160,32},{192,64},{224,... | collective-permute-start | bytes 589832 | tf_op jit(solution)/shard_map/ppermute | solution.py:404
  58.3 8.0 %collective-permute-start.10 = (bf16[64,1536]{1,0:T(8,128)(2,1)S(1)}, bf16[64,1536]{1,0:T(8,128)(2,1)S(1)}, u32[]{:S(2)}, u32[]{:S(2)}) collective-permute-start(bf16[64,1536]{1,0:T(8,128)(2,1)S(1)} %get-tuple-element.84), channel_id=1, source_target_pairs={{0,192},{32,224},{64,0},{96,32},{128,64},{160,96},{192,128},{224,1... | collective-permute-start | bytes 589832 | tf_op jit(solution)/shard_map/ppermute | solution.py:404
  67.0 5.4 %collective-permute-start.13 = (bf16[64,768]{1,0:T(8,128)(2,1)S(1)}, bf16[64,768]{1,0:T(8,128)(2,1)S(1)}, u32[]{:S(2)}, u32[]{:S(2)}) collective-permute-start(bf16[64,768]{1,0:T(8,128)(2,1)S(1)} %get-tuple-element.85.h0), channel_id=1, source_target_pairs={{0,192},{32,224},{64,0},{96,32},{128,64},{160,96},{192,128},{224,1... | collective-permute-start | bytes 294920 | tf_op jit(solution)/shard_map/ppermute | solution.py:404
  69.7 5.4 %collective-permute-start.12 = (bf16[64,768]{1,0:T(8,128)(2,1)S(1)}, bf16[64,768]{1,0:T(8,128)(2,1)S(1)}, u32[]{:S(2)}, u32[]{:S(2)}) collective-permute-start(bf16[64,768]{1,0:T(8,128)(2,1)S(1)} %get-tuple-element.85.h0), channel_id=1, source_target_pairs={{0,128},{32,160},{64,192},{96,224},{128,0},{160,32},{192,64},{224,... | collective-permute-start | bytes 294920 | tf_op jit(solution)/shard_map/ppermute | solution.py:404
  70.8 5.4 %collective-permute-start.11 = (bf16[64,768]{1,0:T(8,128)(2,1)S(1)}, bf16[64,768]{1,0:T(8,128)(2,1)S(1)}, u32[]{:S(2)}, u32[]{:S(2)}) collective-permute-start(bf16[64,768]{1,0:T(8,128)(2,1)S(1)} %get-tuple-element.85.h0), channel_id=1, source_target_pairs={{0,64},{32,96},{64,128},{96,160},{128,192},{160,224},{192,0},{224,... | collective-permute-start | bytes 294920 | tf_op jit(solution)/shard_map/ppermute | solution.py:404
  78.5 33.3 %all-to-all-start.3 = ((bf16[32,16,1024]{2,1,0:T(8,128)(2,1)}), bf16[32,16,1024]{2,1,0:T(8,128)(2,1)S(1)}, u32[]{:S(2)}, u32[]{:S(2)}) async-start(bf16[32,16,1024]{2,1,0:T(8,128)(2,1)} %bitcast.49), calls=%async_computation.3 | async-start | bytes 2097152 | tf_op jit(solution)/shard_map/all_to_all | solution.py:414
  87.2 9.7 %copy-start.3 = (f32[64,1536]{1,0:T(8,128)S(1)}, f32[64,1536]{1,0:T(8,128)}, u32[]{:S(2)}) copy-start(f32[64,1536]{1,0:T(8,128)} %get-tuple-element.88.pre_ref) | copy-start | bytes 1179652
  90.5 18.3 %copy-start.4 = (bf16[512,256]{1,0:T(8,128)(2,1)S(1)}, bf16[512,256]{1,0:T(8,128)(2,1)}, u32[]{:S(2)}) copy-start(bf16[512,256]{1,0:T(8,128)(2,1)} %get-tuple-element.91.widen_ref) | copy-start | bytes 786436
  90.5 6.0 %collective-permute-start.5 = (bf16[64,768]{1,0:T(8,128)(2,1)S(1)}, bf16[64,768]{1,0:T(8,128)(2,1)S(1)}, u32[]{:S(2)}, u32[]{:S(2)}) collective-permute-start(bf16[64,768]{1,0:T(8,128)(2,1)S(1)} %get-tuple-element.78), channel_id=1, source_target_pairs={{0,64},{32,96},{64,128},{96,160},{128,192},{160,224},{192,0},{224,... | collective-permute-start | bytes 294920 | tf_op jit(solution)/shard_map/ppermute | solution.py:404
  91.0 5.5 %collective-permute-start.6 = (bf16[64,768]{1,0:T(8,128)(2,1)S(1)}, bf16[64,768]{1,0:T(8,128)(2,1)S(1)}, u32[]{:S(2)}, u32[]{:S(2)}) collective-permute-start(bf16[64,768]{1,0:T(8,128)(2,1)S(1)} %get-tuple-element.79), channel_id=1, source_target_pairs={{0,128},{32,160},{64,192},{96,224},{128,0},{160,32},{192,64},{224,... | collective-permute-start | bytes 294920 | tf_op jit(solution)/shard_map/ppermute | solution.py:404
  92.6 4.3 %collective-permute-start.7 = (bf16[64,768]{1,0:T(8,128)(2,1)S(1)}, bf16[64,768]{1,0:T(8,128)(2,1)S(1)}, u32[]{:S(2)}, u32[]{:S(2)}) collective-permute-start(bf16[64,768]{1,0:T(8,128)(2,1)S(1)} %get-tuple-element.80), channel_id=1, source_target_pairs={{0,192},{32,224},{64,0},{96,32},{128,64},{160,96},{192,128},{224,1... | collective-permute-start | bytes 294920 | tf_op jit(solution)/shard_map/ppermute | solution.py:404
  97.6 7.5 %collective-permute-start.16 = (bf16[64,1536]{1,0:T(8,128)(2,1)S(1)}, bf16[64,1536]{1,0:T(8,128)(2,1)S(1)}, u32[]{:S(2)}, u32[]{:S(2)}) collective-permute-start(bf16[64,1536]{1,0:T(8,128)(2,1)S(1)} %shard_map.125.g0), channel_id=1, source_target_pairs={{0,192},{32,224},{64,0},{96,32},{128,64},{160,96},{192,128},{224,1... | collective-permute-start | bytes 589832 | tf_op jit(solution)/shard_map/ppermute | solution.py:404
  100.3 6.3 %collective-permute-start.15 = (bf16[64,1536]{1,0:T(8,128)(2,1)S(1)}, bf16[64,1536]{1,0:T(8,128)(2,1)S(1)}, u32[]{:S(2)}, u32[]{:S(2)}) collective-permute-start(bf16[64,1536]{1,0:T(8,128)(2,1)S(1)} %shard_map.125.g0), channel_id=1, source_target_pairs={{0,128},{32,160},{64,192},{96,224},{128,0},{160,32},{192,64},{224,... | collective-permute-start | bytes 589832 | tf_op jit(solution)/shard_map/ppermute | solution.py:404
  101.0 7.7 %collective-permute-start.14 = (bf16[64,1536]{1,0:T(8,128)(2,1)S(1)}, bf16[64,1536]{1,0:T(8,128)(2,1)S(1)}, u32[]{:S(2)}, u32[]{:S(2)}) collective-permute-start(bf16[64,1536]{1,0:T(8,128)(2,1)S(1)} %shard_map.125.g0), channel_id=1, source_target_pairs={{0,64},{32,96},{64,128},{96,160},{128,192},{160,224},{192,0},{224,... | collective-permute-start | bytes 589832 | tf_op jit(solution)/shard_map/ppermute | solution.py:404
  111.8 9.3 %copy-start.13 = (bf16[32,16,1024]{2,1,0:T(8,128)(2,1)}, bf16[32,16,1024]{2,1,0:T(8,128)(2,1)S(1)}, u32[]{:S(2)}) copy-start(bf16[32,16,1024]{2,1,0:T(8,128)(2,1)S(1)} %all-to-all-done.3) | copy-start | bytes 3145732
  111.9 37.5 %all-to-all-start.2 = ((bf16[32,16,1024]{2,1,0:T(8,128)(2,1)}), bf16[32,16,1024]{2,1,0:T(8,128)(2,1)S(1)}, u32[]{:S(2)}, u32[]{:S(2)}) async-start(bf16[32,16,1024]{2,1,0:T(8,128)(2,1)} %bitcast.47), calls=%async_computation.2 | async-start | bytes 2097152 | tf_op jit(solution)/shard_map/all_to_all | solution.py:414
  128.9 18.5 %collective-permute-start.22 = (bf16[512,1536]{1,0:T(8,128)(2,1)}, bf16[512,1536]{1,0:T(8,128)(2,1)S(1)}, u32[]{:S(2)}, u32[]{:S(2)}) collective-permute-start(bf16[512,1536]{1,0:T(8,128)(2,1)} %get-tuple-element.114), channel_id=1, source_target_pairs={{0,32},{32,0},{64,96},{96,64},{128,160},{160,128},{192,224},{224,1... | collective-permute-start | bytes 4718600 | tf_op jit(solution)/shard_map/ppermute | solution.py:401
  135.1 12.2 %collective-permute-start.23 = (bf16[768,512]{1,0:T(8,128)(2,1)}, bf16[768,512]{1,0:T(8,128)(2,1)S(1)}, u32[]{:S(2)}, u32[]{:S(2)}) collective-permute-start(bf16[768,512]{1,0:T(8,128)(2,1)} %get-tuple-element.115), channel_id=1, source_target_pairs={{0,32},{32,0},{64,96},{96,64},{128,160},{160,128},{192,224},{224,1... | collective-permute-start | bytes 2359304 | tf_op jit(solution)/shard_map/ppermute | solution.py:401
  135.2 10.2 %collective-permute-start.17 = (f32[256,512]{1,0:T(8,128)}, f32[256,512]{1,0:T(8,128)}, u32[]{:S(2)}, u32[]{:S(2)}) collective-permute-start(f32[256,512]{1,0:T(8,128)} %get-tuple-element.101), channel_id=1, source_target_pairs={{0,32},{32,0},{64,96},{96,64},{128,160},{160,128},{192,224},{224,1... | collective-permute-start | bytes 1572872 | tf_op jit(solution)/shard_map/ppermute | solution.py:401
  135.6 2.9 %collective-permute-start.20 = (f32[32,16]{1,0:T(8,128)S(1)}, f32[32,16]{1,0:T(8,128)S(1)}, u32[]{:S(2)}, u32[]{:S(2)}) collective-permute-start(f32[32,16]{1,0:T(8,128)S(1)} %get-tuple-element.110), channel_id=1, source_target_pairs={{0,192},{32,224},{64,0},{96,32},{128,64},{160,96},{192,128},{224,1... | collective-permute-start | bytes 6152 | tf_op jit(solution)/shard_map/ppermute | solution.py:404
  135.9 6.4 %collective-permute-start.19 = (f32[32,16]{1,0:T(8,128)S(1)}, f32[32,16]{1,0:T(8,128)S(1)}, u32[]{:S(2)}, u32[]{:S(2)}) collective-permute-start(f32[32,16]{1,0:T(8,128)S(1)} %get-tuple-element.110), channel_id=1, source_target_pairs={{0,128},{32,160},{64,192},{96,224},{128,0},{160,32},{192,64},{224,... | collective-permute-start | bytes 6152 | tf_op jit(solution)/shard_map/ppermute | solution.py:404
  138.5 4.1 %collective-permute-start.18 = (f32[32,16]{1,0:T(8,128)S(1)}, f32[32,16]{1,0:T(8,128)S(1)}, u32[]{:S(2)}, u32[]{:S(2)}) collective-permute-start(f32[32,16]{1,0:T(8,128)S(1)} %get-tuple-element.110), channel_id=1, source_target_pairs={{0,64},{32,96},{64,128},{96,160},{128,192},{160,224},{192,0},{224,... | collective-permute-start | bytes 6152 | tf_op jit(solution)/shard_map/ppermute | solution.py:404
  142.6 2.7 %collective-permute-start.21 = (bf16[32,16]{1,0:T(8,128)(2,1)S(1)}, bf16[32,16]{1,0:T(8,128)(2,1)S(1)}, u32[]{:S(2)}, u32[]{:S(2)}) collective-permute-start(bf16[32,16]{1,0:T(8,128)(2,1)S(1)} %add_convert_fusion.2), channel_id=1, source_target_pairs={{0,32},{32,0},{64,96},{96,64},{128,160},{160,128},{192,224},{224,1... | collective-permute-start | bytes 3080 | tf_op jit(solution)/shard_map/ppermute | solution.py:401
  150.3 2.2 %collective-permute-start.24 = (f32[256,512]{1,0:T(8,128)S(1)}, f32[256,512]{1,0:T(8,128)S(1)}, u32[]{:S(2)}, u32[]{:S(2)}) collective-permute-start(f32[256,512]{1,0:T(8,128)S(1)} %shard_map.133), channel_id=1, source_target_pairs={{0,32},{32,0},{64,96},{96,64},{128,160},{160,128},{192,224},{224,1... | collective-permute-start | bytes 1572872 | tf_op jit(solution)/shard_map/ppermute | solution.py:401

commit v5 on v4

--- a/solution.py
+++ b/solution.py
@@ -312,6 +312,16 @@
     mine_out.wait()
 
 
+def place_dots(ids, mine_ref, other_ref, out_ref):
+    owners, experts = mine_ref.shape[0], out_ref.shape[1]
+    out = jnp.zeros(out_ref.shape, F32)
+    for ref, core in ((mine_ref, ids[0]), (other_ref, 1 - ids[0])):
+        expert = 2 * iota((owners, experts), 0) + core
+        there = jnp.where(iota((owners, experts), 1) == expert, 1.0, 0.0).astype(BF)
+        out = out + dot_tn(ref[...], there)
+    out_ref[...] = out.astype(BF)
+
+
 def adder_of(ids, slot_ref, count, slots):
     token_row = slot_row(slot_ref[...].astype(F32), ids[0], slots)
     return jnp.where(iota((count, slots), 0).astype(F32) == token_row, 1.0, 0.0).astype(BF)
@@ -574,11 +584,9 @@
     moe_out = (out_mine + swap(out_theirs)).astype(BF)
     *dots, weight_grads = lax.optimization_barrier((*gather_x(dots), weight_grads))
     dots = sum(dots).astype(BF)
-    dots_other = swap(dots)
-    gate_grad = jnp.where(
-        core == 0, jnp.stack([dots, dots_other], 1), jnp.stack([dots_other, dots], 1)
-    )
-    gate_grad = gate_grad.reshape(experts, pair).T
+    (gate_grad,) = call(
+        place_dots, ids, (dots, swap(dots)), [((pair, experts), BF)], 4 * pair * experts * senders
+    )
     grad_gate_w, grad_up_w, grad_down_w = call(
         weights_got,
         ids,

time: 154 us -> 154 us (level)
  starting transfers between devices: 66.7 us -> 68.5 us
    ppermute x10, starting transfers between devices: 14 us -> 15.8 us  [swap(): return lax.ppermute(value, 'dp', [(i, i ^ 1) for i in range(devices)])]
    pallas_call x16 -> x17, Pallas kernels: 36.3 us -> 35.7 us  [call(): pl.pallas_call(kernel, out_shape=[pltpu.HBM(s, t) if n in placed else jax...]
  transfers between devices with their start and end apart: 29 -> 29, of which waited for: 15 -> 16; matrix products, arithmetic and copies ran while one was open for 2% -> 1% of each run, Pallas kernels for 22% -> 22%
where the time goes in v5:
time: 154 us; the launch traced here: 153 us
  starting transfers between devices  68.5 us (44%)
  waiting for transfers between devices  43.8 us (28%)
  Pallas kernels  35.7 us (23%)
  local copies, waits for them, and re-layouts  2.48 us (2%)
  other arithmetic  1.63 us (1%)
    all_to_all x4, starting transfers between devices, exchange(): lax.all_to_all(value, 'expert', split_axis=0, concat_axis=0, tiled=True)  35.8 us
    pallas_call x17, Pallas kernels, call(): pl.pallas_call(kernel, out_shape=[pltpu.HBM(s, t) if n in placed else jax...  35.7 us
    ppermute x15, waiting for transfers between devices, along(): lax.ppermute(value, 'dp', [(i, (i + 2 * k) % devices) for i in range(devi...  23.1 us
    ppermute x15, starting transfers between devices, along(): lax.ppermute(value, 'dp', [(i, (i + 2 * k) % devices) for i in range(devi...  16.9 us
    all_to_all x4, waiting for transfers between devices, exchange(): lax.all_to_all(value, 'expert', split_axis=0, concat_axis=0, tiled=True)  16.8 us
    ppermute x10, starting transfers between devices, swap(): return lax.ppermute(value, 'dp', [(i, i ^ 1) for i in range(devices)])  15.8 us
    ppermute x10, waiting for transfers between devices, swap(): return lax.ppermute(value, 'dp', [(i, i ^ 1) for i in range(devices)])  3.97 us
  transfers between devices with their start and end apart: 29, of which 16 were waited for; matrix products, arithmetic and copies ran while one was open for 1% of the time, Pallas kernels for 22%

profile of v5, /device:TPU:1, one launch (start us, length us, event | category | flops | bytes accessed | tf_op | source)
XLA Modules:
  0.0 153.2 jit_solution(14338158319013158710)
XLA Ops:
  0.6 3.3 %collective-permute-start.4 = (bf16[256,512]{1,0:T(8,128)(2,1)}, bf16[256,512]{1,0:T(8,128)(2,1)S(1)}, u32[]{:S(2)}, u32[]{:S(2)}) collective-permute-start(bf16[256,512]{1,0:T(8,128)(2,1)} %tokens_hbm.1), channel_id=1, source_target_pairs={{0,32},{32,0},{64,96},{96,64},{128,160},{160,128},{192,224},{224,1... | collective-permute-start | bytes 786440 | tf_op jit(solution)/shard_map/ppermute | solution.py:411
  4.0 1.8 %shard_map.119 = (bf16[512,512]{1,0:T(8,128)(2,1)S(1)}, bf16[512,256]{1,0:T(8,128)(2,1)S(1)}) custom-call(s32[2]{0:T(128)S(1)} %pad_add_fusion.ids, s32[16,64]{1,0:T(8,128)} %bitcast.33, bf16[256,512]{1,0:T(8,128)(2,1)} %tokens_hbm.1), custom_call_target="tpu_custom_call" | custom-call | flops 134217728 | bytes 1052672 | tf_op jit(solution)/shard_map/pallas_call | solution.py:44
  5.9 1.6 %shard_map.120 = bf16[512,1024]{1,0:T(8,128)(2,1)} custom-call(s32[2]{0:T(128)S(1)} %pad_add_fusion.ids, bf16[512,512]{1,0:T(8,128)(2,1)S(1)} %get-tuple-element.69.half_ref, bf16[512,256]{1,0:T(8,128)(2,1)S(1)} %get-tuple-element.70.picker_ref, bf16[256,512]{1,0:T(8,128)(2,1)S(1)} %collective-permute-done.4.tokens_ref), custom_call_target="tpu_custom_call" | custom-call | flops 134217728 | bytes 2097152 | tf_op jit(solution)/shard_map/pallas_call | solution.py:44
  7.5 9.7 %all-to-all-start.1 = ((bf16[32,16,1024]{2,1,0:T(8,128)(2,1)}), bf16[32,16,1024]{2,1,0:T(8,128)(2,1)}, u32[]{:S(2)}, u32[]{:S(2)}) async-start(bf16[32,16,1024]{2,1,0:T(8,128)(2,1)} %bitcast.40), calls=%async_computation.1 | async-start | bytes 2097152 | tf_op jit(solution)/shard_map/all_to_all | solution.py:424
  17.8 0.9 copy-done.11
  20.2 2.5 %collective-permute-done.other_ref.other_hbm = bf16[256,512]{1,0:T(8,128)(2,1)S(1)} collective-permute-done((bf16[256,512]{1,0:T(8,128)(2,1)S(1)}, bf16[256,512]{1,0:T(8,128)(2,1)S(1)}, u32[]{:S(2)}, u32[]{:S(2)}) %collective-permute-start) | collective-permute-done | bytes 262176 | tf_op jit(solution)/shard_map/ppermute | solution.py:411
  22.7 2.0 %shard_map.118 = bf16[512,1024]{1,0:T(8,128)(2,1)} custom-call(s32[2]{0:T(128)S(1)} %pad_add_fusion.ids, s32[16,64]{1,0:T(8,128)S(1)} %bitcast.34, bf16[16,64]{1,0:T(8,128)(2,1)S(1)} %bitcast.38, bf16[256,512]{1,0:T(8,128)(2,1)S(1)} %copy-done.5, bf16[256,512]{1,0:T(8,128)(2,1)S(1)} %collective-permute-done.other_ref.other_hbm), custom_call_target="tpu_custom_call" | custom-call | flops 268435456 | bytes 1579008 | tf_op jit(solution)/shard_map/pallas_call | solution.py:44
  24.8 0.9 copy-done.1
  25.9 16.8 %all-to-all-done.1 = bf16[32,16,1024]{2,1,0:T(8,128)(2,1)} async-done(((bf16[32,16,1024]{2,1,0:T(8,128)(2,1)}), bf16[32,16,1024]{2,1,0:T(8,128)(2,1)}, u32[]{:S(2)}, u32[]{:S(2)}) %all-to-all-start.1) | async-done | bytes 1048608 | tf_op jit(solution)/shard_map/all_to_all | solution.py:424
  42.6 8.1 %all-to-all-start = ((bf16[32,16,1024]{2,1,0:T(8,128)(2,1)}), bf16[32,16,1024]{2,1,0:T(8,128)(2,1)}, u32[]{:S(2)}, u32[]{:S(2)}) async-start(bf16[32,16,1024]{2,1,0:T(8,128)(2,1)} %bitcast.41), calls=%async_computation | async-start | bytes 2097152 | tf_op jit(solution)/shard_map/all_to_all | solution.py:424
  50.8 3.8 %shard_map.121 = (bf16[256,1024]{1,0:T(8,128)(2,1)}, bf16[256,512]{1,0:T(8,128)(2,1)}, bf16[512,256]{1,0:T(8,128)(2,1)S(1)}, f32[64,1536]{1,0:T(8,128)S(1)}, bf1...) custom-call(s32[2]{0:T(128)S(1)} %pad_add_fusion.ids, ...), custom_call_target="tpu_custom_call" | custom-call | flops 1073741824 | bytes 6225920 | tf_op jit(solution)/shard_map/pallas_call | solution.py:44
  54.6 1.3 collective-permute-start.8
  55.8 2.5 %collective-permute-start.9 = (bf16[64,1536]{1,0:T(8,128)(2,1)S(1)}, bf16[64,1536]{1,0:T(8,128)(2,1)S(1)}, u32[]{:S(2)}, u32[]{:S(2)}) collective-permute-start(bf16[64,1536]{1,0:T(8,128)(2,1)S(1)} %get-tuple-element.83), channel_id=1, source_target_pairs={{0,128},{32,160},{64,192},{96,224},{128,0},{160,32},{192,64},{224,... | collective-permute-start | bytes 589832 | tf_op jit(solution)/shard_map/ppermute | solution.py:414
  58.3 1.2 collective-permute-start.10
  59.4 1.7 %collective-permute-done.8.r1 = bf16[64,1536]{1,0:T(8,128)(2,1)S(1)} collective-permute-done((bf16[64,1536]{1,0:T(8,128)(2,1)S(1)}, bf16[64,1536]{1,0:T(8,128)(2,1)S(1)}, u32[]{:S(2)}, u32[]{:S(2)}) %collective-permute-start.8) | collective-permute-done | bytes 196640 | tf_op jit(solution)/shard_map/ppermute | solution.py:414
  61.1 5.2 %collective-permute-done.9.r2 = bf16[64,1536]{1,0:T(8,128)(2,1)S(1)} collective-permute-done((bf16[64,1536]{1,0:T(8,128)(2,1)S(1)}, bf16[64,1536]{1,0:T(8,128)(2,1)S(1)}, u32[]{:S(2)}, u32[]{:S(2)}) %collective-permute-start.9) | collective-permute-done | bytes 196640 | tf_op jit(solution)/shard_map/ppermute | solution.py:414
  67.0 2.8 %collective-permute-start.13 = (bf16[64,768]{1,0:T(8,128)(2,1)S(1)}, bf16[64,768]{1,0:T(8,128)(2,1)S(1)}, u32[]{:S(2)}, u32[]{:S(2)}) collective-permute-start(bf16[64,768]{1,0:T(8,128)(2,1)S(1)} %get-tuple-element.85.h0), channel_id=1, source_target_pairs={{0,192},{32,224},{64,0},{96,32},{128,64},{160,96},{192,128},{224,1... | collective-permute-start | bytes 294920 | tf_op jit(solution)/shard_map/ppermute | solution.py:414
  69.7 1.1 collective-permute-start.12
  70.8 1.6 %collective-permute-done.13.h3 = bf16[64,768]{1,0:T(8,128)(2,1)S(1)} collective-permute-done((bf16[64,768]{1,0:T(8,128)(2,1)S(1)}, bf16[64,768]{1,0:T(8,128)(2,1)S(1)}, u32[]{:S(2)}, u32[]{:S(2)}) %collective-permute-start.13) | collective-permute-done | bytes 98336 | tf_op jit(solution)/shard_map/ppermute | solution.py:414
  72.4 2.8 %collective-permute-done.12.h2 = bf16[64,768]{1,0:T(8,128)(2,1)S(1)} collective-permute-done((bf16[64,768]{1,0:T(8,128)(2,1)S(1)}, bf16[64,768]{1,0:T(8,128)(2,1)S(1)}, u32[]{:S(2)}, u32[]{:S(2)}) %collective-permute-start.12) | collective-permute-done | bytes 98336 | tf_op jit(solution)/shard_map/ppermute | solution.py:414
  75.1 1.1 collective-permute-done.11.h1
  76.2 2.3 %shard_map.124 = (bf16[256,768]{1,0:T(8,128)(2,1)}, bf16[512,1024]{1,0:T(8,128)(2,1)}, bf16[512,256]{1,0:T(8,128)(2,1)}, f32[64,1536]{1,0:T(8,128)}) custom-call(s32[2]{0:T(128)S(1)} %pad_add_fusion.ids, bf16[64,768]{1,0:T(8,128)(2,1)S(1)} %get-tuple-element.85.h0, bf16[64,768]{1,0:T(8,128)(2,1)S(1)} %collective-permute-done.11.h1, ...), custom_call_target="tpu_custom_call" | custom-call | flops 671088640 | bytes 4718592 | tf_op jit(solution)/shard_map/pallas_call | solution.py:44
  78.5 8.7 %all-to-all-start.3 = ((bf16[32,16,1024]{2,1,0:T(8,128)(2,1)}), bf16[32,16,1024]{2,1,0:T(8,128)(2,1)S(1)}, u32[]{:S(2)}, u32[]{:S(2)}) async-start(bf16[32,16,1024]{2,1,0:T(8,128)(2,1)} %bitcast.44), calls=%async_computation.3 | async-start | bytes 2097152 | tf_op jit(solution)/shard_map/all_to_all | solution.py:424
  87.2 3.3 %shard_map.122 = (bf16[256,1024]{1,0:T(8,128)(2,1)}, f32[64,768]{1,0:T(8,128)S(1)}, bf16[64,768]{1,0:T(8,128)(2,1)S(1)}, bf16[64,768]{1,0:T(8,128)(2,1)S(1)}, bf16[64,768]{1,0:T(8,128)(2,1)S(1)}) custom-call(s32[2]{0:T(128)S(1)} %pad_add_fusion.ids, bf16[512,1024]{1,0:T(8,128)(2,1)} %bitcast.13.got_hbm, bf16[256,512]{1,0:T(8,128)(2,1)} %get-tuple-element.74.narrow_hbm, ...), custom_call_target="tpu_custom_call" | custom-call | flops 671088640 | bytes 3899392 | tf_op jit(solution)/shard_map/pallas_call | solution.py:44
  91.0 1.6 %collective-permute-start.6 = (bf16[64,768]{1,0:T(8,128)(2,1)S(1)}, bf16[64,768]{1,0:T(8,128)(2,1)S(1)}, u32[]{:S(2)}, u32[]{:S(2)}) collective-permute-start(bf16[64,768]{1,0:T(8,128)(2,1)S(1)} %get-tuple-element.79), channel_id=1, source_target_pairs={{0,128},{32,160},{64,192},{96,224},{128,0},{160,32},{192,64},{224,... | collective-permute-start | bytes 294920 | tf_op jit(solution)/shard_map/ppermute | solution.py:414
  92.6 2.0 %collective-permute-start.7 = (bf16[64,768]{1,0:T(8,128)(2,1)S(1)}, bf16[64,768]{1,0:T(8,128)(2,1)S(1)}, u32[]{:S(2)}, u32[]{:S(2)}) collective-permute-start(bf16[64,768]{1,0:T(8,128)(2,1)S(1)} %get-tuple-element.80), channel_id=1, source_target_pairs={{0,192},{32,224},{64,0},{96,32},{128,64},{160,96},{192,128},{224,1... | collective-permute-start | bytes 294920 | tf_op jit(solution)/shard_map/ppermute | solution.py:414
  94.5 2.0 %collective-permute-done.5.r1 = bf16[64,768]{1,0:T(8,128)(2,1)S(1)} collective-permute-done((bf16[64,768]{1,0:T(8,128)(2,1)S(1)}, bf16[64,768]{1,0:T(8,128)(2,1)S(1)}, u32[]{:S(2)}, u32[]{:S(2)}) %collective-permute-start.5) | collective-permute-done | bytes 98336 | tf_op jit(solution)/shard_map/ppermute | solution.py:414
  97.6 2.8 %collective-permute-start.16 = (bf16[64,1536]{1,0:T(8,128)(2,1)S(1)}, bf16[64,1536]{1,0:T(8,128)(2,1)S(1)}, u32[]{:S(2)}, u32[]{:S(2)}) collective-permute-start(bf16[64,1536]{1,0:T(8,128)(2,1)S(1)} %shard_map.125.g0), channel_id=1, source_target_pairs={{0,192},{32,224},{64,0},{96,32},{128,64},{160,96},{192,128},{224,1... | collective-permute-start | bytes 589832 | tf_op jit(solution)/shard_map/ppermute | solution.py:414
  101.0 1.7 %shard_map.126.wo_u_ref = bf16[512,768]{1,0:T(8,128)(2,1)S(1)} custom-call(s32[2]{0:T(128)S(1)} %pad_add_fusion.ids, bf16[512,768]{1,0:T(8,128)(2,1)} %copy-done.9), custom_call_target="tpu_custom_call" | custom-call | bytes 1572864 | tf_op jit(solution)/shard_map/pallas_call | solution.py:44
  102.7 2.3 %collective-permute-done.16.g3 = bf16[64,1536]{1,0:T(8,128)(2,1)S(1)} collective-permute-done((bf16[64,1536]{1,0:T(8,128)(2,1)S(1)}, bf16[64,1536]{1,0:T(8,128)(2,1)S(1)}, u32[]{:S(2)}, u32[]{:S(2)}) %collective-permute-start.16) | collective-permute-done | bytes 196640 | tf_op jit(solution)/shard_map/ppermute | solution.py:414
  105.1 1.6 %collective-permute-done.15.g2 = bf16[64,1536]{1,0:T(8,128)(2,1)S(1)} collective-permute-done((bf16[64,1536]{1,0:T(8,128)(2,1)S(1)}, bf16[64,1536]{1,0:T(8,128)(2,1)S(1)}, u32[]{:S(2)}, u32[]{:S(2)}) %collective-permute-start.15) | collective-permute-done | bytes 196640 | tf_op jit(solution)/shard_map/ppermute | solution.py:414
  106.7 2.1 %collective-permute-done.14.g1 = bf16[64,1536]{1,0:T(8,128)(2,1)S(1)} collective-permute-done((bf16[64,1536]{1,0:T(8,128)(2,1)S(1)}, bf16[64,1536]{1,0:T(8,128)(2,1)S(1)}, u32[]{:S(2)}, u32[]{:S(2)}) %collective-permute-start.14) | collective-permute-done | bytes 196640 | tf_op jit(solution)/shard_map/ppermute | solution.py:414
  108.8 3.1 %shard_map.127 = (bf16[256,1536]{1,0:T(8,128)(2,1)}, bf16[512,1024]{1,0:T(8,128)(2,1)}) custom-call(s32[2]{0:T(128)S(1)} %pad_add_fusion.ids, bf16[64,1536]{1,0:T(8,128)(2,1)S(1)} %shard_map.125.g0, bf16[64,1536]{1,0:T(8,128)(2,1)S(1)} %collective-permute-done.14.g1, bf16[64,1536]{1,0:T(8,128)(2,1)S(1)} %collective-permute-done.15.g2, ...), custom_call_target="tpu_custom_call" | custom-call | flops 1073741824 | bytes 6029312 | tf_op jit(solution)/shard_map/pallas_call | solution.py:44
  111.9 9.2 %all-to-all-start.2 = ((bf16[32,16,1024]{2,1,0:T(8,128)(2,1)}), bf16[32,16,1024]{2,1,0:T(8,128)(2,1)S(1)}, u32[]{:S(2)}, u32[]{:S(2)}) async-start(bf16[32,16,1024]{2,1,0:T(8,128)(2,1)} %bitcast.42), calls=%async_computation.2 | async-start | bytes 2097152 | tf_op jit(solution)/shard_map/all_to_all | solution.py:424
  121.2 3.0 %shard_map.128 = (f32[256,512]{1,0:T(8,128)}, f32[256,512]{1,0:T(8,128)S(1)}, f32[32,16]{1,0:T(8,128)S(1)}) custom-call(s32[2]{0:T(128)S(1)} %pad_add_fusion.ids, bf16[512,1024]{1,0:T(8,128)(2,1)} %bitcast.43, bf16[256,512]{1,0:T(8,128)(2,1)} %own_hbm.1, bf16[256,512]{1,0:T(8,128)(2,1)} %copy-done.6, s32[16,64]{1,0:T(8,128)S(1)} %bitcast.35, ...), custom_call_target="tpu_custom_call" | custom-call | flops 536870912 | bytes 2629632 | tf_op jit(solution)/shard_map/pallas_call | solution.py:44
  124.2 2.8 %shard_map.131 = (bf16[512,1536]{1,0:T(8,128)(2,1)S(1)}, bf16[768,512]{1,0:T(8,128)(2,1)S(1)}) custom-call(s32[2]{0:T(128)S(1)} %pad_add_fusion.ids, bf16[256,1024]{1,0:T(8,128)(2,1)} %get-tuple-element.103.rows_in_hbm, bf16[256,1536]{1,0:T(8,128)(2,1)} %get-tuple-element.104.grads_hbm, bf16[256,768]{1,0:T(8,128)(2,1)} %get-tuple-element.105.hidden_hbm, ...), custom_call_target="tpu_custom_call" | custom-call | flops 603979776 | bytes 4587520 | tf_op jit(solution)/shard_map/pallas_call | solution.py:44
  127.0 6.2 %collective-permute-start.22 = (bf16[512,1536]{1,0:T(8,128)(2,1)S(1)}, bf16[512,1536]{1,0:T(8,128)(2,1)S(1)}, u32[]{:S(2)}, u32[]{:S(2)}) collective-permute-start(bf16[512,1536]{1,0:T(8,128)(2,1)S(1)} %get-tuple-element.114), channel_id=1, source_target_pairs={{0,32},{32,0},{64,96},{96,64},{128,160},{160,128},{192,224},{224,1... | collective-permute-start | bytes 4718600 | tf_op jit(solution)/shard_map/ppermute | solution.py:411
  134.4 2.2 %collective-permute-done.20 = f32[32,16]{1,0:T(8,128)S(1)} collective-permute-done((f32[32,16]{1,0:T(8,128)S(1)}, f32[32,16]{1,0:T(8,128)S(1)}, u32[]{:S(2)}, u32[]{:S(2)}) %collective-permute-start.20) | collective-permute-done | bytes 2080 | tf_op jit(solution)/shard_map/ppermute | solution.py:414
  136.6 3.8 %shard_map.129 = (bf16[2,512,768]{2,1,0:T(8,128)(2,1)}, bf16[2,512,768]{2,1,0:T(8,128)(2,1)}, bf16[2,768,512]{2,1,0:T(8,128)(2,1)}) custom-call(s32[2]{0:T(128)S(1)} %pad_add_fusion.ids, bf16[256,1024]{1,0:T(8,128)(2,1)} %get-tuple-element.103.rows_in_hbm, bf16[256,1536]{1,0:T(8,128)(2,1)} %get-tuple-element.104.grads_hbm, ...), custom_call_target="tpu_custom_call" | custom-call | flops 603979776 | bytes 6946816 | tf_op jit(solution)/shard_map/pallas_call | solution.py:44
  140.8 1.9 %collective-permute-start.21 = (bf16[32,16]{1,0:T(8,128)(2,1)S(1)}, bf16[32,16]{1,0:T(8,128)(2,1)S(1)}, u32[]{:S(2)}, u32[]{:S(2)}) collective-permute-start(bf16[32,16]{1,0:T(8,128)(2,1)S(1)} %add_convert_fusion.2.mine_ref), channel_id=1, source_target_pairs={{0,32},{32,0},{64,96},{96,64},{128,160},{160,128},{192,224},{224,1... | collective-permute-start | bytes 3080 | tf_op jit(solution)/shard_map/ppermute | solution.py:411
  142.6 0.8 collective-permute-done.21.other_ref
  143.5 1.3 shard_map.130
  144.8 0.8 add_convert_fusion.1
  145.5 2.0 %shard_map.132 = (bf16[2,512,768]{2,1,0:T(8,128)(2,1)}, bf16[2,512,768]{2,1,0:T(8,128)(2,1)}, bf16[2,768,512]{2,1,0:T(8,128)(2,1)}) custom-call(s32[2]{0:T(128)S(1)} %pad_add_fusion.ids, bf16[512,1536]{1,0:T(8,128)(2,1)S(1)} %collective-permute-done.22.got_in_ref, ...), custom_call_target="tpu_custom_call", output_to_operand_aliasing={{0}: (3, {}), {1}: (4, {}), {2}: (5, {})} | custom-call | bytes 11796480 | tf_op jit(solution)/shard_map/pallas_call | solution.py:44
  147.5 0.9 shard_map.134
  148.5 2.4 %collective-permute-start.24 = (f32[256,512]{1,0:T(8,128)S(1)}, f32[256,512]{1,0:T(8,128)S(1)}, u32[]{:S(2)}, u32[]{:S(2)}) collective-permute-start(f32[256,512]{1,0:T(8,128)S(1)} %shard_map.134), channel_id=1, source_target_pairs={{0,32},{32,0},{64,96},{96,64},{128,160},{160,128},{192,224},{224,1... | collective-permute-start | bytes 1572872 | tf_op jit(solution)/shard_map/ppermute | solution.py:411
  150.9 0.9 shard_map.133
  152.5 0.8 add_convert_fusion
  (64 shorter events, 7.2 us)
Async XLA Ops:
  0.6 5.2 %collective-permute-start.4 = (bf16[256,512]{1,0:T(8,128)(2,1)}, bf16[256,512]{1,0:T(8,128)(2,1)S(1)}, u32[]{:S(2)}, u32[]{:S(2)}) collective-permute-start(bf16[256,512]{1,0:T(8,128)(2,1)} %tokens_hbm.1), channel_id=1, source_target_pairs={{0,32},{32,0},{64,96},{96,64},{128,160},{160,128},{192,224},{224,1... | collective-permute-start | bytes 786440 | tf_op jit(solution)/shard_map/ppermute | solution.py:411
  7.5 9.8 %copy-start.10 = (bf16[2,512,768]{2,1,0:T(8,128)(2,1)S(1)}, bf16[2,512,768]{2,1,0:T(8,128)(2,1)}, u32[]{:S(2)}) copy-start(bf16[2,512,768]{2,1,0:T(8,128)(2,1)} %param.11) | copy-start | bytes 4718596
  7.5 35.2 %all-to-all-start.1 = ((bf16[32,16,1024]{2,1,0:T(8,128)(2,1)}), bf16[32,16,1024]{2,1,0:T(8,128)(2,1)}, u32[]{:S(2)}, u32[]{:S(2)}) async-start(bf16[32,16,1024]{2,1,0:T(8,128)(2,1)} %bitcast.40), calls=%async_computation.1 | async-start | bytes 2097152 | tf_op jit(solution)/shard_map/all_to_all | solution.py:424
  17.3 1.4 copy-start.11
  17.4 1.8 %copy-start.12 = (bf16[2,768,512]{2,1,0:T(8,128)(2,1)S(1)}, bf16[2,768,512]{2,1,0:T(8,128)(2,1)}, u32[]{:S(2)}) copy-start(bf16[2,768,512]{2,1,0:T(8,128)(2,1)} %param.13) | copy-start | bytes 4718596
  17.4 7.3 %collective-permute-start.1 = (bf16[512,768]{1,0:T(8,128)(2,1)S(1)}, bf16[512,768]{1,0:T(8,128)(2,1)S(1)}, u32[]{:S(2)}, u32[]{:S(2)}) collective-permute-start(bf16[512,768]{1,0:T(8,128)(2,1)S(1)} %get-tuple-element.132), channel_id=1, source_target_pairs={{0,32},{32,0},{64,96},{96,64},{128,160},{160,128},{192,224},{224,1... | collective-permute-start | bytes 2359304 | tf_op jit(solution)/shard_map/ppermute | solution.py:411
  18.8 1.1 copy-start.5
  18.8 3.9 %copy-start.7 = (s32[1,64,16]{1,2,0:T(8,128)S(1)}, s32[1,64,16]{1,2,0:T(8,128)}, u32[]{:S(2)}) copy-start(s32[1,64,16]{1,2,0:T(8,128)} %param.9) | copy-start | bytes 12292
  18.8 3.9 %copy-start.8 = (bf16[1,64,16]{1,2,0:T(8,128)(2,1)S(1)}, bf16[1,64,16]{1,2,0:T(8,128)(2,1)}, u32[]{:S(2)}) copy-start(bf16[1,64,16]{1,2,0:T(8,128)(2,1)} %param.10) | copy-start | bytes 6148
  18.8 5.9 %collective-permute-start.2 = (bf16[512,768]{1,0:T(8,128)(2,1)S(1)}, bf16[512,768]{1,0:T(8,128)(2,1)S(1)}, u32[]{:S(2)}, u32[]{:S(2)}) collective-permute-start(bf16[512,768]{1,0:T(8,128)(2,1)S(1)} %get-tuple-element.130), channel_id=1, source_target_pairs={{0,32},{32,0},{64,96},{96,64},{128,160},{160,128},{192,224},{224,1... | collective-permute-start | bytes 2359304 | tf_op jit(solution)/shard_map/ppermute | solution.py:411
  19.3 56.8 %copy-start = (bf16[768,512]{1,0:T(8,128)(2,1)}, bf16[768,512]{1,0:T(8,128)(2,1)S(1)}, u32[]{:S(2)}) copy-start(bf16[768,512]{1,0:T(8,128)(2,1)S(1)} %get-tuple-element.75.wd_hbm.wd_ref) | copy-start | bytes 2359300
  19.3 5.4 %collective-permute-start.3 = (bf16[768,512]{1,0:T(8,128)(2,1)S(1)}, bf16[768,512]{1,0:T(8,128)(2,1)S(1)}, u32[]{:S(2)}, u32[]{:S(2)}) collective-permute-start(bf16[768,512]{1,0:T(8,128)(2,1)S(1)} %get-tuple-element.128), channel_id=1, source_target_pairs={{0,32},{32,0},{64,96},{96,64},{128,160},{160,128},{192,224},{224,1... | collective-permute-start | bytes 2359304 | tf_op jit(solution)/shard_map/ppermute | solution.py:411
  19.8 2.9 %collective-permute-start = (bf16[256,512]{1,0:T(8,128)(2,1)S(1)}, bf16[256,512]{1,0:T(8,128)(2,1)S(1)}, u32[]{:S(2)}, u32[]{:S(2)}) collective-permute-start(bf16[256,512]{1,0:T(8,128)(2,1)S(1)} %copy-done.5), channel_id=1, source_target_pairs={{0,32},{32,0},{64,96},{96,64},{128,160},{160,128},{192,224},{224,1... | collective-permute-start | bytes 786440 | tf_op jit(solution)/shard_map/ppermute | solution.py:411
  22.7 2.1 %copy-start.6 = (bf16[256,512]{1,0:T(8,128)(2,1)}, bf16[256,512]{1,0:T(8,128)(2,1)S(1)}, u32[]{:S(2)}) copy-start(bf16[256,512]{1,0:T(8,128)(2,1)S(1)} %collective-permute-done.other_ref.other_hbm) | copy-start | bytes 786436
  24.8 1.1 copy-start.9
  24.8 0.9 copy-start.1
  42.6 35.8 %all-to-all-start = ((bf16[32,16,1024]{2,1,0:T(8,128)(2,1)}), bf16[32,16,1024]{2,1,0:T(8,128)(2,1)}, u32[]{:S(2)}, u32[]{:S(2)}) async-start(bf16[32,16,1024]{2,1,0:T(8,128)(2,1)} %bitcast.41), calls=%async_computation | async-start | bytes 2097152 | tf_op jit(solution)/shard_map/all_to_all | solution.py:424
  50.8 25.4 %copy-start.2 = (bf16[768,512]{1,0:T(8,128)(2,1)S(1)}, bf16[768,512]{1,0:T(8,128)(2,1)}, u32[]{:S(2)}) copy-start(bf16[768,512]{1,0:T(8,128)(2,1)} %copy-done.1) | copy-start | bytes 2359300
  54.6 6.5 %collective-permute-start.8 = (bf16[64,1536]{1,0:T(8,128)(2,1)S(1)}, bf16[64,1536]{1,0:T(8,128)(2,1)S(1)}, u32[]{:S(2)}, u32[]{:S(2)}) collective-permute-start(bf16[64,1536]{1,0:T(8,128)(2,1)S(1)} %get-tuple-element.82), channel_id=1, source_target_pairs={{0,64},{32,96},{64,128},{96,160},{128,192},{160,224},{192,0},{224,... | collective-permute-start | bytes 589832 | tf_op jit(solution)/shard_map/ppermute | solution.py:414
  55.8 10.5 %collective-permute-start.9 = (bf16[64,1536]{1,0:T(8,128)(2,1)S(1)}, bf16[64,1536]{1,0:T(8,128)(2,1)S(1)}, u32[]{:S(2)}, u32[]{:S(2)}) collective-permute-start(bf16[64,1536]{1,0:T(8,128)(2,1)S(1)} %get-tuple-element.83), channel_id=1, source_target_pairs={{0,128},{32,160},{64,192},{96,224},{128,0},{160,32},{192,64},{224,... | collective-permute-start | bytes 589832 | tf_op jit(solution)/shard_map/ppermute | solution.py:414
  58.3 8.0 %collective-permute-start.10 = (bf16[64,1536]{1,0:T(8,128)(2,1)S(1)}, bf16[64,1536]{1,0:T(8,128)(2,1)S(1)}, u32[]{:S(2)}, u32[]{:S(2)}) collective-permute-start(bf16[64,1536]{1,0:T(8,128)(2,1)S(1)} %get-tuple-element.84), channel_id=1, source_target_pairs={{0,192},{32,224},{64,0},{96,32},{128,64},{160,96},{192,128},{224,1... | collective-permute-start | bytes 589832 | tf_op jit(solution)/shard_map/ppermute | solution.py:414
  67.0 5.4 %collective-permute-start.13 = (bf16[64,768]{1,0:T(8,128)(2,1)S(1)}, bf16[64,768]{1,0:T(8,128)(2,1)S(1)}, u32[]{:S(2)}, u32[]{:S(2)}) collective-permute-start(bf16[64,768]{1,0:T(8,128)(2,1)S(1)} %get-tuple-element.85.h0), channel_id=1, source_target_pairs={{0,192},{32,224},{64,0},{96,32},{128,64},{160,96},{192,128},{224,1... | collective-permute-start | bytes 294920 | tf_op jit(solution)/shard_map/ppermute | solution.py:414
  69.7 5.4 %collective-permute-start.12 = (bf16[64,768]{1,0:T(8,128)(2,1)S(1)}, bf16[64,768]{1,0:T(8,128)(2,1)S(1)}, u32[]{:S(2)}, u32[]{:S(2)}) collective-permute-start(bf16[64,768]{1,0:T(8,128)(2,1)S(1)} %get-tuple-element.85.h0), channel_id=1, source_target_pairs={{0,128},{32,160},{64,192},{96,224},{128,0},{160,32},{192,64},{224,... | collective-permute-start | bytes 294920 | tf_op jit(solution)/shard_map/ppermute | solution.py:414
  70.8 5.4 %collective-permute-start.11 = (bf16[64,768]{1,0:T(8,128)(2,1)S(1)}, bf16[64,768]{1,0:T(8,128)(2,1)S(1)}, u32[]{:S(2)}, u32[]{:S(2)}) collective-permute-start(bf16[64,768]{1,0:T(8,128)(2,1)S(1)} %get-tuple-element.85.h0), channel_id=1, source_target_pairs={{0,64},{32,96},{64,128},{96,160},{128,192},{160,224},{192,0},{224,... | collective-permute-start | bytes 294920 | tf_op jit(solution)/shard_map/ppermute | solution.py:414
  78.5 33.4 %all-to-all-start.3 = ((bf16[32,16,1024]{2,1,0:T(8,128)(2,1)}), bf16[32,16,1024]{2,1,0:T(8,128)(2,1)S(1)}, u32[]{:S(2)}, u32[]{:S(2)}) async-start(bf16[32,16,1024]{2,1,0:T(8,128)(2,1)} %bitcast.44), calls=%async_computation.3 | async-start | bytes 2097152 | tf_op jit(solution)/shard_map/all_to_all | solution.py:424
  87.2 9.7 %copy-start.3 = (f32[64,1536]{1,0:T(8,128)S(1)}, f32[64,1536]{1,0:T(8,128)}, u32[]{:S(2)}) copy-start(f32[64,1536]{1,0:T(8,128)} %get-tuple-element.88.pre_ref) | copy-start | bytes 1179652
  90.5 18.3 %copy-start.4 = (bf16[512,256]{1,0:T(8,128)(2,1)S(1)}, bf16[512,256]{1,0:T(8,128)(2,1)}, u32[]{:S(2)}) copy-start(bf16[512,256]{1,0:T(8,128)(2,1)} %get-tuple-element.91.widen_ref) | copy-start | bytes 786436
  90.5 6.0 %collective-permute-start.5 = (bf16[64,768]{1,0:T(8,128)(2,1)S(1)}, bf16[64,768]{1,0:T(8,128)(2,1)S(1)}, u32[]{:S(2)}, u32[]{:S(2)}) collective-permute-start(bf16[64,768]{1,0:T(8,128)(2,1)S(1)} %get-tuple-element.78), channel_id=1, source_target_pairs={{0,64},{32,96},{64,128},{96,160},{128,192},{160,224},{192,0},{224,... | collective-permute-start | bytes 294920 | tf_op jit(solution)/shard_map/ppermute | solution.py:414
  91.0 5.5 %collective-permute-start.6 = (bf16[64,768]{1,0:T(8,128)(2,1)S(1)}, bf16[64,768]{1,0:T(8,128)(2,1)S(1)}, u32[]{:S(2)}, u32[]{:S(2)}) collective-permute-start(bf16[64,768]{1,0:T(8,128)(2,1)S(1)} %get-tuple-element.79), channel_id=1, source_target_pairs={{0,128},{32,160},{64,192},{96,224},{128,0},{160,32},{192,64},{224,... | collective-permute-start | bytes 294920 | tf_op jit(solution)/shard_map/ppermute | solution.py:414
  92.6 4.3 %collective-permute-start.7 = (bf16[64,768]{1,0:T(8,128)(2,1)S(1)}, bf16[64,768]{1,0:T(8,128)(2,1)S(1)}, u32[]{:S(2)}, u32[]{:S(2)}) collective-permute-start(bf16[64,768]{1,0:T(8,128)(2,1)S(1)} %get-tuple-element.80), channel_id=1, source_target_pairs={{0,192},{32,224},{64,0},{96,32},{128,64},{160,96},{192,128},{224,1... | collective-permute-start | bytes 294920 | tf_op jit(solution)/shard_map/ppermute | solution.py:414
  97.6 7.5 %collective-permute-start.16 = (bf16[64,1536]{1,0:T(8,128)(2,1)S(1)}, bf16[64,1536]{1,0:T(8,128)(2,1)S(1)}, u32[]{:S(2)}, u32[]{:S(2)}) collective-permute-start(bf16[64,1536]{1,0:T(8,128)(2,1)S(1)} %shard_map.125.g0), channel_id=1, source_target_pairs={{0,192},{32,224},{64,0},{96,32},{128,64},{160,96},{192,128},{224,1... | collective-permute-start | bytes 589832 | tf_op jit(solution)/shard_map/ppermute | solution.py:414
  100.3 6.3 %collective-permute-start.15 = (bf16[64,1536]{1,0:T(8,128)(2,1)S(1)}, bf16[64,1536]{1,0:T(8,128)(2,1)S(1)}, u32[]{:S(2)}, u32[]{:S(2)}) collective-permute-start(bf16[64,1536]{1,0:T(8,128)(2,1)S(1)} %shard_map.125.g0), channel_id=1, source_target_pairs={{0,128},{32,160},{64,192},{96,224},{128,0},{160,32},{192,64},{224,... | collective-permute-start | bytes 589832 | tf_op jit(solution)/shard_map/ppermute | solution.py:414
  101.0 7.7 %collective-permute-start.14 = (bf16[64,1536]{1,0:T(8,128)(2,1)S(1)}, bf16[64,1536]{1,0:T(8,128)(2,1)S(1)}, u32[]{:S(2)}, u32[]{:S(2)}) collective-permute-start(bf16[64,1536]{1,0:T(8,128)(2,1)S(1)} %shard_map.125.g0), channel_id=1, source_target_pairs={{0,64},{32,96},{64,128},{96,160},{128,192},{160,224},{192,0},{224,... | collective-permute-start | bytes 589832 | tf_op jit(solution)/shard_map/ppermute | solution.py:414
  111.9 9.3 %copy-start.13 = (bf16[32,16,1024]{2,1,0:T(8,128)(2,1)}, bf16[32,16,1024]{2,1,0:T(8,128)(2,1)S(1)}, u32[]{:S(2)}) copy-start(bf16[32,16,1024]{2,1,0:T(8,128)(2,1)S(1)} %all-to-all-done.3) | copy-start | bytes 3145732
  111.9 35.6 %all-to-all-start.2 = ((bf16[32,16,1024]{2,1,0:T(8,128)(2,1)}), bf16[32,16,1024]{2,1,0:T(8,128)(2,1)S(1)}, u32[]{:S(2)}, u32[]{:S(2)}) async-start(bf16[32,16,1024]{2,1,0:T(8,128)(2,1)} %bitcast.42), calls=%async_computation.2 | async-start | bytes 2097152 | tf_op jit(solution)/shard_map/all_to_all | solution.py:424
  127.0 17.8 %copy-start.14 = (f32[256,512]{1,0:T(8,128)S(1)}, f32[256,512]{1,0:T(8,128)}, u32[]{:S(2)}) copy-start(f32[256,512]{1,0:T(8,128)} %get-tuple-element.94) | copy-start | bytes 1572868
  127.0 18.5 %collective-permute-start.22 = (bf16[512,1536]{1,0:T(8,128)(2,1)S(1)}, bf16[512,1536]{1,0:T(8,128)(2,1)S(1)}, u32[]{:S(2)}, u32[]{:S(2)}) collective-permute-start(bf16[512,1536]{1,0:T(8,128)(2,1)S(1)} %get-tuple-element.114), channel_id=1, source_target_pairs={{0,32},{32,0},{64,96},{96,64},{128,160},{160,128},{192,224},{224,1... | collective-permute-start | bytes 4718600 | tf_op jit(solution)/shard_map/ppermute | solution.py:411
  133.2 12.3 %collective-permute-start.23 = (bf16[768,512]{1,0:T(8,128)(2,1)S(1)}, bf16[768,512]{1,0:T(8,128)(2,1)S(1)}, u32[]{:S(2)}, u32[]{:S(2)}) collective-permute-start(bf16[768,512]{1,0:T(8,128)(2,1)S(1)} %get-tuple-element.115), channel_id=1, source_target_pairs={{0,32},{32,0},{64,96},{96,64},{128,160},{160,128},{192,224},{224,1... | collective-permute-start | bytes 2359304 | tf_op jit(solution)/shard_map/ppermute | solution.py:411
  133.3 11.4 %collective-permute-start.17 = (f32[256,512]{1,0:T(8,128)S(1)}, f32[256,512]{1,0:T(8,128)S(1)}, u32[]{:S(2)}, u32[]{:S(2)}) collective-permute-start(f32[256,512]{1,0:T(8,128)S(1)} %get-tuple-element.101), channel_id=1, source_target_pairs={{0,32},{32,0},{64,96},{96,64},{128,160},{160,128},{192,224},{224,1... | collective-permute-start | bytes 1572872 | tf_op jit(solution)/shard_map/ppermute | solution.py:411
  133.7 2.9 %collective-permute-start.20 = (f32[32,16]{1,0:T(8,128)S(1)}, f32[32,16]{1,0:T(8,128)S(1)}, u32[]{:S(2)}, u32[]{:S(2)}) collective-permute-start(f32[32,16]{1,0:T(8,128)S(1)} %get-tuple-element.110), channel_id=1, source_target_pairs={{0,192},{32,224},{64,0},{96,32},{128,64},{160,96},{192,128},{224,1... | collective-permute-start | bytes 6152 | tf_op jit(solution)/shard_map/ppermute | solution.py:414
  134.1 6.4 %collective-permute-start.19 = (f32[32,16]{1,0:T(8,128)S(1)}, f32[32,16]{1,0:T(8,128)S(1)}, u32[]{:S(2)}, u32[]{:S(2)}) collective-permute-start(f32[32,16]{1,0:T(8,128)S(1)} %get-tuple-element.110), channel_id=1, source_target_pairs={{0,128},{32,160},{64,192},{96,224},{128,0},{160,32},{192,64},{224,... | collective-permute-start | bytes 6152 | tf_op jit(solution)/shard_map/ppermute | solution.py:414
  136.6 4.1 %collective-permute-start.18 = (f32[32,16]{1,0:T(8,128)S(1)}, f32[32,16]{1,0:T(8,128)S(1)}, u32[]{:S(2)}, u32[]{:S(2)}) collective-permute-start(f32[32,16]{1,0:T(8,128)S(1)} %get-tuple-element.110), channel_id=1, source_target_pairs={{0,64},{32,96},{64,128},{96,160},{128,192},{160,224},{192,0},{224,... | collective-permute-start | bytes 6152 | tf_op jit(solution)/shard_map/ppermute | solution.py:414
  140.8 2.7 %collective-permute-start.21 = (bf16[32,16]{1,0:T(8,128)(2,1)S(1)}, bf16[32,16]{1,0:T(8,128)(2,1)S(1)}, u32[]{:S(2)}, u32[]{:S(2)}) collective-permute-start(bf16[32,16]{1,0:T(8,128)(2,1)S(1)} %add_convert_fusion.2.mine_ref), channel_id=1, source_target_pairs={{0,32},{32,0},{64,96},{96,64},{128,160},{160,128},{192,224},{224,1... | collective-permute-start | bytes 3080 | tf_op jit(solution)/shard_map/ppermute | solution.py:411
  148.5 4.0 %collective-permute-start.24 = (f32[256,512]{1,0:T(8,128)S(1)}, f32[256,512]{1,0:T(8,128)S(1)}, u32[]{:S(2)}, u32[]{:S(2)}) collective-permute-start(f32[256,512]{1,0:T(8,128)S(1)} %shard_map.134), channel_id=1, source_target_pairs={{0,32},{32,0},{64,96},{96,64},{128,160},{160,128},{192,224},{224,1... | collective-permute-start | bytes 1572872 | tf_op jit(solution)/shard_map/ppermute | solution.py:411
